TPU v7x, 32 devices: a whole 2x2x4 slice. The times are simulated.
32 devices in a mesh: dp: 8 (over y, x, core), tensor: 4 (over z).
Axes of the slice: x: 2, y: 2, z: 4, core: 2. Of those that a mesh axis runs over, the one named last changes fastest.
Arguments:
- inputs: bfloat16 [16384, 384], P(('dp', 'tensor')), may hold values from -6 to 6
- lengths: int32 [16], P('dp'), may hold values from 256 to 1024, as said below
- expert_ids: int32 [16384, 2], P('dp'), may hold values from 0 to 7, all different within a row; in each aligned block of 2048 rows (0 to 2047, 2048 to 4095, ...) at most 1024 rows name the same one
- gain_attn: bfloat16 [384], replicated, may hold values from 0.5 to 1.5
- w_query: bfloat16 [384, 384], P(None, 'tensor'), may hold values from -0.3125 to 0.3125
- w_key: bfloat16 [384, 384], P(None, 'tensor'), may hold values from -0.3125 to 0.3125
- w_value: bfloat16 [384, 384], P(None, 'tensor'), may hold values from -0.3125 to 0.3125
- w_out: bfloat16 [384, 384], P('tensor'), may hold values from -1.5 to 1.5
- gain_ffn: bfloat16 [384], replicated, may hold values from 0.5 to 1.5
- router: bfloat16 [384, 8], replicated, may hold values from -0.21875 to 0.21875
- shared_gate_vec: bfloat16 [384], replicated, may hold values from -0.3125 to 0.3125
- exp_gate: bfloat16 [8, 384, 768], P(None, None, 'tensor'), may hold values from -0.3125 to 0.3125
- exp_up: bfloat16 [8, 384, 768], P(None, None, 'tensor'), may hold values from -0.3125 to 0.3125
- exp_down: bfloat16 [8, 768, 384], P(None, 'tensor'), may hold values from -0.875 to 0.875
- sh_gate: bfloat16 [384, 1536], P(None, 'tensor'), may hold values from -0.3125 to 0.3125
- sh_up: bfloat16 [384, 1536], P(None, 'tensor'), may hold values from -0.3125 to 0.3125
- sh_down: bfloat16 [1536, 384], P('tensor'), may hold values from -0.3125 to 0.3125
- cotangent: bfloat16 [16384, 384], P(('dp', 'tensor')), may hold values from -6 to 6
Outputs:
- output: bfloat16 [16384, 384], P(('dp', 'tensor'))
- d_inputs: float32 [16384, 384], P(('dp', 'tensor'))
- d_gain_attn: float32 [384], replicated
- d_w_query: float32 [384, 384], P(None, 'tensor')
- d_w_key: float32 [384, 384], P(None, 'tensor')
- d_w_value: float32 [384, 384], P(None, 'tensor')
- d_w_out: float32 [384, 384], P('tensor')
- d_gain_ffn: float32 [384], replicated
- d_router: float32 [384, 8], replicated
- d_shared_gate_vec: float32 [384], replicated
- d_exp_gate: float32 [8, 384, 768], P(None, None, 'tensor')
- d_exp_up: float32 [8, 384, 768], P(None, None, 'tensor')
- d_exp_down: float32 [8, 768, 384], P(None, 'tensor')
- d_sh_gate: float32 [384, 1536], P(None, 'tensor')
- d_sh_up: float32 [384, 1536], P(None, 'tensor')
- d_sh_down: float32 [1536, 384], P('tensor')
Inputs may be any that keep to these rules, and one draw needn't show every extreme that they name: `lengths`: in every draw some series has all 1024 points valid. `expert_ids`: each row names two different experts; within the 2048 rows of one dp group (aligned blocks) no expert is named by more than 1024 rows.
All inputs are finite; a program needn't handle non-finite values.
Results may differ from a plain program's by a relative error of at most 0.022.
Values may be sent and summed in bfloat16 or wider, within the bound.
A program may use at most 192 MiB of HBM per device.

v0:
```python
import jax
import jax.numpy as jnp
from jax import lax
from jax.sharding import PartitionSpec as P

HEAD_DIM = 32
LEN = 1024


HIGH = lax.Precision.HIGHEST


def norm_rows(values, gain):
    factor = lax.rsqrt(jnp.mean(values * values, axis=-1, keepdims=True) + 1e-06)
    return values * factor * gain


def silu_parts(values):
    sigma = lax.logistic(values)
    return (values * sigma, sigma * (1.0 + values * (1.0 - sigma)))


def rotary_tables(length, head_dim):
    half = head_dim // 2
    freqs = 10000.0 ** (-jnp.arange(half, dtype=jnp.float32) / half)
    angles = jnp.arange(length, dtype=jnp.float32)[:, None] * freqs[None, :]
    return (jnp.cos(angles), jnp.sin(angles))


def rotate(values, cosine, sine):
    half = values.shape[-1] // 2
    first = values[..., :half]
    second = values[..., half:]
    cos_wide = cosine[:, None, :]
    sin_wide = sine[:, None, :]
    return jnp.concatenate(
        [first * cos_wide - second * sin_wide, first * sin_wide + second * cos_wide], axis=-1
    )


def allowed_keys(length, count):
    position = jnp.arange(count, dtype=jnp.int32)
    return (position[None, :] <= position[:, None]) & (position[None, :] < length)


def route_slots(expert_ids, experts, capacity):
    flat_ids = expert_ids.reshape(-1)
    onehot = (flat_ids[:, None] == jnp.arange(experts, dtype=jnp.int32)[None, :]).astype(jnp.int32)
    ranks = jnp.sum(jnp.cumsum(onehot, axis=0) * onehot, axis=1) - 1
    slots = flat_ids * capacity + ranks
    owners = jnp.arange(flat_ids.shape[0], dtype=jnp.int32) // expert_ids.shape[1]
    slot_tokens = jnp.zeros((experts * capacity,), jnp.int32).at[slots].set(owners)
    return (slot_tokens, slots.reshape(expert_ids.shape))


def per_device(
    inputs,
    lengths,
    expert_ids,
    gain_attn,
    w_query,
    w_key,
    w_value,
    w_out,
    gain_ffn,
    router,
    shared_gate_vec,
    exp_gate,
    exp_up,
    exp_down,
    sh_gate,
    sh_up,
    sh_down,
    cotangent,
):
    width = inputs.shape[1]
    local_width = w_query.shape[1]
    local_heads = local_width // HEAD_DIM
    experts = exp_gate.shape[0]
    scale = HEAD_DIM ** (-0.5)
    cosine, sine = rotary_tables(LEN, HEAD_DIM)
    resid = inputs.astype(jnp.float32)
    norm_attn, attn_pull = jax.vjp(norm_rows, resid, gain_attn.astype(jnp.float32))
    attn_in = lax.all_gather(norm_attn.astype(jnp.bfloat16), "tensor", axis=0, tiled=True)
    group_rows = attn_in.shape[0]
    seq_count = group_rows // LEN
    capacity = group_rows // 2
    joined = jnp.concatenate([w_query, w_key, w_value], axis=1)
    projected = jnp.dot(attn_in, joined, preferred_element_type=jnp.float32)
    shaped = projected.reshape(seq_count, LEN, 3, local_heads, HEAD_DIM)
    queries = rotate(shaped[:, :, 0], cosine, sine).astype(jnp.bfloat16)
    keys = rotate(shaped[:, :, 1], cosine, sine).astype(jnp.bfloat16)
    values = shaped[:, :, 2].astype(jnp.bfloat16)

    def attend(items):
        query_one, key_one, value_one, length = items
        scores = (
            jnp.einsum("qhd,khd->hqk", query_one, key_one, preferred_element_type=jnp.float32)
            * scale
        )
        scores = jnp.where(allowed_keys(length, LEN)[None], scores, -1e30)
        row_max = jnp.max(scores, axis=-1, keepdims=True)
        weights = jnp.exp(scores - row_max)
        row_total = jnp.sum(weights, axis=-1, keepdims=True)
        probs_low = (weights / row_total).astype(jnp.bfloat16)
        mixed = jnp.einsum("hqk,khd->qhd", probs_low, value_one, preferred_element_type=jnp.float32)
        return (mixed.astype(jnp.bfloat16), row_max[..., 0] + jnp.log(row_total[..., 0]))

    heads_out, logsum = lax.map(attend, (queries, keys, values, lengths))
    heads_flat = heads_out.reshape(group_rows, local_width)
    rows_part = heads_flat
    attn_own = lax.psum_scatter(
        jnp.dot(rows_part, w_out, preferred_element_type=jnp.float32).astype(jnp.bfloat16),
        "tensor",
        scatter_dimension=0,
        tiled=True,
    ).astype(jnp.float32)
    middle = resid + attn_own
    norm_ffn, ffn_pull = jax.vjp(norm_rows, middle, gain_ffn.astype(jnp.float32))
    ffn_in = lax.all_gather(norm_ffn.astype(jnp.bfloat16), "tensor", axis=0, tiled=True)
    logits = jnp.dot(ffn_in, router, preferred_element_type=jnp.float32)
    expo = jnp.exp(logits - jnp.max(logits, axis=-1, keepdims=True))
    route = expo / jnp.sum(expo, axis=-1, keepdims=True)
    chosen = (expert_ids[:, :, None] == jnp.arange(experts, dtype=jnp.int32)[None, None, :]).astype(
        jnp.float32
    )
    gates = jnp.sum(route[:, None, :] * chosen, axis=-1)
    shared_scale = lax.logistic(
        jnp.dot(ffn_in, shared_gate_vec[:, None], preferred_element_type=jnp.float32)
    )
    slot_tokens, slots = route_slots(expert_ids, experts, capacity)
    expert_in = ffn_in[slot_tokens].reshape(experts, capacity, width)
    gate_pre = jnp.einsum("ecd,edf->ecf", expert_in, exp_gate, preferred_element_type=jnp.float32)
    up_pre = jnp.einsum("ecd,edf->ecf", expert_in, exp_up, preferred_element_type=jnp.float32)
    gate_act, gate_slope = silu_parts(gate_pre)
    hidden = (gate_act * up_pre).astype(jnp.bfloat16)
    expert_out = jnp.einsum(
        "ecf,efd->ecd", hidden, exp_down, preferred_element_type=jnp.float32
    ).reshape(experts * capacity, width)
    picked = expert_out[slots]
    routed = jnp.sum(gates[:, :, None] * picked, axis=1)
    sh_gate_pre = jnp.dot(ffn_in, sh_gate, preferred_element_type=jnp.float32)
    sh_up_pre = jnp.dot(ffn_in, sh_up, preferred_element_type=jnp.float32)
    sh_act, sh_slope = silu_parts(sh_gate_pre)
    sh_hidden = (sh_act * sh_up_pre).astype(jnp.bfloat16)
    sh_result = jnp.dot(sh_hidden, sh_down, preferred_element_type=jnp.float32)
    ffn_part = routed + shared_scale * sh_result
    ffn_own = lax.psum_scatter(
        ffn_part.astype(jnp.bfloat16), "tensor", scatter_dimension=0, tiled=True
    ).astype(jnp.float32)
    output = (middle + ffn_own).astype(jnp.bfloat16)
    grad_out = cotangent.astype(jnp.float32)
    grad_full = lax.all_gather(cotangent, "tensor", axis=0, tiled=True)
    gate_grads = jnp.sum(grad_full[:, None, :] * picked, axis=-1)
    scale_grad = jnp.sum(grad_full * sh_result, axis=-1, keepdims=True)
    slot_gates = (
        jnp.zeros((experts * capacity,), jnp.float32).at[slots.reshape(-1)].set(gates.reshape(-1))
    )
    expert_grad = (
        (slot_gates[:, None] * grad_full[slot_tokens])
        .astype(jnp.bfloat16)
        .reshape(experts, capacity, width)
    )
    d_exp_down = jnp.einsum("ecf,ecd->efd", hidden, expert_grad, preferred_element_type=jnp.float32)
    hidden_grad = jnp.einsum(
        "ecd,efd->ecf", expert_grad, exp_down, preferred_element_type=jnp.float32
    )
    gate_pre_grad = (hidden_grad * up_pre * gate_slope).astype(jnp.bfloat16)
    up_pre_grad = (hidden_grad * gate_act).astype(jnp.bfloat16)
    d_exp_gate = jnp.einsum(
        "ecd,ecf->edf", expert_in, gate_pre_grad, preferred_element_type=jnp.float32
    )
    d_exp_up = jnp.einsum(
        "ecd,ecf->edf", expert_in, up_pre_grad, preferred_element_type=jnp.float32
    )
    slot_input_grad = jnp.einsum(
        "ecf,edf->ecd", gate_pre_grad, exp_gate, preferred_element_type=jnp.float32
    )
    slot_input_grad = slot_input_grad + jnp.einsum(
        "ecf,edf->ecd", up_pre_grad, exp_up, preferred_element_type=jnp.float32
    )
    ffn_grad = jnp.sum(slot_input_grad.reshape(experts * capacity, width)[slots], axis=1)
    sh_grad = (shared_scale * grad_full).astype(jnp.bfloat16)
    d_sh_down = jnp.einsum("tf,td->fd", sh_hidden, sh_grad, preferred_element_type=jnp.float32)
    sh_hidden_grad = jnp.einsum("td,fd->tf", sh_grad, sh_down, preferred_element_type=jnp.float32)
    sh_gate_grad = (sh_hidden_grad * sh_up_pre * sh_slope).astype(jnp.bfloat16)
    sh_up_grad = (sh_hidden_grad * sh_act).astype(jnp.bfloat16)
    d_sh_gate = jnp.einsum("td,tf->df", ffn_in, sh_gate_grad, preferred_element_type=jnp.float32)
    d_sh_up = jnp.einsum("td,tf->df", ffn_in, sh_up_grad, preferred_element_type=jnp.float32)
    ffn_grad = ffn_grad + jnp.einsum(
        "tf,df->td", sh_gate_grad, sh_gate, preferred_element_type=jnp.float32
    )
    ffn_grad = ffn_grad + jnp.einsum(
        "tf,df->td", sh_up_grad, sh_up, preferred_element_type=jnp.float32
    )
    route_grad = jnp.sum(gate_grads[:, :, None] * chosen, axis=1)
    logit_grad = route * (route_grad - jnp.sum(route * route_grad, axis=-1, keepdims=True))
    scale_pre_grad = scale_grad * shared_scale * (1.0 - shared_scale)
    ffn_grad = ffn_grad + jnp.dot(
        logit_grad, router.astype(jnp.float32).T, precision=HIGH, preferred_element_type=jnp.float32
    )
    ffn_grad = ffn_grad + scale_pre_grad * shared_gate_vec.astype(jnp.float32)[None, :]
    d_router = jnp.einsum(
        "td,te->de", ffn_in, logit_grad, precision=HIGH, preferred_element_type=jnp.float32
    )
    d_shared_vec = jnp.einsum(
        "td,tk->d", ffn_in, scale_pre_grad, precision=HIGH, preferred_element_type=jnp.float32
    )
    ffn_own_grad = lax.psum_scatter(
        ffn_grad.astype(jnp.bfloat16), "tensor", scatter_dimension=0, tiled=True
    ).astype(jnp.float32)
    middle_norm_grad, d_gain_ffn = ffn_pull(ffn_own_grad)
    middle_grad = grad_out + middle_norm_grad
    attn_grad_full = lax.all_gather(middle_grad.astype(jnp.bfloat16), "tensor", axis=0, tiled=True)
    d_w_out = jnp.einsum(
        "tc,td->cd", heads_flat, attn_grad_full, preferred_element_type=jnp.float32
    )
    heads_grad = jnp.einsum("td,cd->tc", attn_grad_full, w_out, preferred_element_type=jnp.float32)
    heads_grad = heads_grad.astype(jnp.bfloat16).reshape(seq_count, LEN, local_heads, HEAD_DIM)

    def attend_back(items):
        query_one, key_one, value_one, grad_one, logsum_one, length = items
        scores = (
            jnp.einsum("qhd,khd->hqk", query_one, key_one, preferred_element_type=jnp.float32)
            * scale
        )
        allowed = allowed_keys(length, LEN)[None]
        probs = jnp.where(allowed, jnp.exp(scores - logsum_one[..., None]), 0.0)
        probs_low = probs.astype(jnp.bfloat16)
        value_grad = jnp.einsum(
            "hqk,qhd->khd", probs_low, grad_one, preferred_element_type=jnp.float32
        )
        probs_grad = jnp.einsum(
            "qhd,khd->hqk", grad_one, value_one, preferred_element_type=jnp.float32
        )
        row_dot = jnp.sum(probs * probs_grad, axis=-1, keepdims=True)
        score_grad = (probs * (probs_grad - row_dot)).astype(jnp.bfloat16)
        query_grad = (
            jnp.einsum("hqk,khd->qhd", score_grad, key_one, preferred_element_type=jnp.float32)
            * scale
        )
        key_grad = (
            jnp.einsum("hqk,qhd->khd", score_grad, query_one, preferred_element_type=jnp.float32)
            * scale
        )
        return (query_grad, key_grad, value_grad)

    query_grads, key_grads, value_grads = lax.map(
        attend_back, (queries, keys, values, heads_grad, logsum, lengths)
    )
    proj_grad = jnp.stack(
        [
            rotate(query_grads, cosine, -sine).astype(jnp.bfloat16),
            rotate(key_grads, cosine, -sine).astype(jnp.bfloat16),
            value_grads.astype(jnp.bfloat16),
        ],
        axis=2,
    )
    proj_grad = proj_grad.reshape(group_rows, 3 * local_width)
    d_joined = jnp.einsum("td,tc->dc", attn_in, proj_grad, preferred_element_type=jnp.float32)
    d_w_query = d_joined[:, :local_width]
    d_w_key = d_joined[:, local_width : 2 * local_width]
    d_w_value = d_joined[:, 2 * local_width :]
    rows_part = proj_grad
    attn_own_grad = lax.psum_scatter(
        jnp.einsum("tc,dc->td", rows_part, joined, preferred_element_type=jnp.float32).astype(
            jnp.bfloat16
        ),
        "tensor",
        scatter_dimension=0,
        tiled=True,
    ).astype(jnp.float32)
    input_norm_grad, d_gain_attn = attn_pull(attn_own_grad)
    d_inputs = middle_grad + input_norm_grad
    summed = lax.psum(
        (
            d_w_query,
            d_w_key,
            d_w_value,
            d_w_out,
            d_exp_gate,
            d_exp_up,
            d_exp_down,
            d_sh_gate,
            d_sh_up,
            d_sh_down,
        ),
        "dp",
    )
    small_sums = lax.psum((d_gain_attn, d_gain_ffn, d_router, d_shared_vec), ("dp", "tensor"))
    return (
        output,
        d_inputs,
        small_sums[0],
        summed[0],
        summed[1],
        summed[2],
        summed[3],
        small_sums[1],
        small_sums[2],
        small_sums[3],
        summed[4],
        summed[5],
        summed[6],
        summed[7],
        summed[8],
        summed[9],
    )


def solution(mesh):
    in_specs = (
        P(("dp", "tensor"), None),
        P("dp"),
        P("dp", None),
        P(),
        P(None, "tensor"),
        P(None, "tensor"),
        P(None, "tensor"),
        P("tensor", None),
        P(),
        P(),
        P(),
        P(None, None, "tensor"),
        P(None, None, "tensor"),
        P(None, "tensor", None),
        P(None, "tensor"),
        P(None, "tensor"),
        P("tensor", None),
        P(("dp", "tensor"), None),
    )
    out_specs = (
        P(("dp", "tensor"), None),
        P(("dp", "tensor"), None),
        P(),
        P(None, "tensor"),
        P(None, "tensor"),
        P(None, "tensor"),
        P("tensor", None),
        P(),
        P(),
        P(),
        P(None, None, "tensor"),
        P(None, None, "tensor"),
        P(None, "tensor", None),
        P(None, "tensor"),
        P(None, "tensor"),
        P("tensor", None),
    )
    return jax.shard_map(
        per_device, mesh=mesh, in_specs=in_specs, out_specs=out_specs, check_vma=False
    )
```

profile of v0, /device:TPU:1, one launch (start us, length us, event | category | flops | bytes accessed | tf_op | source)
XLA Modules:
  0.0 839.8 jit_solution(17821587790991874097)
XLA Ops:
  17.9 33.6 %all-gather.5.cloned.1.call-done = bf16[2048,384]{1,0:T(8,128)(2,1)} async-done(((bf16[512,384]{1,0:T(8,128)(2,1)}), bf16[2048,384]{1,0:T(8,128)(2,1)}) %all-gather.5.cloned.1.call-update) | async-done | bytes 1572880 | tf_op jit(solution)/shard_map/all_gather | solution.py:84
  61.2 44.6 %while.26 = (s32[]{:T(128)}, bf16[2,1024,3,32]{1,3,2,0:T(8,128)(2,1)S(1)}, f32[2,3,1024]{2,1,0:T(4,128)}, bf16[2,1024,3,32]{1,3,2,0:T(8,128)(2,1)S(1)}, s32[2]{0...) while((s32[]{:T(128)}, ...), condition=%wide.region_4.5_spmd, body=%wide.region_1.4_spmd.sunk | while | flops 442595328 | bytes 42844272 | solution.py:109
  91.2 7.3 fusion.196
  114.8 28.4 %reduce-scatter.5.cloned.1.call-done = bf16[512,384]{1,0:T(8,128)(2,1)} async-done(((bf16[2048,384]{1,0:T(8,128)(2,1)}), bf16[512,384]{1,0:T(8,128)(2,1)}) %reduce-scatter.5.cloned.1.call-update) | async-done | bytes 393232 | tf_op jit(solution)/shard_map/reduce_scatter | solution.py:112
  154.9 15.5 %scatter_custom_fusion = s32[8192]{0:T(1024)S(1)} fusion(s32[4096]{0:T(1024)S(1)} %bitcast.242, s32[4096]{0:T(1024)S(1)} %add_select_fusion, s32[]{:T(128)} %copy.155), kind=kCustom, calls=%fused_computation.179 | custom fusion | bytes 32772 | tf_op jit(solution)/shard_map/scatter | solution.py:52
  170.5 10.4 %all-gather.9.cloned.1.call-done = bf16[2048,384]{1,0:T(8,128)(2,1)} async-done(((bf16[512,384]{1,0:T(8,128)(2,1)}), bf16[2048,384]{1,0:T(8,128)(2,1)}) %all-gather.9.cloned.1.call-update) | async-done | bytes 1572880 | tf_op jit(solution)/shard_map/all_gather | solution.py:153
  184.3 33.1 %gather_fusion.2 = bf16[8192,384]{1,0:T(8,128)(2,1)} fusion(bf16[2048,384]{1,0:T(8,128)(2,1)S(1)} %copy-done.4, s32[8192]{0:T(1024)S(1)} %fusion.89), kind=kCustom, calls=%fused_computation.2 | custom fusion | bytes 12615680 | tf_op jit(solution)/shard_map/gather | solution.py:160
  230.9 16.2 %scatter_custom_fusion.1 = f32[8192]{0:T(1024)} fusion(s32[4096]{0:T(1024)} %bitcast.243, f32[4096]{0:T(1024)} %reshape.452, f32[]{:T(128)} %constant.91.clone.1), kind=kCustom, calls=%fused_computation.177 | custom fusion | bytes 33280 | tf_op jit(solution)/shard_map/scatter | solution.py:157
  258.9 33.1 %gather_fusion = bf16[8192,384]{1,0:T(8,128)(2,1)} fusion(bf16[2048,384]{1,0:T(8,128)(2,1)S(1)} %copy-done.2, s32[8192]{0:T(1024)S(1)} %fusion.89), kind=kCustom, calls=%fused_computation | custom fusion | bytes 12615680 | tf_op jit(solution)/shard_map/gather | solution.py:132
  292.0 8.3 fusion.108
  305.3 9.9 %multiply_convert_fusion.1 = (bf16[8,1024,192]{1,2,0:T(8,128)(2,1)}, bf16[8,1024,192]{1,2,0:T(8,128)(2,1)S(1)}, bf16[8,1024,192]{1,2,0:T(8,128)(2,1)}) fusion(f32[8,1024,192]{1,2,0:T(8,128)} %fusion.107, f32[8,1024,192]{1,2,0:T(8,128)} %fusion.108, bf16[8,192,384]{2,1,0:T(8,128)(2,1)S(1)} %copy-done, bf16[8,1024,384]{2,1,0:T(8,128)(2,1)S(1)} %bitcast.225, ...), kind=kOutput, calls=%fused_computation.74 | convolution fusion | flops 1240989696 | bytes 29523968 | tf_op jit(solution)/shard_map/ecd,efd->ecf/dot_general | solution.py:165
  319.8 9.3 %convolution_add_fusion = f32[8,1024,384]{2,1,0:T(8,128)} fusion(f32[8,1024,384]{2,1,0:T(8,128)S(1)} %fusion.113, bf16[8,1024,192]{1,2,0:T(8,128)(2,1)} %get-tuple-element.211, bf16[8,384,192]{1,2,0:T(8,128)(2,1)} %param.34), kind=kOutput, calls=%fused_computation.82 | convolution fusion | flops 1211105280 | bytes 29491200 | tf_op jit(solution)/shard_map/ecf,edf->ecd/dot_general | solution.py:179
  329.1 22.0 %gather_fusion.3 = f32[4096,384]{1,0:T(8,128)} fusion(f32[8192,384]{1,0:T(8,128)} %bitcast.217, s32[4096]{0:T(1024)S(1)} %broadcast_clamp_fusion), kind=kCustom, calls=%fused_computation.3 | custom fusion | bytes 12599296 | tf_op jit(solution)/shard_map/gather | solution.py:182
  351.1 8.2 reshape.437
  359.3 35.3 %reduce_sum.179 = f32[2048,384]{1,0:T(8,128)} reduce(f32[2048,2,384]{2,1,0:T(2,128)} %reshape.437, f32[]{:T(128)} %constant.91.clone.1), dimensions={1}, to_apply=%region_17.18 | reduce | flops 786432 | bytes 9437188 | tf_op jit(solution)/shard_map/reduce_sum | solution.py:182
  394.6 8.9 %fusion.109 = f32[8,1024,384]{2,1,0:T(8,128)} fusion(bf16[8,1024,192]{1,2,0:T(8,128)(2,1)} %get-tuple-element.213, bf16[8,192,384]{2,1,0:T(8,128)(2,1)S(1)} %copy-done), kind=kOutput, calls=%fused_computation.203 | convolution fusion | flops 1207959552 | bytes 16908288 | tf_op jit(solution)/shard_map/ecf,efd->ecd/dot_general | solution.py:137
  403.6 21.6 %gather_fusion.1 = f32[4096,384]{1,0:T(8,128)} fusion(f32[8192,384]{1,0:T(8,128)} %bitcast.218, s32[4096]{0:T(1024)S(1)} %broadcast_clamp_fusion), kind=kCustom, calls=%fused_computation.1 | custom fusion | bytes 12599296 | tf_op jit(solution)/shard_map/gather | solution.py:140
  425.2 8.3 reshape.417
  433.5 19.4 %multiply_reduce_fusion.1 = (f32[2048,2]{1,0:T(8,128)}, f32[2048,384]{1,0:T(8,128)}) fusion(f32[2048,2,384]{2,1,0:T(2,128)} %reshape.417, f32[2048,384]{1,0:T(8,128)} %convert_element_type.159, f32[2048,2]{1,0:T(8,128)S(1)} %copy-done.24), kind=kLoop, calls=%fused_computation.73 | loop fusion | flops 5500928 | bytes 12615680 | tf_op jit(solution)/shard_map/reduce_sum | solution.py:154
  464.3 34.2 %reduce-scatter.9.cloned.1.call-done = bf16[512,384]{1,0:T(8,128)(2,1)} async-done(((bf16[2048,384]{1,0:T(8,128)(2,1)}), bf16[512,384]{1,0:T(8,128)(2,1)}) %reduce-scatter.9.cloned.1.call-update) | async-done | bytes 393232 | tf_op jit(solution)/shard_map/reduce_scatter | solution.py:209
  502.7 36.2 %all-gather.11.cloned.1.call-done = bf16[2048,384]{1,0:T(8,128)(2,1)} async-done(((bf16[512,384]{1,0:T(8,128)(2,1)}), bf16[2048,384]{1,0:T(8,128)(2,1)}) %all-gather.11.cloned.1.call-update) | async-done | bytes 1572880 | tf_op jit(solution)/shard_map/all_gather | solution.py:214
  541.4 48.5 %while.27 = (s32[]{:T(128)}, f32[2,1024,3,32]{1,3,2,0:T(8,128)}, f32[2,1024,3,32]{1,3,2,0:T(8,128)S(1)}, bf16[2,1024,3,32]{1,3,2,0:T(8,128)(2,1)}, bf16[2,1024,3...) while((s32[]{:T(128)}, f32[2,1024,3,32]{1,3,2,0:T(8,128)}, ...), condition=%wide.region_26.27_spmd, body=%wide.region_24.26_spmd.sunk | while | flops 1056110592 | bytes 110660856 | solution.py:248
  633.2 42.1 %all-reduce = (f32[384]{0:T(512)}, f32[384]{0:T(512)}, f32[384,8]{0,1:T(8,128)}, f32[384]{0:T(512)}) all-reduce(f32[384]{0:T(512)S(1)} %get-tuple-element.157, f32[384]{0:T(512)S(1)} %copy-done.99, f32[384,8]{0,1:T(8,128)S(1)} %fusion.91, f32[384]{0:T(512)S(1)} %convolution_reduce_fusion), channel_id=1, replica_groups=mesh['dp'=8,'tensor'=4] {'dp','tensor'}, use_global_device_ids=true, to_apply=%region_30.31 | all-reduce | flops 4224 | bytes 33792 | tf_op jit(solution)/shard_map/psum | solution.py:290
  678.1 138.6 %all-reduce.4.cloned.1.call-done = (f32[384,96]{0,1:T(8,128)}, f32[384,96]{0,1:T(8,128)}, f32[384,96]{0,1:T(8,128)}, f32[96,384]{1,0:T(8,128)}, f32[8,384,192]{1...) async-done(((f32[384,96]{0,1:T(8,128)}, f32[384,96]{0,1:T(8,128)}, ...) | async-done | bytes 9437200 | tf_op jit(solution)/shard_map/psum | solution.py:275
  (390 shorter events, 243.8 us)
Async XLA Ops:
  7.2 298.1 %copy-start = (bf16[8,192,384]{2,1,0:T(8,128)(2,1)S(1)}, bf16[8,192,384]{2,1,0:T(8,128)(2,1)}, u32[]{:S(2)}) copy-start(bf16[8,192,384]{2,1,0:T(8,128)(2,1)} %param.35) | copy-start | bytes 3538948
  7.2 44.3 %all-gather.5.cloned.1.call-start = ((), (), s32[]{:S(2)}) async-start(), calls=%async_computation.4 | async-start | bytes 1966080 | tf_op jit(solution)/shard_map/all_gather | solution.py:84
  12.3 130.9 %reduce-scatter.5.cloned.1.call-start = ((), (), s32[]{:S(2)}) async-start(), calls=%async_computation.5 | async-start | bytes 1966080 | tf_op jit(solution)/shard_map/reduce_scatter | solution.py:112
  61.2 45.9 %copy-start.59 = (bf16[96,384]{1,0:T(8,128)(2,1)S(1)}, bf16[96,384]{1,0:T(8,128)(2,1)}, u32[]{:S(2)}) copy-start(bf16[96,384]{1,0:T(8,128)(2,1)} %param.29) | copy-start | bytes 221188
  108.9 72.0 %all-gather.9.cloned.1.call-start = ((), (), s32[]{:S(2)}) async-start(), calls=%async_computation.8 | async-start | bytes 1966080 | tf_op jit(solution)/shard_map/all_gather | solution.py:153
  109.6 109.2 %all-gather.7.cloned.1.call-start = ((), (), s32[]{:S(2)}) async-start(), calls=%async_computation.6 | async-start | bytes 1966080 | tf_op jit(solution)/shard_map/all_gather | solution.py:120
  146.3 352.2 %reduce-scatter.9.cloned.1.call-start = ((), (), s32[]{:S(2)}) async-start(), calls=%async_computation.9 | async-start | bytes 1966080 | tf_op jit(solution)/shard_map/reduce_scatter | solution.py:209
  464.2 74.7 %copy-start.60 = (bf16[96,384]{1,0:T(8,128)(2,1)S(1)}, bf16[96,384]{1,0:T(8,128)(2,1)}, u32[]{:S(2)}) copy-start(bf16[96,384]{1,0:T(8,128)(2,1)} %param.29) | copy-start | bytes 221188
  464.2 74.7 %all-gather.11.cloned.1.call-start = ((), (), s32[]{:S(2)}) async-start(), calls=%async_computation.10 | async-start | bytes 1966080 | tf_op jit(solution)/shard_map/all_gather | solution.py:214
  500.4 40.9 %copy-start.19 = (bf16[2,1024,3,32]{1,3,2,0:T(8,128)(2,1)S(1)}, bf16[2,1024,3,32]{1,3,2,0:T(8,128)(2,1)}, u32[]{:S(2)}) copy-start(bf16[2,1024,3,32]{1,3,2,0:T(8,128)(2,1)} %copy-done.18) | copy-start | bytes 1179652
  500.4 40.9 %copy-start.28 = (bf16[2,1024,3,32]{1,3,2,0:T(8,128)(2,1)S(1)}, bf16[2,1024,3,32]{1,3,2,0:T(8,128)(2,1)}, u32[]{:S(2)}) copy-start(bf16[2,1024,3,32]{1,3,2,0:T(8,128)(2,1)} %copy-done.27) | copy-start | bytes 1179652
  500.4 40.9 %copy-start.62 = (f32[2,3,1024]{2,1,0:T(4,128)S(1)}, f32[2,3,1024]{2,1,0:T(4,128)}, u32[]{:S(2)}) copy-start(f32[2,3,1024]{2,1,0:T(4,128)} %get-tuple-element.390) | copy-start | bytes 73732
  500.4 40.9 %copy-start.104 = (s32[2]{0:T(128)S(1)}, s32[2]{0:T(128)}, u32[]{:S(2)}) copy-start(s32[2]{0:T(128)} %param.23) | copy-start | bytes 28
  502.6 129.2 %reduce-scatter.11.cloned.1.call-start = ((), (), s32[]{:S(2)}) async-start(), calls=%async_computation.11 | async-start | bytes 1966080 | tf_op jit(solution)/shard_map/reduce_scatter | solution.py:265
  541.4 48.5 %copy-start.51 = (f32[1024,16]{0,1:T(8,128)S(1)}, f32[1024,16]{0,1:T(8,128)}, u32[]{:S(2)}) copy-start(f32[1024,16]{0,1:T(8,128)} %get-tuple-element.242) | copy-start | bytes 196612
  597.6 77.8 %reduce-scatter.7.cloned.1.call-start = ((), (), s32[]{:S(2)}) async-start(), calls=%async_computation.7 | async-start | bytes 1966080 | tf_op jit(solution)/shard_map/reduce_scatter | solution.py:148
  598.4 218.4 %all-reduce.4.cloned.1.call-start = ((), (), s32[]{:S(2)}) async-start(), calls=%async_computation.12 | async-start | bytes 18874368 | tf_op jit(solution)/shard_map/psum | solution.py:275
  622.8 52.6 %copy-start.95 = (f32[512]{0:T(512)S(1)}, f32[512]{0:T(512)}, u32[]{:S(2)}) copy-start(f32[512]{0:T(512)} %copy-done.94) | copy-start | bytes 6148
  622.8 52.6 %copy-start.23 = (bf16[512,384]{1,0:T(8,128)(2,1)S(1)}, bf16[512,384]{1,0:T(8,128)(2,1)}, u32[]{:S(2)}) copy-start(bf16[512,384]{1,0:T(8,128)(2,1)} %reduce-scatter.5.cloned.1.call-done) | copy-start | bytes 1179652
  622.8 52.6 %copy-start.34 = (bf16[512,384]{1,0:T(8,128)(2,1)S(1)}, bf16[512,384]{1,0:T(8,128)(2,1)}, u32[]{:S(2)}) copy-start(bf16[512,384]{1,0:T(8,128)(2,1)} %param.39) | copy-start | bytes 1179652
  622.8 52.6 %copy-start.35 = (bf16[512,384]{1,0:T(8,128)(2,1)S(1)}, bf16[512,384]{1,0:T(8,128)(2,1)}, u32[]{:S(2)}) copy-start(bf16[512,384]{1,0:T(8,128)(2,1)} %reduce-scatter.9.cloned.1.call-done) | copy-start | bytes 1179652
  622.9 52.6 %copy-start.81 = (f32[384]{0:T(512)S(1)}, f32[384]{0:T(512)}, u32[]{:S(2)}) copy-start(f32[384]{0:T(512)} %copy-done.79) | copy-start | bytes 4612
  622.9 52.6 %copy-start.84 = (f32[512]{0:T(512)S(1)}, f32[512]{0:T(512)}, u32[]{:S(2)}) copy-start(f32[512]{0:T(512)} %copy-done.82) | copy-start | bytes 6148
  622.9 52.6 %copy-start.93 = (f32[512]{0:T(512)S(1)}, f32[512]{0:T(512)}, u32[]{:S(2)}) copy-start(f32[512]{0:T(512)} %copy-done.92) | copy-start | bytes 6148
  (98 other events, 758.4 us)
Sparse Core Ops, SparseCore 0:
  12.4 39.0 all-gather.4
  109.0 34.0 reduce-scatter.4
  144.7 36.0 all-gather.8
  182.9 35.9 all-gather.6
  464.3 34.0 reduce-scatter.8
  502.8 36.0 all-gather.10
  597.7 34.0 reduce-scatter.10
  634.1 35.3 reduce-scatter.6
  676.2 140.5 all-reduce.3
where the time goes:
time: 851 us; the launch traced here: 840 us
  waiting for transfers between devices  291 us (34%)
  local copies, waits for them, and re-layouts  215 us (25%)
  matrix products  156 us (18%)
  other arithmetic  118 us (14%)
  blocking collectives  42.1 us (5%)
  between operations  15.5 us (2%)
    psum x1, waiting for transfers between devices, per_device(): lax.psum((d_w_query, d_w_key, d_w_value, d_w_out, d_exp_gate, d_exp_up, d...  139 us
    psum x1, blocking collectives, per_device(): lax.psum((d_gain_attn, d_gain_ffn, d_router, d_shared_vec), ('dp', 'tenso...  42.1 us
    all_gather x1, waiting for transfers between devices, per_device(): lax.all_gather(middle_grad.astype(jnp.bfloat16), 'tensor', axis=0, tiled=...  36.2 us
    reduce_sum x1, other arithmetic, per_device(): jnp.sum(slot_input_grad.reshape(experts * capacity, width)[slots], axis=1)  35.3 us
    reduce_scatter x1, waiting for transfers between devices, per_device(): lax.psum_scatter(ffn_grad.astype(jnp.bfloat16), 'tensor', scatter_dimensi...  34.2 us
    all_gather x1, waiting for transfers between devices, per_device(): lax.all_gather(norm_attn.astype(jnp.bfloat16), 'tensor', axis=0, tiled=True)  33.6 us
    gather x1, local copies, waits for them, and re-layouts, per_device(): expert_in = ffn_in[slot_tokens].reshape(experts, capacity, width)  33.1 us
    gather x1, local copies, waits for them, and re-layouts, per_device(): grad_full[slot_tokens]  33.1 us
  transfers between devices with their start and end apart: 9, of which 8 were waited for; matrix products, arithmetic and copies ran while one was open for 12% of the time, Pallas kernels for 0%

commit v1 on v0

v1 whole, which is shorter than its diff:
```python
import functools

import jax
import jax.numpy as jnp
import numpy as np
from jax import lax
from jax.experimental import pallas as pl
from jax.experimental.pallas import tpu as pltpu
from jax.sharding import PartitionSpec as P

HD = 32
LEN = 1024
NT = 4
LANES = 128
QB = 256
BF = jnp.bfloat16
F32 = jnp.float32
MESH = pl.DeviceIdType.MESH
NEG = -1e30
SCALE = HD**-0.5
LOG2E = 1.4426950408889634
LN2 = 0.6931471805599453


def nn(a, b):
    return lax.dot_general(a, b, (((1,), (0,)), ((), ())), preferred_element_type=F32)


def nt(a, b):
    return lax.dot_general(a, b, (((1,), (1,)), ((), ())), preferred_element_type=F32)


def inv_rms(v):
    return lax.rsqrt(jnp.mean(v * v, axis=-1, keepdims=True) + 1e-06)


def rms_back(v, grad, gain):
    r = inv_rms(v)
    u = v * r
    g = grad * gain
    return r * (g - u * jnp.mean(g * u, axis=-1, keepdims=True)), grad * u


def up16(n):
    return -(-n // 16) * 16


class Plan:
    def __init__(self, nd, rows, width, experts, eff, ff):
        self.nd, self.R, self.W = nd, rows, width
        self.G = NT * rows
        self.NG = width // LANES
        self.HC = width // NT
        self.B = 2 * eff
        self.EB = experts // 2
        self.NB = self.EB + 1
        assert ff == self.B == width and LEN == 2 * rows
        self.E, self.eff, self.ff = experts, eff, ff
        self.share = min(4, nd)
        self.nc = nd // 2
        total = 3 * self.NB * width
        self.piece = up16(-(-total // nd))
        self.half = self.nc * self.piece
        self.total = total
        self.flat = 2 * self.half
        self.hp = 2 * self.HC
        self.pr = max(16, self.hp // self.nc)
        self.owners = self.hp // self.pr
        assert self.owners * self.pr == self.hp and self.pr % 16 == 0 and self.owners <= self.nc


class Sems:
    def __init__(self):
        self.n = 0

    def take(self, n):
        base = self.n
        self.n += n
        return base


def sem_plan(p):
    s, names = Sems(), {}
    names["w"] = s.take(3 * (4 // p.share))
    names["f"] = s.take(3 * (4 // p.share) * max(p.share - 1, 1))
    names["x"] = s.take(1)
    names["c"] = s.take(3)
    names["n"] = s.take(6)
    names["dx"] = s.take(3)
    names["o"] = s.take(3)
    names["h1"] = s.take(1)
    names["h2"] = s.take(max(p.nc - 1, 1))
    names["h3"] = s.take(max(p.nc - 1, 1))
    names["h4"] = s.take(p.nc)
    names["px"] = s.take(1)
    names["f1"] = s.take(1)
    names["f2"] = s.take(max(p.nc - 1, 1))
    names["f3"] = s.take(3)
    names["f4"] = s.take(p.nd - 1)
    names["s1"] = s.take(p.nd - 1)
    names["s2"] = s.take(3)
    return s.n, names


def kernel(
    p,
    names,
    len_ref,
    ids_ref,
    gains,
    watt,
    rext,
    x_hbm,
    cot_hbm,
    eg_hbm,
    eu_hbm,
    ed_hbm,
    sg_hbm,
    su_hbm,
    sd_hbm,
    cosk,
    sink,
    cost,
    sint,
    out_ref,
    din_ref,
    res_hbm,
    att_ref,
    sm_ref,
    send,
    recv,
    lsem,
    wfull,
    xs,
    xn,
    cotg,
    normg,
    wg,
    wu,
    wd,
    qT,
    qN,
    kN,
    kT,
    vN,
    vT,
    oT,
    lse,
    bias,
    mid,
    dx_own,
    out_own,
    dxr,
    outr,
    acc,
    drext,
    stage,
    h1,
    h2,
    res,
    agrad,
    dON,
    dOT,
    delta,
    pxs,
    pxr,
    A,
    f1,
    f2,
    fD,
    f3,
    att,
    smr,
    smz,
):
    R, W, NG = p.R, p.W, p.NG
    dp, z = lax.axis_index("dp"), lax.axis_index("tensor")
    zlo = lax.rem(z, 2)
    zk = [z, z + 1 - 2 * zlo, lax.rem(z + 2, NT), NT - 1 - z]
    core = lax.rem(dp, 2)
    chip = lax.div(dp, 2)
    mate = dp + 1 - 2 * core
    half_own = zlo

    def remote(src, dst, kind, i, dev):
        j = names[kind] + i
        return pltpu.make_async_remote_copy(
            src_ref=src, dst_ref=dst, send_sem=send.at[j], recv_sem=recv.at[j], device_id=dev, device_id_type=MESH
        )

    def to_z(k):
        return (dp, zk[k])

    def chip_at(j):
        return lax.rem(chip + j, p.nc)

    def on_chip(j):
        return (2 * chip_at(j) + core, z)

    V = pltpu.VMEM
    x_in, cot_in = xs.at[half_own], cotg.at[z]
    loads = [
        pltpu.make_async_copy(src, dst, lsem.at[i])
        for i, (src, dst) in enumerate(
            [
                (x_hbm, x_in),
                (cot_hbm, cot_in),
                (eg_hbm, wg.at[: p.EB]),
                (eu_hbm, wu.at[: p.EB]),
                (ed_hbm, wd.at[: p.EB]),
                (sg_hbm, agrad.at[:W]),
                (su_hbm, pxs.at[:W]),
                (sd_hbm, wd.at[p.EB]),
            ]
        )
    ]
    for c in loads:
        c.start()
    barrier = pltpu.get_barrier_semaphore()
    for k in (1, 2, 3):
        pl.semaphore_signal(barrier, inc=1, device_id=to_z(k), device_id_type=MESH)

    def greet(j, carry):
        pl.semaphore_signal(barrier, inc=1, device_id=(lax.rem(dp + j, p.nd), z), device_id_type=MESH)
        return carry

    lax.fori_loop(1, p.nd, greet, 0)
    pl.semaphore_wait(barrier, 3 + p.nd - 1)

    S = p.share
    member = lax.rem(dp, S)
    base = dp - member
    own_cols = pl.ds(pl.multiple_of(z * p.HC, 32), p.HC)

    def cols_of(k):
        return pl.ds(pl.multiple_of(zk[k] * p.HC, 32), p.HC)

    def w_send(k, i):
        m = member + S * i
        return remote(watt.at[m], wfull.at[m, own_cols], "w", (k - 1) * (4 // S) + i, to_z(k))

    def w_recv(k, i):
        m = member + S * i
        return remote(watt.at[m], wfull.at[m, cols_of(k)], "w", (k - 1) * (4 // S) + i, to_z(k))

    def w_forward(k, i, j):
        m = member + S * i
        there = base + lax.rem(member + j, S)
        return remote(
            wfull.at[m, cols_of(k)],
            wfull.at[m, cols_of(k)],
            "f",
            ((k - 1) * (4 // S) + i) * (S - 1) + j - 1,
            (there, z),
        )

    x_copy = remote(x_in, x_in, "x", 0, to_z(1))
    for k in (1, 2, 3):
        for i in range(4 // S):
            w_send(k, i).start()
    loads[0].wait()
    x_copy.start()
    for m in range(4):
        wfull[m, own_cols] = watt[m]
    gain_attn, gain_ffn = gains[0:1], gains[1:2]

    def mask_rows(i, carry):
        key = lax.broadcasted_iota(jnp.int32, (QB, R), 0) + i * QB
        query = lax.broadcasted_iota(jnp.int32, (QB, R), 1) + half_own * R
        length = len_ref[lax.div(z, 2)]
        bias[pl.ds(pl.multiple_of(i * QB, QB), QB)] = jnp.where((key <= query) & (key < length), 0.0, NEG)
        return carry

    lax.fori_loop(0, LEN // QB, mask_rows, 0)
    for k in (1, 2, 3):
        for i in range(4 // S):
            w_recv(k, i).wait_recv()
            for j in range(1, S):
                w_forward(k, i, j).start()

    for c in loads[1:]:
        c.wait()
    wg[p.EB] = agrad[:W].T
    wu[p.EB] = pxs[:W].T
    x_copy.wait_recv()
    for k in (1, 2, 3):
        remote(cot_in, cot_in, "c", k - 1, to_z(k)).start()

    def norm_half(i, carry):
        v = xs[i].astype(F32)
        xn[pl.ds(pl.multiple_of(i * R, R), R)] = (v * inv_rms(v) * gain_attn).astype(BF)
        return carry

    lax.fori_loop(0, 2, norm_half, 0)
    for k in (1, 2, 3):
        for i in range(4 // S):
            for j in range(1, S):
                w_forward(k, i, j).wait_recv()

    own_pos = pl.ds(pl.multiple_of(half_own * R, R), R)
    lane = lax.broadcasted_iota(jnp.int32, (1, LANES), 1)
    low_half = lax.rem(lane, HD) < HD // 2

    def swap_halves(v):
        return jnp.where(low_half, pltpu.roll(v, LANES - HD // 2, 1), pltpu.roll(v, HD // 2, 1))

    q_pre = nt(wfull[0], xn[own_pos])
    cos_own, sin_own = cost[:, own_pos], sint[:, own_pos]
    for h in range(W // HD):
        a = q_pre[h * HD : h * HD + HD // 2]
        b = q_pre[h * HD + HD // 2 : (h + 1) * HD]
        qT[h * HD : h * HD + HD // 2] = ((a * cos_own - b * sin_own) * (SCALE * LOG2E)).astype(BF)
        qT[h * HD + HD // 2 : (h + 1) * HD] = ((a * sin_own + b * cos_own) * (SCALE * LOG2E)).astype(BF)

    def project(i, carry):
        rows = pl.ds(pl.multiple_of(i * QB, QB), QB)
        xb = xn[rows]
        k_pre = nt(xb, wfull[1])
        v_pre = nt(xb, wfull[2])
        c, s = cosk[rows], sink[rows]
        for g in range(NG):
            kg = k_pre[:, g * LANES : (g + 1) * LANES]
            kN[g, rows] = (kg * c + swap_halves(kg) * s).astype(BF)
            vN[g, rows] = v_pre[:, g * LANES : (g + 1) * LANES].astype(BF)
        return carry

    lax.fori_loop(0, LEN // QB, project, 0)
    for g in range(NG):
        rows = slice(g * LANES, (g + 1) * LANES)
        kT[rows] = kN[g].T
        vT[rows] = vN[g].T
        qN[g] = qT[rows].T

    head_row = lax.div(lax.broadcasted_iota(jnp.int32, (LANES, 1), 0), HD)
    head_lane = lax.div(lane, HD)
    HPG = LANES // HD

    def scores(g, h, qb):
        qg = qT[pl.ds(pl.multiple_of(g * LANES, LANES), LANES), qb * QB : (qb + 1) * QB]
        masked = jnp.where(head_row == h, qg, jnp.zeros_like(qg))
        return nn(kN[g], masked) + bias[:, qb * QB : (qb + 1) * QB]

    for qb in range(R // QB):
        cols = slice(qb * QB, (qb + 1) * QB)

        def heads(g, carry):
            for h in range(HPG):
                s = scores(g, h, qb)
                top = jnp.max(s, axis=0, keepdims=True)
                e = jnp.exp2(s - top)
                total = jnp.sum(e, axis=0, keepdims=True)
                at = pl.ds(pl.multiple_of(g * LANES + h * HD, HD), HD)
                o = nn(vT[at], e.astype(BF)) * (1.0 / total)
                oT[at, cols] = o.astype(BF)
                lse[pl.ds(g * HPG + h, 1), cols] = top + jnp.log(total) * LOG2E
            return carry

        lax.fori_loop(0, NG, heads, 0)
        rows = slice(qb * QB, (qb + 1) * QB)
        m = x_in[rows].astype(F32) + nn(oT[:, cols].T, wfull[3])
        mid[rows] = m
        normg[z, rows] = (m * inv_rms(m) * gain_ffn).astype(BF)
        for k in (1, 2, 3):
            remote(normg.at[z, rows], normg.at[z, rows], "n", (k - 1) * 2 + qb, to_z(k)).start()

    for k in (1, 2, 3):
        remote(cot_in, cot_in, "c", k - 1, to_z(k)).wait_recv()

    def zero_acc(i, carry):
        acc[pl.ds(pl.multiple_of(i * 16, 16), 16)] = jnp.zeros((16, W), F32)
        return carry

    lax.fori_loop(0, p.total // 16, zero_acc, 0)
    drext[...] = jnp.zeros_like(drext)
    zhi = lax.div(z, 2)

    def chunk_of(k):
        return 2 * lax.rem(zhi + lax.div(k, 2), 2) + lax.rem(zlo + lax.rem(k, 2), 2)

    def unit(C_s, G_s, RG_s, xT, gT, out_acc, dx_acc, k, carry):
        c = chunk_of(k)

        @pl.when(k > 0)
        def _():
            for b in range(R // QB):
                part = normg.at[c, b * QB : (b + 1) * QB]
                remote(part, part, "n", (k - 1) * 2 + b, (dp, c)).wait_recv()

        x = normg[c]
        xT[...] = x.T
        gT[...] = cotg[c].T
        logits = nn(x, rext[...])
        is_expert = lane < p.E
        lg = jnp.where(is_expert, logits, NEG)
        ex = jnp.exp(lg - jnp.max(lg, axis=-1, keepdims=True))
        route = ex / jnp.sum(ex, axis=-1, keepdims=True)
        at = pl.ds(pl.multiple_of(c * R, R), R)
        down = lax.broadcasted_iota(jnp.int32, (LANES, R), 0)
        named = (down == ids_ref[0:1, at]) | (down == ids_ref[1:2, at]) | ((down >= p.E) & (down < p.E + 2))
        chosen = jnp.where(named, 1.0, 0.0).T
        C_s[...] = chosen
        gate = jnp.where(is_expert, route, lax.logistic(logits)) * chosen
        G_s[...] = gate
        RG_s[...] = jnp.zeros_like(RG_s)
        out_acc[...] = jnp.zeros_like(out_acc)
        dx_acc[...] = jnp.zeros_like(dx_acc)

        def block(b, carry):
            xb, gb = normg[c], cotg[c]
            a = nt(xb, wg[b])
            u = nt(xb, wu[b])
            hg = nt(gb, wd[b])
            gates = G_s[...]
            first = jnp.sum(jnp.where(lane == 2 * b, gates, 0.0), axis=-1, keepdims=True)
            second = jnp.sum(jnp.where(lane == 2 * b + 1, gates, 0.0), axis=-1, keepdims=True)
            wide = lax.broadcasted_iota(jnp.int32, (1, p.B), 1) < p.eff
            gc = jnp.where(wide, first, second)
            sig = 0.5 * jnp.tanh(0.5 * a) + 0.5
            act = a * sig
            slope = sig + act - act * sig
            h = act * u
            prod = h * hg
            s0 = jnp.sum(jnp.where(wide, prod, 0.0), axis=-1, keepdims=True)
            s1 = jnp.sum(jnp.where(wide, 0.0, prod), axis=-1, keepdims=True)
            RG_s[...] += jnp.where(lane == 2 * b, s0, 0.0) + jnp.where(lane == 2 * b + 1, s1, 0.0)
            hs = (h * gc).astype(BF)
            hgs = hg * gc
            da = (hgs * u * slope).astype(BF)
            du = (hgs * act).astype(BF)
            out_acc[...] += nn(hs, wd[b])
            dx_acc[...] += nn(da, wg[b]) + nn(du, wu[b])
            xt = xT[...]

            def add(kind, value):
                at = pl.ds(pl.multiple_of((kind * p.NB + b) * W, W), W)
                acc[at] += value

            add(0, nn(xt, da))
            add(1, nn(xt, du))
            add(2, nn(gT[...], hs))
            return carry

        lax.fori_loop(0, p.NB, block, 0)
        rg = RG_s[...] * C_s[...]
        gate = G_s[...]
        dot = jnp.sum(jnp.where(is_expert, gate * rg, 0.0), axis=-1, keepdims=True)
        logits = nn(normg[c], rext[...])
        lg = jnp.where(is_expert, logits, NEG)
        ex = jnp.exp(lg - jnp.max(lg, axis=-1, keepdims=True))
        route = ex / jnp.sum(ex, axis=-1, keepdims=True)
        lgrad = jnp.where(is_expert, route * (rg - dot), rg * gate * (1.0 - gate)).astype(BF)
        drext[...] += nn(xT[...], lgrad)
        dx = dx_acc[...] + nt(lgrad, rext[...])

        @pl.when(k == 0)
        def _():
            dx_own[...] = dx
            out_own[...] = out_acc[...]

        @pl.when(k > 0)
        def _():
            normg[c] = dx.astype(BF)
            cotg[c] = out_acc[...].astype(BF)
            remote(normg.at[c], dxr.at[k - 1], "dx", k - 1, (dp, c)).start()

        return carry

    def chunks(C_s, G_s, RG_s, xT, gT, out_acc, dx_acc):
        lax.fori_loop(0, NT, functools.partial(unit, C_s, G_s, RG_s, xT, gT, out_acc, dx_acc), 0)

    pl.run_scoped(
        chunks, V((R, LANES), F32), V((R, LANES), F32), V((R, LANES), F32), V((W, R), BF), V((W, R), BF), V((R, W), F32), V((R, W), F32)
    )

    def to_stage(i, carry):
        at = pl.ds(pl.multiple_of(i * W, W), W)
        turned = (lax.rem(i, p.NB) < p.EB) | (i >= 2 * p.NB)

        @pl.when(turned)
        def _():
            stage[at] = acc[at].astype(BF).T

        @pl.when(jnp.logical_not(turned))
        def _():
            stage[at] = acc[at].astype(BF)

        return carry

    own_half = pl.multiple_of(core * p.half, 16)
    mate_half = pl.multiple_of((1 - core) * p.half, 16)
    lax.fori_loop(0, 3 * p.NB, to_stage, 0)
    if p.flat > p.total:
        stage[p.total :] = jnp.zeros((p.flat - p.total, W), BF)
    h1_copy = remote(stage.at[pl.ds(mate_half, p.half)], h1, "h1", 0, (mate, z))
    h1_copy.start()

    for k in (1, 2, 3):
        remote(normg.at[zk[k]], dxr.at[k - 1], "dx", k - 1, to_z(k)).wait_recv()
    for k in (1, 2, 3):
        remote(cotg.at[zk[k]], outr.at[k - 1], "o", k - 1, to_z(k)).start()
    dn = dx_own[...] + dxr[0].astype(F32) + dxr[1].astype(F32) + dxr[2].astype(F32)
    mid_back, dgain = rms_back(mid[...], dn, gain_ffn)
    sm_own = jnp.sum(dgain, axis=0, keepdims=True)
    mg = cot_in[...].astype(F32) + mid_back
    dx_own[...] = mg
    ag = mg.astype(BF)
    agrad[...] = ag
    dO = nt(ag, wfull[3])
    for g in range(NG):
        dON[g] = dO[:, g * LANES : (g + 1) * LANES].astype(BF)
    dOt = nt(wfull[3], ag).astype(BF)
    dOT[...] = dOt
    both = dOt.astype(F32) * oT[...].astype(F32)
    for h in range(W // HD):
        delta[h : h + 1] = jnp.sum(both[h * HD : (h + 1) * HD], axis=0, keepdims=True)

    def piece_at(j):
        return pl.ds(pl.multiple_of(core * p.half + chip_at(j) * p.piece, 16), p.piece)

    h1_copy.wait_recv()

    def add_mate(i, carry):
        near = pl.ds(pl.multiple_of(i * 16, 16), 16)
        at = pl.ds(pl.multiple_of(own_half + i * 16, 16), 16)
        stage[at] = (stage[at].astype(F32) + h1[near].astype(F32)).astype(BF)
        return carry

    lax.fori_loop(0, p.half // 16, add_mate, 0)

    def h2_copy(j):
        return remote(stage.at[piece_at(j)], h2.at[j - 1], "h2", j - 1, on_chip(j))

    for j in range(1, p.nc):
        h2_copy(j).start()

    dw = [acc.at[m * W : (m + 1) * W] for m in range(4)]
    dxn = acc.at[4 * W : 4 * W + LEN]
    dw[3][...] = nn(oT[...], agrad[...])
    dxn[...] = jnp.zeros_like(dxn)

    def back_group(pT, dsT, dk_acc, dv_acc, dqT, g, carry):
        at_g = pl.ds(pl.multiple_of(g * LANES, LANES), LANES)
        for qb in range(R // QB):
            cols = slice(qb * QB, (qb + 1) * QB)
            for h in range(HPG):
                s = scores(g, h, qb)
                prob = jnp.exp2(s - lse[pl.ds(g * HPG + h, 1), cols])
                og = dOT[at_g, cols]
                d_prob = nn(vN[g], jnp.where(head_row == h, og, jnp.zeros_like(og)))
                ds = (prob * (d_prob - delta[pl.ds(g * HPG + h, 1), cols])).astype(BF)
                pT[:, h * QB : (h + 1) * QB] = prob.astype(BF)
                dsT[:, h * QB : (h + 1) * QB] = ds
                at = pl.ds(pl.multiple_of(g * LANES + h * HD, HD), HD)
                dqT[h * HD : (h + 1) * HD, cols] = nn(kT[at], ds) * SCALE
            og, qg = dON[g, cols], qN[g, cols]
            o_heads = jnp.concatenate([jnp.where(head_lane == h, og, jnp.zeros_like(og)) for h in range(HPG)], axis=0)
            q_heads = jnp.concatenate([jnp.where(head_lane == h, qg, jnp.zeros_like(qg)) for h in range(HPG)], axis=0)
            dv = nn(pT[...], o_heads)
            dk = nn(dsT[...], q_heads) * LN2
            if qb == 0:
                dv_acc[...] = dv
                dk_acc[...] = dk
            else:
                dv_acc[...] += dv
                dk_acc[...] += dk
        dv = dv_acc[...].astype(BF)
        dk = dk_acc[...]
        dk = (dk * cosk[...] - swap_halves(dk) * sink[...]).astype(BF)
        parts = []
        for h in range(HPG):
            a = dqT[h * HD : h * HD + HD // 2]
            b = dqT[h * HD + HD // 2 : (h + 1) * HD]
            parts += [a * cos_own + b * sin_own, b * cos_own - a * sin_own]
        dq = jnp.concatenate(parts, axis=0).astype(BF)
        dw[0][at_g] = nn(dq, xn[own_pos])
        dw[1][at_g] = nn(dk.T, xn[...])
        dw[2][at_g] = nn(dv.T, xn[...])
        dxn[...] += nn(dk, wfull[1, at_g]) + nn(dv, wfull[2, at_g])
        dxn[own_pos] += nn(dq.T, wfull[0, at_g])
        return carry

    def back(pT, dsT, dk_acc, dv_acc, dqT):
        lax.fori_loop(0, NG, functools.partial(back_group, pT, dsT, dk_acc, dv_acc, dqT), 0)

    wide = V((LEN, HPG * QB), BF)
    pl.run_scoped(back, wide, wide, V((LEN, LANES), F32), V((LEN, LANES), F32), V((LANES, R), F32))

    pxs[...] = dxn[pl.ds(pl.multiple_of((1 - half_own) * R, R), R)].astype(BF)
    px_copy = remote(pxs, pxr, "px", 0, to_z(1))
    px_copy.start()

    for t in range(NT):
        for m in range(4):
            row = m * p.HC
            A[t, row // p.hp, row % p.hp : row % p.hp + p.HC] = dw[m][t * p.HC : (t + 1) * p.HC].astype(BF)
    f1_copy = remote(A.at[:, 1 - core], f1, "f1", 0, (mate, z))
    f1_copy.start()

    dg = jnp.zeros((1, W), F32)
    for half in range(2):
        v = xs[half].astype(F32)
        dg += jnp.sum(dxn[half * R : (half + 1) * R] * (v * inv_rms(v)), axis=0, keepdims=True)
    smr[dp, 0:1] = dg
    smr[dp, 1:2] = sm_own
    smr[dp, 2:16] = drext[...].T[0:14]

    def small(j):
        there = lax.rem(dp + j, p.nd)
        return remote(smr.at[dp], smr.at[dp], "s1", j - 1, (there, z))

    for j in range(1, p.nd):
        small(j).start()

    for j in range(1, p.nc):
        h2_copy(j).wait_recv()

    def add_chips(i, carry):
        near = pl.ds(pl.multiple_of(i * 16, 16), 16)
        at = pl.ds(pl.multiple_of(own_half + chip * p.piece + i * 16, 16), 16)
        v = stage[at].astype(F32)
        for j in range(1, p.nc):
            v += h2[j - 1, near].astype(F32)
        res[at] = v.astype(BF)
        return carry

    lax.fori_loop(0, p.piece // 16, add_chips, 0)

    def h3_copy(j):
        return remote(res.at[piece_at(0)], res.at[piece_at(0)], "h3", j - 1, on_chip(j))

    def h4_copy(j):
        return remote(res.at[piece_at(j)], res.at[piece_at(j)], "h4", j, (mate, z))

    for j in range(1, p.nc):
        h3_copy(j).start()
    h4_copy(0).start()

    f1_copy.wait_recv()
    for t in range(NT):
        A[t, core] = (A[t, core].astype(F32) + f1[t].astype(F32)).astype(BF)

    def chip_rows(j):
        return pl.ds(pl.multiple_of(chip_at(j) * p.pr, 16), p.pr)

    def f2_copy(j):
        return remote(A.at[:, core, chip_rows(j)], f2.at[j - 1], "f2", j - 1, on_chip(j))

    def owner(c):
        return (lambda f: f()) if p.owners == p.nc else pl.when(c < p.owners)

    owns = owner(chip)
    for j in range(1, p.nc):
        owner(chip_at(j))(lambda j=j: f2_copy(j).start())

    def f3_copy(k):
        return remote(fD.at[zk[k]], f3.at[k - 1], "f3", k - 1, to_z(k))

    @owns
    def _():
        for j in range(1, p.nc):
            f2_copy(j).wait_recv()
        for t in range(NT):
            v = A[t, core, chip_rows(0)].astype(F32)
            for j in range(1, p.nc):
                v += f2[j - 1, t].astype(F32)
            fD[t] = v.astype(BF)
        for k in (1, 2, 3):
            f3_copy(k).start()

    for j in range(1, p.nd):
        small(j).wait_recv()
    total = smr[0]
    for j in range(1, p.nd):
        total += smr[j]
    smz[z] = total

    def small_z(k):
        return remote(smz.at[z], smz.at[z], "s2", k - 1, to_z(k))

    for k in (1, 2, 3):
        small_z(k).start()
    def f4_copy(j):
        there = lax.rem(dp + j, p.nd)
        part = att.at[core, chip_rows(0)]
        return remote(part, part, "f4", j - 1, (there, z))

    @owns
    def _():
        for k in (1, 2, 3):
            f3_copy(k).wait_recv()
        v = fD[z].astype(F32)
        for k in (1, 2, 3):
            v += f3[k - 1].astype(F32)
        att[core, chip_rows(0)] = v.astype(BF)
        for j in range(1, p.nd):
            f4_copy(j).start()

    px_copy.wait_recv()
    dn = dxn[own_pos] + pxr[...].astype(F32)
    x_back, _ = rms_back(x_in[...].astype(F32), dn, gain_attn)
    din_ref[...] = dx_own[...] + x_back
    for k in (1, 2, 3):
        remote(cotg.at[zk[k]], outr.at[k - 1], "o", k - 1, to_z(k)).wait_recv()
    whole = mid[...] + (out_own[...] + outr[0].astype(F32) + outr[1].astype(F32) + outr[2].astype(F32))
    out_ref[...] = whole.astype(BF)

    for k in (1, 2, 3):
        small_z(k).wait_recv()
    sm_ref[...] = smz[0] + smz[1] + smz[2] + smz[3]
    for j in range(1, p.nc):
        h3_copy(j).wait_recv()
        h4_copy(p.nc - j).start()
    for j in range(p.nc):
        h4_copy(j).wait_recv()
    write = pltpu.make_async_copy(res, res_hbm, lsem.at[0])
    write.start()
    for j in range(1, p.nd):
        sender = lax.rem(dp + p.nd - j, p.nd)
        owner(lax.div(sender, 2))(lambda j=j: f4_copy(j).wait_recv())
    for c in range(2):
        att_ref[c * p.hp : (c + 1) * p.hp] = att[c]

    for k in (1, 2, 3):
        for i in range(4 // S):
            w_send(k, i).wait_send()
            for j in range(1, S):
                w_forward(k, i, j).wait_send()
        remote(cot_in, cot_in, "c", k - 1, to_z(k)).wait_send()
        for b in range(R // QB):
            part = normg.at[z, b * QB : (b + 1) * QB]
            remote(part, part, "n", (k - 1) * 2 + b, to_z(k)).wait_send()
        remote(normg.at[zk[k]], dxr.at[k - 1], "dx", k - 1, to_z(k)).wait_send()
        remote(cotg.at[zk[k]], outr.at[k - 1], "o", k - 1, to_z(k)).wait_send()
        small_z(k).wait_send()
    x_copy.wait_send()
    h1_copy.wait_send()
    px_copy.wait_send()
    f1_copy.wait_send()
    for j in range(1, p.nc):
        h2_copy(j).wait_send()
        h3_copy(j).wait_send()
        owner(chip_at(j))(lambda j=j: f2_copy(j).wait_send())
    for j in range(p.nc):
        h4_copy(j).wait_send()
    for j in range(1, p.nd):
        small(j).wait_send()

    @owns
    def _():
        for k in (1, 2, 3):
            f3_copy(k).wait_send()
        for j in range(1, p.nd):
            f4_copy(j).wait_send()

    write.wait()


def tables():
    half = HD // 2
    freqs = 10000.0 ** (-np.arange(half, dtype=np.float32) / np.float32(half))
    angles = np.arange(LEN, dtype=np.float32)[:, None] * freqs.astype(np.float32)[None, :]
    cosine, sine = np.cos(angles).astype(np.float32), np.sin(angles).astype(np.float32)
    reps = LANES // HD
    cos_wide = np.tile(np.concatenate([cosine, cosine], axis=1), (1, reps))
    sin_wide = np.tile(np.concatenate([-sine, sine], axis=1), (1, reps))
    return cos_wide, sin_wide, np.ascontiguousarray(cosine.T), np.ascontiguousarray(sine.T)


def per_device(
    nd,
    inputs,
    lengths,
    expert_ids,
    gain_attn,
    w_query,
    w_key,
    w_value,
    w_out,
    gain_ffn,
    router,
    shared_gate_vec,
    exp_gate,
    exp_up,
    exp_down,
    sh_gate,
    sh_up,
    sh_down,
    cotangent,
):
    R, W = inputs.shape
    experts, _, eff = exp_gate.shape
    ff = sh_gate.shape[1]
    p = Plan(nd, R, W, experts, eff, ff)
    number, names = sem_plan(p)
    gains = jnp.stack([gain_attn, gain_ffn]).astype(F32)
    watt = jnp.stack([w_query.T, w_key.T, w_value.T, w_out])
    vec = shared_gate_vec[:, None]
    rext = jnp.concatenate([router, vec, vec, jnp.zeros((W, LANES - experts - 2), BF)], axis=1)
    eg = exp_gate.swapaxes(1, 2).reshape(p.EB, p.B, W)
    eu = exp_up.swapaxes(1, 2).reshape(p.EB, p.B, W)
    ed = exp_down.reshape(p.EB, p.B, W)
    cosk, sink, cost, sint = tables()
    vm = pl.BlockSpec(memory_space=pltpu.VMEM)
    hbm = pl.BlockSpec(memory_space=pl.ANY)
    V = pltpu.VMEM
    hc = W // HD
    scratch = [
        pltpu.SemaphoreType.DMA((number,)),
        pltpu.SemaphoreType.DMA((number,)),
        pltpu.SemaphoreType.DMA((8,)),
        V((4, W, W), BF),
        V((2, R, W), BF),
        V((LEN, W), BF),
        V((NT, R, W), BF),
        V((NT, R, W), BF),
        V((p.NB, W, p.B), BF),
        V((p.NB, W, p.B), BF),
        V((p.NB, p.B, W), BF),
        V((W, R), BF),
        V((p.NG, R, LANES), BF),
        V((p.NG, LEN, LANES), BF),
        V((W, LEN), BF),
        V((p.NG, LEN, LANES), BF),
        V((W, LEN), BF),
        V((W, R), BF),
        V((up16(hc), R), F32),
        V((LEN, R), F32),
        V((R, W), F32),
        V((R, W), F32),
        V((R, W), F32),
        V((3, R, W), BF),
        V((3, R, W), BF),
        V((p.total, W), F32),
        V((W, LANES), F32),
        V((p.flat, W), BF),
        V((p.half, W), BF),
        V((max(p.nc - 1, 1), p.piece, W), BF),
        V((p.flat, W), BF),
        V((R, W), BF),
        V((p.NG, R, LANES), BF),
        V((W, R), BF),
        V((up16(hc), R), F32),
        V((R, W), BF),
        V((R, W), BF),
        V((NT, 2, p.hp, W), BF),
        V((NT, p.hp, W), BF),
        V((max(p.nc - 1, 1), NT, p.pr, W), BF),
        V((NT, p.pr, W), BF),
        V((3, p.pr, W), BF),
        V((2, p.hp, W), BF),
        V((nd, 16, W), F32),
        V((NT, 16, W), F32),
    ]
    output, d_inputs, res, att, small = pl.pallas_call(
        functools.partial(kernel, p, names),
        out_shape=[
            jax.ShapeDtypeStruct((R, W), BF),
            jax.ShapeDtypeStruct((R, W), F32),
            jax.ShapeDtypeStruct((p.flat, W), BF),
            jax.ShapeDtypeStruct((2 * p.hp, W), BF),
            jax.ShapeDtypeStruct((16, W), F32),
        ],
        in_specs=[pl.BlockSpec(memory_space=pltpu.SMEM)] + [vm] * 4 + [hbm] * 8 + [vm] * 4,
        out_specs=[vm, vm, hbm, vm, vm],
        scratch_shapes=scratch,
        compiler_params=pltpu.CompilerParams(collective_id=0, has_side_effects=True, vmem_limit_bytes=63 << 20),
        name="block",
    )(
        lengths,
        expert_ids.T,
        gains,
        watt,
        rext,
        inputs,
        cotangent,
        eg,
        eu,
        ed,
        sh_gate,
        sh_up,
        sh_down,
        jnp.asarray(cosk),
        jnp.asarray(sink),
        jnp.asarray(cost),
        jnp.asarray(sint),
    )
    kinds = res[: p.total].reshape(3, p.NB * p.B, W).astype(F32)

    def routed(kind):
        return kinds[kind, : experts * eff].reshape(experts, eff, W)

    d_exp_gate, d_exp_up = routed(0).swapaxes(1, 2), routed(1).swapaxes(1, 2)
    d_exp_down = routed(2)
    d_sh_gate, d_sh_up = kinds[0, experts * eff :], kinds[1, experts * eff :]
    d_sh_down = kinds[2, experts * eff :]
    att = att[: 4 * p.HC].reshape(4, p.HC, W).astype(F32)
    return (
        output,
        d_inputs,
        small[0],
        att[0].T,
        att[1].T,
        att[2].T,
        att[3],
        small[1],
        small[2 : 2 + experts].T,
        small[2 + experts] + small[3 + experts],
        d_exp_gate,
        d_exp_up,
        d_exp_down,
        d_sh_gate,
        d_sh_up,
        d_sh_down,
    )


def solution(mesh):
    rows = P(("dp", "tensor"), None)
    cols = P(None, "tensor")
    deep = P(None, None, "tensor")
    weights = (cols, cols, cols, P("tensor", None))
    experts = (deep, deep, P(None, "tensor", None), cols, cols, P("tensor", None))
    in_specs = (rows, P("dp"), P("dp", None), P()) + weights + (P(), P(), P()) + experts + (rows,)
    out_specs = (rows, rows, P()) + weights + (P(), P(), P()) + experts
    return jax.shard_map(
        functools.partial(per_device, mesh.shape["dp"]),
        mesh=mesh,
        in_specs=in_specs,
        out_specs=out_specs,
        check_vma=False,
    )
```

time: 851 us -> 233 us (0.27); the launches traced: 840 us -> 233 us
  waiting for transfers between devices: 291 us -> 0 us
  Pallas kernels: 0 us -> 214 us
  local copies, waits for them, and re-layouts: 215 us -> 11.1 us
  matrix products: 156 us -> 0 us
  other arithmetic: 118 us -> 6.73 us
  blocking collectives: 42.1 us -> 0 us
  between operations: 15.5 us -> 0.72 us
    pallas_call x0 -> x1, Pallas kernels: none -> 214 us  [per_device(): pl.pallas_call(functools.partial(kernel, p, names), out_shape=[jax.ShapeD...]
    dot_general x43 -> x0, matrix products: 156 us -> none  [the longest x2 13.4 us: attend(): jnp.einsum('hqk,khd->qhd', probs_low, value_one, preferred_element_type=j...]
    psum x1 -> x0, waiting for transfers between devices: 139 us -> none  [per_device(): lax.psum((d_w_query, d_w_key, d_w_value, d_w_out, d_exp_gate, d_exp_up, d...]
    gather x6 -> x0, local copies, waits for them, and re-layouts: 126 us -> none  [the longest x1 33.1 us: per_device(): expert_in = ffn_in[slot_tokens].reshape(experts, capacity, width)]
    all_gather x4 -> x0, waiting for transfers between devices: 81.6 us -> none  [the longest x1 36.2 us: per_device(): lax.all_gather(middle_grad.astype(jnp.bfloat16), 'tensor', axis=0, tiled=...]
    reduce_sum x13 -> x0, other arithmetic: 75.9 us -> none  [the longest x1 35.3 us: per_device(): jnp.sum(slot_input_grad.reshape(experts * capacity, width)[slots], axis=1)]
    reduce_scatter x4 -> x0, waiting for transfers between devices: 69.5 us -> none  [the longest x1 34.2 us: per_device(): lax.psum_scatter(ffn_grad.astype(jnp.bfloat16), 'tensor', scatter_dimensi...]
    psum x1 -> x0, blocking collectives: 42.1 us -> none  [per_device(): lax.psum((d_gain_attn, d_gain_ffn, d_router, d_shared_vec), ('dp', 'tenso...]
  transfers between devices with their start and end apart: 9 -> 0, of which waited for: 8 -> 0; matrix products, arithmetic and copies ran while one was open for 12% -> 0% of each run, Pallas kernels for 0% -> 0%
where the time goes in v1:
time: 233 us
  Pallas kernels  214 us (92%)
  local copies, waits for them, and re-layouts  11.1 us (5%)
  other arithmetic  6.73 us (3%)
    pallas_call x1, Pallas kernels, per_device(): pl.pallas_call(functools.partial(kernel, p, names), out_shape=[jax.ShapeD...  214 us

profile of v1, /device:TPU:1, one launch (start us, length us, event | category | flops | bytes accessed | tf_op | source)
XLA Modules:
  0.0 232.7 jit_solution(5207304057097118014)
XLA Ops:
  0.6 0.8 broadcast_in_dim.8
  1.4 0.8 copy.39
  2.3 0.1 pad.3.clone
  2.4 0.8 maximum_maximum_fusion.rext
  3.2 1.8 pad_maximum_fusion.watt
  4.9 0.7 stack.24
  5.6 0.7 stack.25
  6.3 0.6 maximum_convert_fusion.gains
  6.9 214.2 %block.1 = (bf16[512,384]{1,0:T(8,128)(2,1)}, f32[512,384]{1,0:T(8,128)}, bf16[5760,384]{1,0:T(8,128)(2,1)}, bf16[384,384]{1,0:T(8,128)(2,1)}, f32[16,384]{1,0:T(8,128)}) custom-call(s32[2]{0:T(128)} %len_ref.1, s32[2,2048]{1,0:T(2,128)} %bitcast.55, f32[2,384]{1,0:T(2,128)} %maximum_convert_fusion.gains, bf16[4,96,384]{2,1,0:T(8,128)(2,1)} %pad_maximum_fusion.watt, ...), custom_call_target="tpu_custom_call" | custom-call | tf_op jit(solution)/shard_map/block/pallas_call | solution.py:854
  221.0 0.0 slice-start
  221.0 0.0 slice-start.1
  221.0 3.0 %convert.1 = f32[3,1920,384]{2,1,0:T(8,128)S(1)} convert(bf16[3,1920,384]{2,1,0:T(8,128)(2,1)} %bitcast.41) | non-fusion elementwise | flops 2211840 | bytes 13271040 | tf_op jit(solution)/shard_map/convert_element_type | solution.py:887
  224.0 1.2 slice_bitcast_fusion
  225.3 0.0 slice-done
  225.3 0.0 slice-done.1
  225.3 0.0 copy-start.3
  225.3 3.1 %fusion = (f32[1,1536,384]{2,1,0:T(8,128)}, f32[1,1536,384]{2,1,0:T(8,128)}, f32[1,1536,384]{2,1,0:T(8,128)}) fusion(bf16[3,1920,384]{2,1,0:T(8,128)(2,1)S(1)} %bitcast.44), kind=kLoop, calls=%fused_computation.13 | loop fusion | bytes 14155776 | tf_op jit(solution)/shard_map/slice | solution.py:890
  228.4 0.0 copy-done.1
  228.4 0.8 slice_bitcast_fusion.3
  229.2 0.6 add_reduce_fusion
  229.8 0.7 slice.67
  230.5 0.6 slice_bitcast_fusion.6
  231.1 0.7 copy.44
  231.8 0.9 copy.45
  (9 shorter events, 0.1 us)
Async XLA Ops:
  221.0 4.2 %slice-start = ((s8[4423680]{0:T(1024)(128)(4,1)}), s8[4194304]{0:T(1024)(128)(4,1)S(1)}, s32[]{:S(2)}) async-start(s8[4423680]{0:T(1024)(128)(4,1)} %bitcast.42), calls=%async_computation | async-start | bytes 8388608
  221.0 4.2 %slice-start.1 = ((s8[4423680]{0:T(1024)(128)(4,1)}), s8[229376]{0:T(1024)(128)(4,1)S(1)}, s32[]{:S(2)}) async-start(s8[4423680]{0:T(1024)(128)(4,1)} %bitcast.42), calls=%async_computation.1 | async-start | bytes 458752
  225.3 3.1 %copy-start.1 = (bf16[384,384]{1,0:T(8,128)(2,1)S(1)}, bf16[384,384]{1,0:T(8,128)(2,1)}, u32[]{:S(2)}) copy-start(bf16[384,384]{1,0:T(8,128)(2,1)} %get-tuple-element.24) | copy-start | bytes 884740
  225.3 3.9 %copy-start.3 = (f32[16,384]{1,0:T(8,128)S(1)}, f32[16,384]{1,0:T(8,128)}, u32[]{:S(2)}) copy-start(f32[16,384]{1,0:T(8,128)} %get-tuple-element.23) | copy-start | bytes 73732
  228.4 2.7 %copy-start.2 = (bf16[512,384]{1,0:T(8,128)(2,1)S(1)}, bf16[512,384]{1,0:T(8,128)(2,1)}, u32[]{:S(2)}) copy-start(bf16[512,384]{1,0:T(8,128)(2,1)} %get-tuple-element.54) | copy-start | bytes 1179652
  228.4 3.5 %copy-start = (f32[512,384]{1,0:T(8,128)S(1)}, f32[512,384]{1,0:T(8,128)}, u32[]{:S(2)}) copy-start(f32[512,384]{1,0:T(8,128)} %get-tuple-element.55) | copy-start | bytes 2359300

commit v2 on v1

--- a/solution.py
+++ b/solution.py
@@ -58,12 +58,8 @@
         self.E, self.eff, self.ff = experts, eff, ff
         self.share = min(4, nd)
         self.nc = nd // 2
-        total = 3 * self.NB * width
-        self.piece = up16(-(-total // nd))
-        self.half = self.nc * self.piece
-        self.total = total
-        self.flat = 2 * self.half
         self.hp = 2 * self.HC
+        assert 2 * self.hp == width == self.B
         self.pr = max(16, self.hp // self.nc)
         self.owners = self.hp // self.pr
         assert self.owners * self.pr == self.hp and self.pr % 16 == 0 and self.owners <= self.nc
@@ -84,14 +80,15 @@
     names["w"] = s.take(3 * (4 // p.share))
     names["f"] = s.take(3 * (4 // p.share) * max(p.share - 1, 1))
     names["x"] = s.take(1)
-    names["c"] = s.take(3)
-    names["n"] = s.take(6)
+    for way in "rl":
+        names["c" + way] = s.take(4)
+        names["n" + way] = s.take(8)
     names["dx"] = s.take(3)
     names["o"] = s.take(3)
-    names["h1"] = s.take(1)
-    names["h2"] = s.take(max(p.nc - 1, 1))
-    names["h3"] = s.take(max(p.nc - 1, 1))
-    names["h4"] = s.take(p.nc)
+    names["h1"] = s.take(p.NB)
+    names["h2"] = s.take(p.NB * max(p.nc - 1, 1))
+    names["h3"] = s.take(p.NB * max(p.nc - 1, 1))
+    names["h4"] = s.take(p.NB * p.nc)
     names["px"] = s.take(1)
     names["f1"] = s.take(1)
     names["f2"] = s.take(max(p.nc - 1, 1))
@@ -107,9 +104,14 @@
     names,
     len_ref,
     ids_ref,
-    gains,
-    watt,
-    rext,
+    gain_attn_ref,
+    gain_ffn_ref,
+    router_ref,
+    vec_ref,
+    wq_ref,
+    wk_ref,
+    wv_ref,
+    wo_ref,
     x_hbm,
     cot_hbm,
     eg_hbm,
@@ -124,13 +126,20 @@
     sint,
     out_ref,
     din_ref,
-    res_hbm,
+    eg_out,
+    eu_out,
+    ed_out,
+    sg_out,
+    su_out,
+    sd_out,
     att_ref,
     sm_ref,
     send,
     recv,
     lsem,
     wfull,
+    rext32,
+    rext,
     xs,
     xn,
     cotg,
@@ -141,9 +150,8 @@
     qT,
     qN,
     kN,
-    kT,
+    kvT,
     vN,
-    vT,
     oT,
     lse,
     bias,
@@ -162,7 +170,6 @@
     dON,
     dOT,
     delta,
-    pxs,
     pxr,
     A,
     f1,
@@ -197,6 +204,58 @@
     def on_chip(j):
         return (2 * chip_at(j) + core, z)
 
+    def hop(kind, buf, way, i, part, rows, at):
+        there = (dp, z + 1) if way == "r" else (dp, z - 1)
+        ref = buf.at[at, rows]
+        parts = 1 if kind == "c" else R // QB
+        return remote(ref, ref, kind + way, i * parts + part, there)
+
+    def send_own(kind, buf, part, rows):
+        @pl.when(z < NT - 1)
+        def _():
+            hop(kind, buf, "r", 0, part, rows, z).start()
+
+        @pl.when(z > 0)
+        def _():
+            hop(kind, buf, "l", 0, part, rows, z).start()
+
+    def own_sent(kind, buf, part, rows):
+        @pl.when(z < NT - 1)
+        def _():
+            hop(kind, buf, "r", 0, part, rows, z).wait_send()
+
+        @pl.when(z > 0)
+        def _():
+            hop(kind, buf, "l", 0, part, rows, z).wait_send()
+
+    def arrive(kind, buf, i, part, rows):
+        @pl.when(z - 1 - i >= 0)
+        def _():
+            hop(kind, buf, "r", i, part, rows, z - 1 - i).wait_recv()
+
+            @pl.when(z < NT - 1)
+            def _():
+                hop(kind, buf, "r", i + 1, part, rows, z - 1 - i).start()
+
+        @pl.when(z + 1 + i < NT)
+        def _():
+            hop(kind, buf, "l", i, part, rows, z + 1 + i).wait_recv()
+
+            @pl.when(z > 0)
+            def _():
+                hop(kind, buf, "l", i + 1, part, rows, z + 1 + i).start()
+
+    def handed_on(kind, buf, c, part, rows):
+        @pl.when((c < z) & (z < NT - 1))
+        def _():
+            hop(kind, buf, "r", z - c, part, rows, c).wait_send()
+
+        @pl.when((c > z) & (z > 0))
+        def _():
+            hop(kind, buf, "l", c - z, part, rows, c).wait_send()
+
+    halves = [slice(i * QB, (i + 1) * QB) for i in range(R // QB)]
+
     V = pltpu.VMEM
     x_in, cot_in = xs.at[half_own], cotg.at[z]
     loads = [
@@ -209,7 +268,7 @@
                 (eu_hbm, wu.at[: p.EB]),
                 (ed_hbm, wd.at[: p.EB]),
                 (sg_hbm, agrad.at[:W]),
-                (su_hbm, pxs.at[:W]),
+                (su_hbm, dOT.at[:, :W]),
                 (sd_hbm, wd.at[p.EB]),
             ]
         )
@@ -237,11 +296,11 @@
 
     def w_send(k, i):
         m = member + S * i
-        return remote(watt.at[m], wfull.at[m, own_cols], "w", (k - 1) * (4 // S) + i, to_z(k))
+        return remote(wfull.at[m, own_cols], wfull.at[m, own_cols], "w", (k - 1) * (4 // S) + i, to_z(k))
 
     def w_recv(k, i):
         m = member + S * i
-        return remote(watt.at[m], wfull.at[m, cols_of(k)], "w", (k - 1) * (4 // S) + i, to_z(k))
+        return remote(wfull.at[m, cols_of(k)], wfull.at[m, cols_of(k)], "w", (k - 1) * (4 // S) + i, to_z(k))
 
     def w_forward(k, i, j):
         m = member + S * i
@@ -254,15 +313,22 @@
             (there, z),
         )
 
+    for m, ref in enumerate((wq_ref, wk_ref, wv_ref, wo_ref)):
+        wfull[m, own_cols] = ref[...]
     x_copy = remote(x_in, x_in, "x", 0, to_z(1))
     for k in (1, 2, 3):
         for i in range(4 // S):
             w_send(k, i).start()
     loads[0].wait()
     x_copy.start()
-    for m in range(4):
-        wfull[m, own_cols] = watt[m]
-    gain_attn, gain_ffn = gains[0:1], gains[1:2]
+    gain_attn = gain_attn_ref[...].astype(F32)
+    gain_ffn = gain_ffn_ref[...].astype(F32)
+    rext32[0 : p.E] = router_ref[...].astype(F32)
+    rext32[p.E : p.E + 1] = vec_ref[...].astype(F32)
+    rext32[p.E + 1 : p.E + 2] = vec_ref[...].astype(F32)
+    rext32[p.E + 2 :] = jnp.zeros((14 - p.E, W), F32)
+    rext[0:16] = rext32[...].astype(BF)
+    rext[16:] = jnp.zeros((LANES - 16, W), BF)
 
     def mask_rows(i, carry):
         key = lax.broadcasted_iota(jnp.int32, (QB, R), 0) + i * QB
@@ -281,10 +347,9 @@
     for c in loads[1:]:
         c.wait()
     wg[p.EB] = agrad[:W].T
-    wu[p.EB] = pxs[:W].T
+    wu[p.EB] = dOT[:, :W].T
     x_copy.wait_recv()
-    for k in (1, 2, 3):
-        remote(cot_in, cot_in, "c", k - 1, to_z(k)).start()
+    send_own("c", cotg, 0, slice(None))
 
     def norm_half(i, carry):
         v = xs[i].astype(F32)
@@ -327,8 +392,7 @@
     lax.fori_loop(0, LEN // QB, project, 0)
     for g in range(NG):
         rows = slice(g * LANES, (g + 1) * LANES)
-        kT[rows] = kN[g].T
-        vT[rows] = vN[g].T
+        kvT[rows] = vN[g].T
         qN[g] = qT[rows].T
 
     head_row = lax.div(lax.broadcasted_iota(jnp.int32, (LANES, 1), 0), HD)
@@ -350,7 +414,7 @@
                 e = jnp.exp2(s - top)
                 total = jnp.sum(e, axis=0, keepdims=True)
                 at = pl.ds(pl.multiple_of(g * LANES + h * HD, HD), HD)
-                o = nn(vT[at], e.astype(BF)) * (1.0 / total)
+                o = nn(kvT[at], e.astype(BF)) * (1.0 / total)
                 oT[at, cols] = o.astype(BF)
                 lse[pl.ds(g * HPG + h, 1), cols] = top + jnp.log(total) * LOG2E
             return carry
@@ -360,36 +424,106 @@
         m = x_in[rows].astype(F32) + nn(oT[:, cols].T, wfull[3])
         mid[rows] = m
         normg[z, rows] = (m * inv_rms(m) * gain_ffn).astype(BF)
-        for k in (1, 2, 3):
-            remote(normg.at[z, rows], normg.at[z, rows], "n", (k - 1) * 2 + qb, to_z(k)).start()
-
-    for k in (1, 2, 3):
-        remote(cot_in, cot_in, "c", k - 1, to_z(k)).wait_recv()
+        if qb == 0:
+            arrive("c", cotg, 0, 0, slice(None))
+        send_own("n", normg, qb, rows)
+    arrive("c", cotg, 1, 0, slice(None))
+    for g in range(NG):
+        kvT[g * LANES : (g + 1) * LANES] = kN[g].T
 
     def zero_acc(i, carry):
         acc[pl.ds(pl.multiple_of(i * 16, 16), 16)] = jnp.zeros((16, W), F32)
         return carry
 
-    lax.fori_loop(0, p.total // 16, zero_acc, 0)
+    lax.fori_loop(0, 3 * p.NB * W // 16, zero_acc, 0)
     drext[...] = jnp.zeros_like(drext)
     zhi = lax.div(z, 2)
 
     def chunk_of(k):
         return 2 * lax.rem(zhi + lax.div(k, 2), 2) + lax.rem(zlo + lax.rem(k, 2), 2)
 
+    def chip_rows(j):
+        return pl.ds(pl.multiple_of(chip_at(j) * p.pr, 16), p.pr)
+
+    def owner(c):
+        return (lambda f: f()) if p.owners == p.nc else pl.when(c < p.owners)
+
+    owns = owner(chip)
+
+    def h1_copy(b):
+        return remote(stage.at[b, :, 1 - core], h1.at[b], "h1", b, (mate, z))
+
+    def h2_copy(b, j):
+        i = b * (p.nc - 1) + j - 1
+        return remote(stage.at[b, :, core, chip_rows(j)], h2.at[j - 1, b], "h2", i, on_chip(j))
+
+    def h3_copy(b, j):
+        part = res.at[b, :, core, chip_rows(0)]
+        return remote(part, part, "h3", b * (p.nc - 1) + j - 1, on_chip(j))
+
+    def h4_copy(b, j):
+        part = res.at[b, :, core, chip_rows(j)]
+        return remote(part, part, "h4", b * p.nc + j, (mate, z))
+
+    def mate_half(b):
+        for kind in range(3):
+            v = acc[pl.ds(pl.multiple_of((3 * b + kind) * W, W), W)].astype(BF)
+            if kind == 2:
+                v = v.T
+                stage[b, kind, 0] = v[: p.hp]
+                stage[b, kind, 1] = v[p.hp :]
+            else:
+
+                @pl.when(b < p.EB)
+                def _(v=v, kind=kind):
+                    w = v.T
+                    stage[b, kind, 0] = w[: p.hp]
+                    stage[b, kind, 1] = w[p.hp :]
+
+                @pl.when(b >= p.EB)
+                def _(v=v, kind=kind):
+                    stage[b, kind, 0] = v[: p.hp]
+                    stage[b, kind, 1] = v[p.hp :]
+
+        h1_copy(b).start()
+
+    def to_chips(b):
+        h1_copy(b).wait_recv()
+        for kind in range(3):
+            stage[b, kind, core] = (stage[b, kind, core].astype(F32) + h1[b, kind].astype(F32)).astype(BF)
+        for j in range(1, p.nc):
+            owner(chip_at(j))(lambda j=j: h2_copy(b, j).start())
+
+    def from_chips(b):
+        @owns
+        def _():
+            for j in range(1, p.nc):
+                h2_copy(b, j).wait_recv()
+            for kind in range(3):
+                v = stage[b, kind, core, chip_rows(0)].astype(F32)
+                for j in range(1, p.nc):
+                    v += h2[j - 1, b, kind].astype(F32)
+                res[b, kind, core, chip_rows(0)] = v.astype(BF)
+            for j in range(1, p.nc):
+                h3_copy(b, j).start()
+            h4_copy(b, 0).start()
+
+    def hand_over(b):
+        for j in range(1, p.nc):
+            sender = lax.rem(chip + p.nc - j, p.nc)
+
+            @owner(sender)
+            def _(j=j):
+                h3_copy(b, j).wait_recv()
+                h4_copy(b, p.nc - j).start()
+
     def unit(C_s, G_s, RG_s, xT, gT, out_acc, dx_acc, k, carry):
         c = chunk_of(k)
-
-        @pl.when(k > 0)
-        def _():
-            for b in range(R // QB):
-                part = normg.at[c, b * QB : (b + 1) * QB]
-                remote(part, part, "n", (k - 1) * 2 + b, (dp, c)).wait_recv()
 
         x = normg[c]
         xT[...] = x.T
         gT[...] = cotg[c].T
-        logits = nn(x, rext[...])
+        logits = nt(x, rext[...])
         is_expert = lane < p.E
         lg = jnp.where(is_expert, logits, NEG)
         ex = jnp.exp(lg - jnp.max(lg, axis=-1, keepdims=True))
@@ -406,6 +540,18 @@
         dx_acc[...] = jnp.zeros_like(dx_acc)
 
         def block(b, carry):
+            @pl.when((b == 0) & (k < NT - 1))
+            def _():
+                arrive("n", normg, k, 0, halves[0])
+
+            @pl.when((b == 3) & (k < NT - 1))
+            def _():
+                arrive("n", normg, k, 1, halves[1])
+
+            @pl.when((b == 1) & (k == 1))
+            def _():
+                arrive("c", cotg, 2, 0, slice(None))
+
             xb, gb = normg[c], cotg[c]
             a = nt(xb, wg[b])
             u = nt(xb, wu[b])
@@ -432,25 +578,38 @@
             xt = xT[...]
 
             def add(kind, value):
-                at = pl.ds(pl.multiple_of((kind * p.NB + b) * W, W), W)
+                at = pl.ds(pl.multiple_of((3 * b + kind) * W, W), W)
                 acc[at] += value
 
             add(0, nn(xt, da))
             add(1, nn(xt, du))
             add(2, nn(gT[...], hs))
+
+            @pl.when(k == NT - 1)
+            def _():
+                mate_half(b)
+
+                @pl.when(b > 0)
+                def _():
+                    to_chips(b - 1)
+
             return carry
 
         lax.fori_loop(0, p.NB, block, 0)
         rg = RG_s[...] * C_s[...]
         gate = G_s[...]
         dot = jnp.sum(jnp.where(is_expert, gate * rg, 0.0), axis=-1, keepdims=True)
-        logits = nn(normg[c], rext[...])
+        logits = nt(normg[c], rext[...])
         lg = jnp.where(is_expert, logits, NEG)
         ex = jnp.exp(lg - jnp.max(lg, axis=-1, keepdims=True))
         route = ex / jnp.sum(ex, axis=-1, keepdims=True)
         lgrad = jnp.where(is_expert, route * (rg - dot), rg * gate * (1.0 - gate)).astype(BF)
         drext[...] += nn(xT[...], lgrad)
-        dx = dx_acc[...] + nt(lgrad, rext[...])
+        dx = dx_acc[...] + nn(lgrad, rext[...])
+
+        for b in range(R // QB):
+            handed_on("n", normg, c, b, halves[b])
+        handed_on("c", cotg, c, 0, slice(None))
 
         @pl.when(k == 0)
         def _():
@@ -472,27 +631,7 @@
         chunks, V((R, LANES), F32), V((R, LANES), F32), V((R, LANES), F32), V((W, R), BF), V((W, R), BF), V((R, W), F32), V((R, W), F32)
     )
 
-    def to_stage(i, carry):
-        at = pl.ds(pl.multiple_of(i * W, W), W)
-        turned = (lax.rem(i, p.NB) < p.EB) | (i >= 2 * p.NB)
-
-        @pl.when(turned)
-        def _():
-            stage[at] = acc[at].astype(BF).T
-
-        @pl.when(jnp.logical_not(turned))
-        def _():
-            stage[at] = acc[at].astype(BF)
-
-        return carry
-
-    own_half = pl.multiple_of(core * p.half, 16)
-    mate_half = pl.multiple_of((1 - core) * p.half, 16)
-    lax.fori_loop(0, 3 * p.NB, to_stage, 0)
-    if p.flat > p.total:
-        stage[p.total :] = jnp.zeros((p.flat - p.total, W), BF)
-    h1_copy = remote(stage.at[pl.ds(mate_half, p.half)], h1, "h1", 0, (mate, z))
-    h1_copy.start()
+    to_chips(p.NB - 1)
 
     for k in (1, 2, 3):
         remote(normg.at[zk[k]], dxr.at[k - 1], "dx", k - 1, to_z(k)).wait_recv()
@@ -514,31 +653,17 @@
     for h in range(W // HD):
         delta[h : h + 1] = jnp.sum(both[h * HD : (h + 1) * HD], axis=0, keepdims=True)
 
-    def piece_at(j):
-        return pl.ds(pl.multiple_of(core * p.half + chip_at(j) * p.piece, 16), p.piece)
-
-    h1_copy.wait_recv()
-
-    def add_mate(i, carry):
-        near = pl.ds(pl.multiple_of(i * 16, 16), 16)
-        at = pl.ds(pl.multiple_of(own_half + i * 16, 16), 16)
-        stage[at] = (stage[at].astype(F32) + h1[near].astype(F32)).astype(BF)
-        return carry
-
-    lax.fori_loop(0, p.half // 16, add_mate, 0)
-
-    def h2_copy(j):
-        return remote(stage.at[piece_at(j)], h2.at[j - 1], "h2", j - 1, on_chip(j))
-
-    for j in range(1, p.nc):
-        h2_copy(j).start()
-
     dw = [acc.at[m * W : (m + 1) * W] for m in range(4)]
     dxn = acc.at[4 * W : 4 * W + LEN]
     dw[3][...] = nn(oT[...], agrad[...])
     dxn[...] = jnp.zeros_like(dxn)
 
     def back_group(pT, dsT, dk_acc, dv_acc, dqT, g, carry):
+        def chips(b, carry):
+            from_chips(b)
+            return carry
+
+        lax.fori_loop(2 * g, jnp.minimum(2 * g + 2, p.NB), chips, 0)
         at_g = pl.ds(pl.multiple_of(g * LANES, LANES), LANES)
         for qb in range(R // QB):
             cols = slice(qb * QB, (qb + 1) * QB)
@@ -551,7 +676,7 @@
                 pT[:, h * QB : (h + 1) * QB] = prob.astype(BF)
                 dsT[:, h * QB : (h + 1) * QB] = ds
                 at = pl.ds(pl.multiple_of(g * LANES + h * HD, HD), HD)
-                dqT[h * HD : (h + 1) * HD, cols] = nn(kT[at], ds) * SCALE
+                dqT[h * HD : (h + 1) * HD, cols] = nn(kvT[at], ds) * SCALE
             og, qg = dON[g, cols], qN[g, cols]
             o_heads = jnp.concatenate([jnp.where(head_lane == h, og, jnp.zeros_like(og)) for h in range(HPG)], axis=0)
             q_heads = jnp.concatenate([jnp.where(head_lane == h, qg, jnp.zeros_like(qg)) for h in range(HPG)], axis=0)
@@ -585,6 +710,7 @@
     wide = V((LEN, HPG * QB), BF)
     pl.run_scoped(back, wide, wide, V((LEN, LANES), F32), V((LEN, LANES), F32), V((LANES, R), F32))
 
+    pxs = agrad
     pxs[...] = dxn[pl.ds(pl.multiple_of((1 - half_own) * R, R), R)].astype(BF)
     px_copy = remote(pxs, pxr, "px", 0, to_z(1))
     px_copy.start()
@@ -600,9 +726,10 @@
     for half in range(2):
         v = xs[half].astype(F32)
         dg += jnp.sum(dxn[half * R : (half + 1) * R] * (v * inv_rms(v)), axis=0, keepdims=True)
-    smr[dp, 0:1] = dg
-    smr[dp, 1:2] = sm_own
-    smr[dp, 2:16] = drext[...].T[0:14]
+    rext32[0:1] = dg
+    rext32[1:2] = sm_own
+    rext32[2:16] = drext[...].T[0:14]
+    smr[dp] = rext32[...].astype(BF)
 
     def small(j):
         there = lax.rem(dp + j, p.nd)
@@ -611,44 +738,13 @@
     for j in range(1, p.nd):
         small(j).start()
 
-    for j in range(1, p.nc):
-        h2_copy(j).wait_recv()
-
-    def add_chips(i, carry):
-        near = pl.ds(pl.multiple_of(i * 16, 16), 16)
-        at = pl.ds(pl.multiple_of(own_half + chip * p.piece + i * 16, 16), 16)
-        v = stage[at].astype(F32)
-        for j in range(1, p.nc):
-            v += h2[j - 1, near].astype(F32)
-        res[at] = v.astype(BF)
-        return carry
-
-    lax.fori_loop(0, p.piece // 16, add_chips, 0)
-
-    def h3_copy(j):
-        return remote(res.at[piece_at(0)], res.at[piece_at(0)], "h3", j - 1, on_chip(j))
-
-    def h4_copy(j):
-        return remote(res.at[piece_at(j)], res.at[piece_at(j)], "h4", j, (mate, z))
-
-    for j in range(1, p.nc):
-        h3_copy(j).start()
-    h4_copy(0).start()
-
     f1_copy.wait_recv()
     for t in range(NT):
         A[t, core] = (A[t, core].astype(F32) + f1[t].astype(F32)).astype(BF)
 
-    def chip_rows(j):
-        return pl.ds(pl.multiple_of(chip_at(j) * p.pr, 16), p.pr)
-
     def f2_copy(j):
         return remote(A.at[:, core, chip_rows(j)], f2.at[j - 1], "f2", j - 1, on_chip(j))
 
-    def owner(c):
-        return (lambda f: f()) if p.owners == p.nc else pl.when(c < p.owners)
-
-    owns = owner(chip)
     for j in range(1, p.nc):
         owner(chip_at(j))(lambda j=j: f2_copy(j).start())
 
@@ -669,9 +765,9 @@
 
     for j in range(1, p.nd):
         small(j).wait_recv()
-    total = smr[0]
+    total = smr[0].astype(F32)
     for j in range(1, p.nd):
-        total += smr[j]
+        total += smr[j].astype(F32)
     smz[z] = total
 
     def small_z(k):
@@ -707,13 +803,34 @@
     for k in (1, 2, 3):
         small_z(k).wait_recv()
     sm_ref[...] = smz[0] + smz[1] + smz[2] + smz[3]
-    for j in range(1, p.nc):
-        h3_copy(j).wait_recv()
-        h4_copy(p.nc - j).start()
-    for j in range(p.nc):
-        h4_copy(j).wait_recv()
-    write = pltpu.make_async_copy(res, res_hbm, lsem.at[0])
-    write.start()
+
+    def hand_all(b, carry):
+        hand_over(b)
+        return carry
+
+    lax.fori_loop(0, p.NB, hand_all, 0)
+
+    def mate_done(b, carry):
+        for j in range(p.nc):
+            owner(chip_at(j))(lambda j=j: h4_copy(b, j).wait_recv())
+        return carry
+
+    lax.fori_loop(0, p.NB, mate_done, 0)
+    writes = [
+        pltpu.make_async_copy(res.at[part, kind], out, lsem.at[i])
+        for i, (part, kind, out) in enumerate(
+            [
+                (slice(0, p.EB), 0, eg_out),
+                (slice(0, p.EB), 1, eu_out),
+                (slice(0, p.EB), 2, ed_out),
+                (slice(p.EB, p.NB), 0, sg_out),
+                (slice(p.EB, p.NB), 1, su_out),
+                (slice(p.EB, p.NB), 2, sd_out),
+            ]
+        )
+    ]
+    for c in writes:
+        c.start()
     for j in range(1, p.nd):
         sender = lax.rem(dp + p.nd - j, p.nd)
         owner(lax.div(sender, 2))(lambda j=j: f4_copy(j).wait_recv())
@@ -725,23 +842,28 @@
             w_send(k, i).wait_send()
             for j in range(1, S):
                 w_forward(k, i, j).wait_send()
-        remote(cot_in, cot_in, "c", k - 1, to_z(k)).wait_send()
-        for b in range(R // QB):
-            part = normg.at[z, b * QB : (b + 1) * QB]
-            remote(part, part, "n", (k - 1) * 2 + b, to_z(k)).wait_send()
         remote(normg.at[zk[k]], dxr.at[k - 1], "dx", k - 1, to_z(k)).wait_send()
         remote(cotg.at[zk[k]], outr.at[k - 1], "o", k - 1, to_z(k)).wait_send()
         small_z(k).wait_send()
+    own_sent("c", cotg, 0, slice(None))
+    for b in range(R // QB):
+        own_sent("n", normg, b, halves[b])
     x_copy.wait_send()
-    h1_copy.wait_send()
     px_copy.wait_send()
     f1_copy.wait_send()
     for j in range(1, p.nc):
-        h2_copy(j).wait_send()
-        h3_copy(j).wait_send()
         owner(chip_at(j))(lambda j=j: f2_copy(j).wait_send())
-    for j in range(p.nc):
-        h4_copy(j).wait_send()
+
+    def sums_sent(b, carry):
+        h1_copy(b).wait_send()
+        for j in range(1, p.nc):
+            owner(chip_at(j))(lambda j=j: h2_copy(b, j).wait_send())
+            owns(lambda j=j: h3_copy(b, j).wait_send())
+        for j in range(p.nc):
+            owner(chip_at(j))(lambda j=j: h4_copy(b, j).wait_send())
+        return carry
+
+    lax.fori_loop(0, p.NB, sums_sent, 0)
     for j in range(1, p.nd):
         small(j).wait_send()
 
@@ -752,7 +874,8 @@
         for j in range(1, p.nd):
             f4_copy(j).wait_send()
 
-    write.wait()
+    for c in writes:
+        c.wait()
 
 
 def tables():
@@ -792,10 +915,6 @@
     ff = sh_gate.shape[1]
     p = Plan(nd, R, W, experts, eff, ff)
     number, names = sem_plan(p)
-    gains = jnp.stack([gain_attn, gain_ffn]).astype(F32)
-    watt = jnp.stack([w_query.T, w_key.T, w_value.T, w_out])
-    vec = shared_gate_vec[:, None]
-    rext = jnp.concatenate([router, vec, vec, jnp.zeros((W, LANES - experts - 2), BF)], axis=1)
     eg = exp_gate.swapaxes(1, 2).reshape(p.EB, p.B, W)
     eu = exp_up.swapaxes(1, 2).reshape(p.EB, p.B, W)
     ed = exp_down.reshape(p.EB, p.B, W)
@@ -809,6 +928,8 @@
         pltpu.SemaphoreType.DMA((number,)),
         pltpu.SemaphoreType.DMA((8,)),
         V((4, W, W), BF),
+        V((16, W), F32),
+        V((LANES, W), BF),
         V((2, R, W), BF),
         V((LEN, W), BF),
         V((NT, R, W), BF),
@@ -821,7 +942,6 @@
         V((p.NG, LEN, LANES), BF),
         V((W, LEN), BF),
         V((p.NG, LEN, LANES), BF),
-        V((W, LEN), BF),
         V((W, R), BF),
         V((up16(hc), R), F32),
         V((LEN, R), F32),
@@ -830,17 +950,16 @@
         V((R, W), F32),
         V((3, R, W), BF),
         V((3, R, W), BF),
-        V((p.total, W), F32),
+        V((3 * p.NB * W, W), F32),
         V((W, LANES), F32),
-        V((p.flat, W), BF),
-        V((p.half, W), BF),
-        V((max(p.nc - 1, 1), p.piece, W), BF),
-        V((p.flat, W), BF),
+        V((p.NB, 3, 2, p.hp, W), BF),
+        V((p.NB, 3, p.hp, W), BF),
+        V((max(p.nc - 1, 1), p.NB, 3, p.pr, W), BF),
+        V((p.NB, 3, 2, p.hp, W), BF),
         V((R, W), BF),
         V((p.NG, R, LANES), BF),
         V((W, R), BF),
         V((up16(hc), R), F32),
-        V((R, W), BF),
         V((R, W), BF),
         V((NT, 2, p.hp, W), BF),
         V((NT, p.hp, W), BF),
@@ -848,29 +967,41 @@
         V((NT, p.pr, W), BF),
         V((3, p.pr, W), BF),
         V((2, p.hp, W), BF),
-        V((nd, 16, W), F32),
+        V((nd, 16, W), BF),
         V((NT, 16, W), F32),
     ]
-    output, d_inputs, res, att, small = pl.pallas_call(
+    routed = jax.ShapeDtypeStruct((p.EB, 2, p.hp, W), BF)
+    shared = jax.ShapeDtypeStruct((1, 2, p.hp, W), BF)
+    results = pl.pallas_call(
         functools.partial(kernel, p, names),
         out_shape=[
             jax.ShapeDtypeStruct((R, W), BF),
             jax.ShapeDtypeStruct((R, W), F32),
-            jax.ShapeDtypeStruct((p.flat, W), BF),
+            routed,
+            routed,
+            routed,
+            shared,
+            shared,
+            shared,
             jax.ShapeDtypeStruct((2 * p.hp, W), BF),
             jax.ShapeDtypeStruct((16, W), F32),
         ],
-        in_specs=[pl.BlockSpec(memory_space=pltpu.SMEM)] + [vm] * 4 + [hbm] * 8 + [vm] * 4,
-        out_specs=[vm, vm, hbm, vm, vm],
+        in_specs=[pl.BlockSpec(memory_space=pltpu.SMEM)] + [vm] * 9 + [hbm] * 8 + [vm] * 4,
+        out_specs=[vm, vm] + [hbm] * 6 + [vm, vm],
         scratch_shapes=scratch,
         compiler_params=pltpu.CompilerParams(collective_id=0, has_side_effects=True, vmem_limit_bytes=63 << 20),
         name="block",
     )(
         lengths,
         expert_ids.T,
-        gains,
-        watt,
-        rext,
+        gain_attn[None],
+        gain_ffn[None],
+        router.T,
+        shared_gate_vec[None],
+        w_query.T,
+        w_key.T,
+        w_value.T,
+        w_out,
         inputs,
         cotangent,
         eg,
@@ -884,34 +1015,68 @@
         jnp.asarray(cost),
         jnp.asarray(sint),
     )
-    kinds = res[: p.total].reshape(3, p.NB * p.B, W).astype(F32)
-
-    def routed(kind):
-        return kinds[kind, : experts * eff].reshape(experts, eff, W)
-
-    d_exp_gate, d_exp_up = routed(0).swapaxes(1, 2), routed(1).swapaxes(1, 2)
-    d_exp_down = routed(2)
-    d_sh_gate, d_sh_up = kinds[0, experts * eff :], kinds[1, experts * eff :]
-    d_sh_down = kinds[2, experts * eff :]
-    att = att[: 4 * p.HC].reshape(4, p.HC, W).astype(F32)
-    return (
-        output,
-        d_inputs,
-        small[0],
-        att[0].T,
-        att[1].T,
-        att[2].T,
-        att[3],
-        small[1],
-        small[2 : 2 + experts].T,
-        small[2 + experts] + small[3 + experts],
-        d_exp_gate,
-        d_exp_up,
-        d_exp_down,
-        d_sh_gate,
-        d_sh_up,
-        d_sh_down,
-    )
+    return widen(p, *results)
+
+
+def widen_kernel(p, out_b, din, eg, eu, ed, sg, su, sd, att, small, *outs):
+    (out_o, din_o, ga_o, wq_o, wk_o, wv_o, wo_o, gf_o, ro_o, ve_o, eg_o, eu_o, ed_o, sg_o, su_o, sd_o) = outs
+    step = pl.program_id(0)
+    for c in range(2):
+        rows = slice(c * p.hp, (c + 1) * p.hp)
+        for src, dst in ((eg, eg_o), (eu, eu_o), (ed, ed_o)):
+            dst[0, rows] = src[0, c].astype(F32)
+
+    @pl.when(step == 0)
+    def _():
+        out_o[...] = out_b[...]
+        din_o[...] = din[...]
+        for m, dst in enumerate((wq_o, wk_o, wv_o, wo_o)):
+            dst[...] = att[m * p.HC : (m + 1) * p.HC].astype(F32)
+        ga_o[...] = small[0:1]
+        gf_o[...] = small[1:2]
+        ro_o[...] = small[2 : 2 + p.E]
+        ve_o[...] = small[2 + p.E : 3 + p.E] + small[3 + p.E : 4 + p.E]
+        for c in range(2):
+            rows = slice(c * p.hp, (c + 1) * p.hp)
+            for src, dst in ((sg, sg_o), (su, su_o), (sd, sd_o)):
+                dst[rows] = src[0, c].astype(F32)
+
+
+def widen(p, *results):
+    R, W = p.R, p.W
+
+    def whole(shape):
+        return pl.BlockSpec(shape, lambda i: (0,) * len(shape))
+
+    def split(shape):
+        return pl.BlockSpec((1,) + shape[1:], lambda i: (i,) + (0,) * (len(shape) - 1))
+
+    blocks = (p.EB, 2, p.hp, W)
+    routed = (p.EB, p.B, W)
+    row, head, sh = (1, W), (p.HC, W), (W, W)
+    shapes = [(R, W), (R, W), row, head, head, head, head, row, (p.E, W), row, routed, routed, routed, sh, sh, sh]
+    out = pl.pallas_call(
+        functools.partial(widen_kernel, p),
+        grid=(p.EB,),
+        out_shape=[jax.ShapeDtypeStruct(s, BF if i == 0 else F32) for i, s in enumerate(shapes)],
+        in_specs=[whole((R, W))] * 2
+        + [split(blocks)] * 3
+        + [whole((1,) + blocks[1:])] * 3
+        + [whole((2 * p.hp, W)), whole((16, W))],
+        out_specs=[split(s) if s == routed else whole(s) for s in shapes],
+        compiler_params=pltpu.CompilerParams(vmem_limit_bytes=48 << 20),
+        name="widen",
+    )(*results)
+    out = list(out)
+    for i in (2, 7, 9):
+        out[i] = out[i][0]
+    for i in (3, 4, 5, 8):
+        out[i] = out[i].T
+    for i in (10, 11, 12):
+        out[i] = out[i].reshape(p.E, p.eff, W)
+    for i in (10, 11):
+        out[i] = out[i].swapaxes(1, 2)
+    return tuple(out)
 
 
 def solution(mesh):

time: 233 us -> 196 us (0.84)
  Pallas kernels: 214 us -> 179 us
  other arithmetic: 6.73 us -> 1.79 us
  local copies, waits for them, and re-layouts: 11.1 us -> 14.2 us
    pallas_call x1, Pallas kernels: 214 us -> 175 us  [per_device(): pl.pallas_call(functools.partial(kernel, p, names), out_shape=[jax.ShapeD...]
    unnamed x15 -> x20, local copies, waits for them, and re-layouts: 2.5 us -> 10.5 us
    pallas_call x0 -> x1, Pallas kernels: none -> 4.5 us  [widen(): pl.pallas_call(functools.partial(widen_kernel, p), grid=(p.EB,), out_shap...]
    slice x2 -> x0, local copies, waits for them, and re-layouts: 3.78 us -> none  [the longest x1 3.11 us: routed(): return kinds[kind, :experts * eff].reshape(experts, eff, W)]
    convert_element_type x3 -> x0, other arithmetic: 3.6 us -> none  [the longest x1 2.97 us: per_device(): kinds = res[:p.total].reshape(3, p.NB * p.B, W).astype(F32)]
    broadcast_in_dim x2 -> x3, local copies, waits for them, and re-layouts: 0.79 us -> 3.73 us  [the longest x1 1.24 us: per_device(): gain_attn[None]]
where the time goes in v2:
time: 196 us
  Pallas kernels  179 us (91%)
  local copies, waits for them, and re-layouts  14.2 us (7%)
    pallas_call x1, Pallas kernels, per_device(): pl.pallas_call(functools.partial(kernel, p, names), out_shape=[jax.ShapeD...  175 us
    unnamed x20, local copies, waits for them, and re-layouts  10.5 us
    pallas_call x1, Pallas kernels, widen(): pl.pallas_call(functools.partial(widen_kernel, p), grid=(p.EB,), out_shap...  4.5 us

profile of v2, /device:TPU:1, one launch (start us, length us, event | category | flops | bytes accessed | tf_op | source)
XLA Modules:
  0.0 195.8 jit_solution(4640218488259977221)
XLA Ops:
  0.6 1.2 broadcast_in_dim.9.gain_attn_ref
  1.9 1.2 broadcast_in_dim.10.gain_ffn_ref
  3.1 1.2 broadcast_in_dim.11.vec_ref
  4.4 174.6 %block.1 = (bf16[512,384]{1,0:T(8,128)(2,1)}, f32[512,384]{1,0:T(8,128)}, bf16[4,2,192,384]{3,2,1,0:T(8,128)(2,1)}, bf16[4,2,192,384]{3,2,1,0:T(8,128)(2,1)}, bf...) custom-call(s32[2]{0:T(128)} %len_ref.1, ...), custom_call_target="tpu_custom_call" | custom-call | tf_op jit(solution)/shard_map/block/pallas_call | solution.py:975
  179.0 0.0 copy-start
  179.0 1.3 copy-done
  180.3 0.0 copy-start.1
  180.3 1.3 copy-done.1
  181.5 0.0 copy-start.2
  181.5 1.3 copy-done.2
  182.8 0.0 copy-start.3
  182.8 1.1 copy-done.3
  183.9 0.0 copy-start.4
  183.9 1.0 copy-done.4
  184.9 0.0 copy-start.5
  184.9 1.0 copy-done.5
  185.9 1.0 copy-done.6
  186.8 1.0 copy-done.7
  187.8 1.0 copy-done.8
  188.8 0.7 copy-done.9
  189.5 4.5 %widen.1 = (bf16[512,384]{1,0:T(8,128)(2,1)}, f32[512,384]{1,0:T(8,128)}, f32[1,384]{1,0:T(1,128)S(1)}, f32[96,384]{1,0:T(8,128)}, f32[96,384]{1,0:T(8,128)}, /*...) custom-call(bf16[512,384]{1,0:T(8,128)(2,1)S(1)} %copy-done.4, ...), custom_call_target="tpu_custom_call" | custom-call | tf_op jit(solution)/shard_map/widen/pallas_call | solution.py:1058
  194.0 0.6 reduce
  194.6 0.6 reduce.1
  195.2 0.6 reduce.2
  (4 shorter events, 0.0 us)
Async XLA Ops:
  179.0 1.3 copy-start
  180.3 1.3 copy-start.1
  181.5 1.3 copy-start.2
  182.8 1.1 copy-start.3
  183.9 1.0 copy-start.4
  184.9 1.0 copy-start.5
  185.9 1.0 copy-start.6
  186.8 1.0 copy-start.7
  187.8 1.0 copy-start.8
  188.8 0.7 copy-start.9

commit v3 on v2

--- a/solution.py
+++ b/solution.py
@@ -13,6 +13,7 @@
 NT = 4
 LANES = 128
 QB = 256
+TILE = 32
 BF = jnp.bfloat16
 F32 = jnp.float32
 MESH = pl.DeviceIdType.MESH
@@ -126,27 +127,24 @@
     sint,
     out_ref,
     din_ref,
-    eg_out,
-    eu_out,
-    ed_out,
-    sg_out,
-    su_out,
-    sd_out,
     att_ref,
     sm_ref,
+    res,
     send,
     recv,
     lsem,
     wfull,
     rext32,
     rext,
+    rextT,
     xs,
     xn,
     cotg,
     normg,
-    wg,
-    wu,
+    wgu,
+    wguT,
     wd,
+    wdT,
     qT,
     qN,
     kN,
@@ -165,7 +163,7 @@
     stage,
     h1,
     h2,
-    res,
+    fin,
     agrad,
     dON,
     dOT,
@@ -264,11 +262,11 @@
             [
                 (x_hbm, x_in),
                 (cot_hbm, cot_in),
-                (eg_hbm, wg.at[: p.EB]),
-                (eu_hbm, wu.at[: p.EB]),
+                (eg_hbm, wgu.at[: p.EB, : p.B]),
+                (eu_hbm, wgu.at[: p.EB, p.B :]),
                 (ed_hbm, wd.at[: p.EB]),
-                (sg_hbm, agrad.at[:W]),
-                (su_hbm, dOT.at[:, :W]),
+                (sg_hbm, wguT.at[p.EB, :, : p.B]),
+                (su_hbm, wguT.at[p.EB, :, p.B :]),
                 (sd_hbm, wd.at[p.EB]),
             ]
         )
@@ -321,14 +319,15 @@
             w_send(k, i).start()
     loads[0].wait()
     x_copy.start()
-    gain_attn = gain_attn_ref[...].astype(F32)
-    gain_ffn = gain_ffn_ref[...].astype(F32)
+    gain_attn = gain_attn_ref[...].astype(F32)[None]
+    gain_ffn = gain_ffn_ref[...].astype(F32)[None]
     rext32[0 : p.E] = router_ref[...].astype(F32)
-    rext32[p.E : p.E + 1] = vec_ref[...].astype(F32)
-    rext32[p.E + 1 : p.E + 2] = vec_ref[...].astype(F32)
+    vec = vec_ref[...].astype(F32)[None]
+    rext32[p.E : p.E + 1] = vec
+    rext32[p.E + 1 : p.E + 2] = vec
     rext32[p.E + 2 :] = jnp.zeros((14 - p.E, W), F32)
-    rext[0:16] = rext32[...].astype(BF)
-    rext[16:] = jnp.zeros((LANES - 16, W), BF)
+    rext[...] = rext32[...].astype(BF)
+    rextT[...] = jnp.concatenate([rext32[...], jnp.zeros((LANES - 16, W), F32)], axis=0).T.astype(BF)
 
     def mask_rows(i, carry):
         key = lax.broadcasted_iota(jnp.int32, (QB, R), 0) + i * QB
@@ -346,8 +345,19 @@
 
     for c in loads[1:]:
         c.wait()
-    wg[p.EB] = agrad[:W].T
-    wu[p.EB] = dOT[:, :W].T
+    for i in range(2):
+        at = slice(i * p.B, (i + 1) * p.B)
+        wgu[p.EB, at] = wguT[p.EB, :, at].T
+
+    def turn(b, carry):
+        for i in range(2):
+            at = slice(i * p.B, (i + 1) * p.B)
+            wguT[b, :, at] = wgu[b, at].T
+        wdT[b] = wd[b].T
+        return carry
+
+    lax.fori_loop(0, p.EB, turn, 0)
+    wdT[p.EB] = wd[p.EB].T
     x_copy.wait_recv()
     send_own("c", cotg, 0, slice(None))
 
@@ -458,32 +468,28 @@
         return remote(stage.at[b, :, core, chip_rows(j)], h2.at[j - 1, b], "h2", i, on_chip(j))
 
     def h3_copy(b, j):
-        part = res.at[b, :, core, chip_rows(0)]
-        return remote(part, part, "h3", b * (p.nc - 1) + j - 1, on_chip(j))
+        i = b * (p.nc - 1) + j - 1
+        return remote(fin.at[b], res.at[b, :, core, chip_rows(0)], "h3", i, on_chip(j))
 
     def h4_copy(b, j):
         part = res.at[b, :, core, chip_rows(j)]
-        return remote(part, part, "h4", b * p.nc + j, (mate, z))
+        return remote(fin.at[b] if j == 0 else part, part, "h4", b * p.nc + j, (mate, z))
+
+    def keep(b):
+        return pltpu.make_async_copy(fin.at[b], res.at[b, :, core, chip_rows(0)], lsem.at[b])
 
     def mate_half(b):
         for kind in range(3):
             v = acc[pl.ds(pl.multiple_of((3 * b + kind) * W, W), W)].astype(BF)
-            if kind == 2:
-                v = v.T
+            stage[b, kind, 0] = v[: p.hp]
+            stage[b, kind, 1] = v[p.hp :]
+
+        @pl.when(b == p.EB)
+        def _():
+            for kind in range(2):
+                v = acc[(3 * p.EB + kind) * W : (3 * p.EB + kind + 1) * W].astype(BF).T
                 stage[b, kind, 0] = v[: p.hp]
                 stage[b, kind, 1] = v[p.hp :]
-            else:
-
-                @pl.when(b < p.EB)
-                def _(v=v, kind=kind):
-                    w = v.T
-                    stage[b, kind, 0] = w[: p.hp]
-                    stage[b, kind, 1] = w[p.hp :]
-
-                @pl.when(b >= p.EB)
-                def _(v=v, kind=kind):
-                    stage[b, kind, 0] = v[: p.hp]
-                    stage[b, kind, 1] = v[p.hp :]
 
         h1_copy(b).start()
 
@@ -503,10 +509,11 @@
                 v = stage[b, kind, core, chip_rows(0)].astype(F32)
                 for j in range(1, p.nc):
                     v += h2[j - 1, b, kind].astype(F32)
-                res[b, kind, core, chip_rows(0)] = v.astype(BF)
+                fin[b, kind] = v.astype(BF)
             for j in range(1, p.nc):
                 h3_copy(b, j).start()
             h4_copy(b, 0).start()
+            keep(b).start()
 
     def hand_over(b):
         for j in range(1, p.nc):
@@ -517,25 +524,25 @@
                 h3_copy(b, j).wait_recv()
                 h4_copy(b, p.nc - j).start()
 
-    def unit(C_s, G_s, RG_s, xT, gT, out_acc, dx_acc, k, carry):
+    def unit(gates, xT, gT, out_acc, dx_acc, k, carry):
         c = chunk_of(k)
 
-        x = normg[c]
-        xT[...] = x.T
+        xT[...] = normg[c].T
         gT[...] = cotg[c].T
-        logits = nt(x, rext[...])
-        is_expert = lane < p.E
+        logits = nn(rext[...], xT[...])
+        down = lax.broadcasted_iota(jnp.int32, (16, R), 0)
+        is_expert = down < p.E
         lg = jnp.where(is_expert, logits, NEG)
-        ex = jnp.exp(lg - jnp.max(lg, axis=-1, keepdims=True))
-        route = ex / jnp.sum(ex, axis=-1, keepdims=True)
+        ex = jnp.exp(lg - jnp.max(lg, axis=0, keepdims=True))
+        route = ex / jnp.sum(ex, axis=0, keepdims=True)
         at = pl.ds(pl.multiple_of(c * R, R), R)
-        down = lax.broadcasted_iota(jnp.int32, (LANES, R), 0)
         named = (down == ids_ref[0:1, at]) | (down == ids_ref[1:2, at]) | ((down >= p.E) & (down < p.E + 2))
-        chosen = jnp.where(named, 1.0, 0.0).T
-        C_s[...] = chosen
+        chosen = jnp.where(named, 1.0, 0.0)
         gate = jnp.where(is_expert, route, lax.logistic(logits)) * chosen
-        G_s[...] = gate
-        RG_s[...] = jnp.zeros_like(RG_s)
+        gates[0] = chosen
+        gates[1] = route
+        gates[2] = gate
+        gates[3] = jnp.zeros_like(gate)
         out_acc[...] = jnp.zeros_like(out_acc)
         dx_acc[...] = jnp.zeros_like(dx_acc)
 
@@ -552,38 +559,32 @@
             def _():
                 arrive("c", cotg, 2, 0, slice(None))
 
-            xb, gb = normg[c], cotg[c]
-            a = nt(xb, wg[b])
-            u = nt(xb, wu[b])
-            hg = nt(gb, wd[b])
-            gates = G_s[...]
-            first = jnp.sum(jnp.where(lane == 2 * b, gates, 0.0), axis=-1, keepdims=True)
-            second = jnp.sum(jnp.where(lane == 2 * b + 1, gates, 0.0), axis=-1, keepdims=True)
-            wide = lax.broadcasted_iota(jnp.int32, (1, p.B), 1) < p.eff
-            gc = jnp.where(wide, first, second)
-            sig = 0.5 * jnp.tanh(0.5 * a) + 0.5
-            act = a * sig
-            slope = sig + act - act * sig
-            h = act * u
-            prod = h * hg
-            s0 = jnp.sum(jnp.where(wide, prod, 0.0), axis=-1, keepdims=True)
-            s1 = jnp.sum(jnp.where(wide, 0.0, prod), axis=-1, keepdims=True)
-            RG_s[...] += jnp.where(lane == 2 * b, s0, 0.0) + jnp.where(lane == 2 * b + 1, s1, 0.0)
-            hs = (h * gc).astype(BF)
-            hgs = hg * gc
-            da = (hgs * u * slope).astype(BF)
-            du = (hgs * act).astype(BF)
-            out_acc[...] += nn(hs, wd[b])
-            dx_acc[...] += nn(da, wg[b]) + nn(du, wu[b])
-            xt = xT[...]
-
-            def add(kind, value):
-                at = pl.ds(pl.multiple_of((3 * b + kind) * W, W), W)
-                acc[at] += value
-
-            add(0, nn(xt, da))
-            add(1, nn(xt, du))
-            add(2, nn(gT[...], hs))
+            au = nn(wgu[b], xT[...])
+            hg = nn(wd[b], gT[...])
+            h_parts, a_parts, u_parts = [], [], []
+            for e in range(2):
+                expert = pl.ds(2 * b + e, 1)
+                gc = gates[2, expert]
+                sums = 0.0
+                for first in range(e * p.eff, (e + 1) * p.eff, TILE):
+                    rows = slice(first, first + TILE)
+                    a, u, back = au[rows], au[p.B + first : p.B + first + TILE], hg[rows]
+                    sig = 0.5 * jnp.tanh(0.5 * a) + 0.5
+                    act = a * sig
+                    slope = sig + act * (1.0 - sig)
+                    h = act * u
+                    sums += jnp.sum((h * back).reshape(TILE // 8, 8, R), axis=0)
+                    scaled = back * gc
+                    h_parts.append((h * gc).astype(BF))
+                    a_parts.append((scaled * u * slope).astype(BF))
+                    u_parts.append((scaled * act).astype(BF))
+                gates[3, expert] = jnp.sum(sums, axis=0, keepdims=True)
+            hs = jnp.concatenate(h_parts, axis=0)
+            dau = jnp.concatenate(a_parts + u_parts, axis=0)
+            out_acc[...] += nn(wdT[b], hs)
+            dx_acc[...] += nn(wguT[b], dau)
+            acc[pl.ds(pl.multiple_of(3 * b * W, W), 2 * W)] += nn(dau, normg[c])
+            acc[pl.ds(pl.multiple_of((3 * b + 2) * W, W), W)] += nn(hs, cotg[c])
 
             @pl.when(k == NT - 1)
             def _():
@@ -596,40 +597,34 @@
             return carry
 
         lax.fori_loop(0, p.NB, block, 0)
-        rg = RG_s[...] * C_s[...]
-        gate = G_s[...]
-        dot = jnp.sum(jnp.where(is_expert, gate * rg, 0.0), axis=-1, keepdims=True)
-        logits = nt(normg[c], rext[...])
-        lg = jnp.where(is_expert, logits, NEG)
-        ex = jnp.exp(lg - jnp.max(lg, axis=-1, keepdims=True))
-        route = ex / jnp.sum(ex, axis=-1, keepdims=True)
-        lgrad = jnp.where(is_expert, route * (rg - dot), rg * gate * (1.0 - gate)).astype(BF)
-        drext[...] += nn(xT[...], lgrad)
-        dx = dx_acc[...] + nn(lgrad, rext[...])
-
+        chosen, route, gate = gates[0], gates[1], gates[2]
+        rg = gates[3] * chosen
+        dot = jnp.sum(jnp.where(is_expert, route * rg, 0.0), axis=0, keepdims=True)
+        lgrad = jnp.where(is_expert, route * (rg - dot), rg * gate * (1.0 - gate))
+        drext[...] += nn(lgrad.astype(BF), normg[c])
+        lwide = jnp.concatenate([lgrad, jnp.zeros((LANES - 16, R), F32)], axis=0).astype(BF)
+        dx = dx_acc[...] + nn(rextT[...], lwide)
         for b in range(R // QB):
             handed_on("n", normg, c, b, halves[b])
         handed_on("c", cotg, c, 0, slice(None))
 
         @pl.when(k == 0)
         def _():
-            dx_own[...] = dx
-            out_own[...] = out_acc[...]
+            dx_own[...] = dx.T
+            out_own[...] = out_acc[...].T
 
         @pl.when(k > 0)
         def _():
-            normg[c] = dx.astype(BF)
-            cotg[c] = out_acc[...].astype(BF)
+            normg[c] = dx.astype(BF).T
+            cotg[c] = out_acc[...].astype(BF).T
             remote(normg.at[c], dxr.at[k - 1], "dx", k - 1, (dp, c)).start()
 
         return carry
 
-    def chunks(C_s, G_s, RG_s, xT, gT, out_acc, dx_acc):
-        lax.fori_loop(0, NT, functools.partial(unit, C_s, G_s, RG_s, xT, gT, out_acc, dx_acc), 0)
-
-    pl.run_scoped(
-        chunks, V((R, LANES), F32), V((R, LANES), F32), V((R, LANES), F32), V((W, R), BF), V((W, R), BF), V((R, W), F32), V((R, W), F32)
-    )
+    def chunks(gates, xT, gT, out_acc, dx_acc):
+        lax.fori_loop(0, NT, functools.partial(unit, gates, xT, gT, out_acc, dx_acc), 0)
+
+    pl.run_scoped(chunks, V((4, 16, R), F32), V((W, R), BF), V((W, R), BF), V((W, R), F32), V((W, R), F32))
 
     to_chips(p.NB - 1)
 
@@ -728,7 +723,7 @@
         dg += jnp.sum(dxn[half * R : (half + 1) * R] * (v * inv_rms(v)), axis=0, keepdims=True)
     rext32[0:1] = dg
     rext32[1:2] = sm_own
-    rext32[2:16] = drext[...].T[0:14]
+    rext32[2:16] = drext[0:14]
     smr[dp] = rext32[...].astype(BF)
 
     def small(j):
@@ -816,21 +811,6 @@
         return carry
 
     lax.fori_loop(0, p.NB, mate_done, 0)
-    writes = [
-        pltpu.make_async_copy(res.at[part, kind], out, lsem.at[i])
-        for i, (part, kind, out) in enumerate(
-            [
-                (slice(0, p.EB), 0, eg_out),
-                (slice(0, p.EB), 1, eu_out),
-                (slice(0, p.EB), 2, ed_out),
-                (slice(p.EB, p.NB), 0, sg_out),
-                (slice(p.EB, p.NB), 1, su_out),
-                (slice(p.EB, p.NB), 2, sd_out),
-            ]
-        )
-    ]
-    for c in writes:
-        c.start()
     for j in range(1, p.nd):
         sender = lax.rem(dp + p.nd - j, p.nd)
         owner(lax.div(sender, 2))(lambda j=j: f4_copy(j).wait_recv())
@@ -859,6 +839,7 @@
         for j in range(1, p.nc):
             owner(chip_at(j))(lambda j=j: h2_copy(b, j).wait_send())
             owns(lambda j=j: h3_copy(b, j).wait_send())
+        owns(lambda: keep(b).wait())
         for j in range(p.nc):
             owner(chip_at(j))(lambda j=j: h4_copy(b, j).wait_send())
         return carry
@@ -873,9 +854,6 @@
             f3_copy(k).wait_send()
         for j in range(1, p.nd):
             f4_copy(j).wait_send()
-
-    for c in writes:
-        c.wait()
 
 
 def tables():
@@ -929,14 +907,16 @@
         pltpu.SemaphoreType.DMA((8,)),
         V((4, W, W), BF),
         V((16, W), F32),
-        V((LANES, W), BF),
+        V((16, W), BF),
+        V((W, LANES), BF),
         V((2, R, W), BF),
         V((LEN, W), BF),
         V((NT, R, W), BF),
         V((NT, R, W), BF),
+        V((p.NB, 2 * p.B, W), BF),
+        V((p.NB, W, 2 * p.B), BF),
+        V((p.NB, p.B, W), BF),
         V((p.NB, W, p.B), BF),
-        V((p.NB, W, p.B), BF),
-        V((p.NB, p.B, W), BF),
         V((W, R), BF),
         V((p.NG, R, LANES), BF),
         V((p.NG, LEN, LANES), BF),
@@ -951,11 +931,11 @@
         V((3, R, W), BF),
         V((3, R, W), BF),
         V((3 * p.NB * W, W), F32),
-        V((W, LANES), F32),
+        V((16, W), F32),
         V((p.NB, 3, 2, p.hp, W), BF),
         V((p.NB, 3, p.hp, W), BF),
         V((max(p.nc - 1, 1), p.NB, 3, p.pr, W), BF),
-        V((p.NB, 3, 2, p.hp, W), BF),
+        V((p.NB, 3, p.pr, W), BF),
         V((R, W), BF),
         V((p.NG, R, LANES), BF),
         V((W, R), BF),
@@ -970,34 +950,27 @@
         V((nd, 16, W), BF),
         V((NT, 16, W), F32),
     ]
-    routed = jax.ShapeDtypeStruct((p.EB, 2, p.hp, W), BF)
-    shared = jax.ShapeDtypeStruct((1, 2, p.hp, W), BF)
     results = pl.pallas_call(
         functools.partial(kernel, p, names),
         out_shape=[
             jax.ShapeDtypeStruct((R, W), BF),
             jax.ShapeDtypeStruct((R, W), F32),
-            routed,
-            routed,
-            routed,
-            shared,
-            shared,
-            shared,
             jax.ShapeDtypeStruct((2 * p.hp, W), BF),
             jax.ShapeDtypeStruct((16, W), F32),
+            jax.ShapeDtypeStruct((p.NB, 3, 2, p.hp, W), BF),
         ],
         in_specs=[pl.BlockSpec(memory_space=pltpu.SMEM)] + [vm] * 9 + [hbm] * 8 + [vm] * 4,
-        out_specs=[vm, vm] + [hbm] * 6 + [vm, vm],
+        out_specs=[vm] * 4 + [hbm],
         scratch_shapes=scratch,
         compiler_params=pltpu.CompilerParams(collective_id=0, has_side_effects=True, vmem_limit_bytes=63 << 20),
         name="block",
     )(
         lengths,
         expert_ids.T,
-        gain_attn[None],
-        gain_ffn[None],
+        gain_attn,
+        gain_ffn,
         router.T,
-        shared_gate_vec[None],
+        shared_gate_vec,
         w_query.T,
         w_key.T,
         w_value.T,
@@ -1018,13 +991,13 @@
     return widen(p, *results)
 
 
-def widen_kernel(p, out_b, din, eg, eu, ed, sg, su, sd, att, small, *outs):
+def widen_kernel(p, out_b, din, att, small, routed, shared, *outs):
     (out_o, din_o, ga_o, wq_o, wk_o, wv_o, wo_o, gf_o, ro_o, ve_o, eg_o, eu_o, ed_o, sg_o, su_o, sd_o) = outs
     step = pl.program_id(0)
     for c in range(2):
         rows = slice(c * p.hp, (c + 1) * p.hp)
-        for src, dst in ((eg, eg_o), (eu, eu_o), (ed, ed_o)):
-            dst[0, rows] = src[0, c].astype(F32)
+        for kind, dst in enumerate((eg_o, eu_o, ed_o)):
+            dst[0, rows] = routed[0, kind, c].astype(F32)
 
     @pl.when(step == 0)
     def _():
@@ -1032,14 +1005,14 @@
         din_o[...] = din[...]
         for m, dst in enumerate((wq_o, wk_o, wv_o, wo_o)):
             dst[...] = att[m * p.HC : (m + 1) * p.HC].astype(F32)
-        ga_o[...] = small[0:1]
-        gf_o[...] = small[1:2]
+        ga_o[...] = small[0]
+        gf_o[...] = small[1]
         ro_o[...] = small[2 : 2 + p.E]
-        ve_o[...] = small[2 + p.E : 3 + p.E] + small[3 + p.E : 4 + p.E]
+        ve_o[...] = small[2 + p.E] + small[3 + p.E]
         for c in range(2):
             rows = slice(c * p.hp, (c + 1) * p.hp)
-            for src, dst in ((sg, sg_o), (su, su_o), (sd, sd_o)):
-                dst[rows] = src[0, c].astype(F32)
+            for kind, dst in enumerate((sg_o, su_o, sd_o)):
+                dst[rows] = shared[0, kind, c].astype(F32)
 
 
 def widen(p, *results):
@@ -1051,25 +1024,22 @@
     def split(shape):
         return pl.BlockSpec((1,) + shape[1:], lambda i: (i,) + (0,) * (len(shape) - 1))
 
-    blocks = (p.EB, 2, p.hp, W)
+    block = (1, 3, 2, p.hp, W)
     routed = (p.EB, p.B, W)
-    row, head, sh = (1, W), (p.HC, W), (W, W)
+    row, head, sh = (W,), (p.HC, W), (W, W)
     shapes = [(R, W), (R, W), row, head, head, head, head, row, (p.E, W), row, routed, routed, routed, sh, sh, sh]
     out = pl.pallas_call(
         functools.partial(widen_kernel, p),
         grid=(p.EB,),
         out_shape=[jax.ShapeDtypeStruct(s, BF if i == 0 else F32) for i, s in enumerate(shapes)],
         in_specs=[whole((R, W))] * 2
-        + [split(blocks)] * 3
-        + [whole((1,) + blocks[1:])] * 3
-        + [whole((2 * p.hp, W)), whole((16, W))],
+        + [whole((2 * p.hp, W)), whole((16, W))]
+        + [pl.BlockSpec(block, lambda i: (i, 0, 0, 0, 0)), pl.BlockSpec(block, lambda i: (p.EB, 0, 0, 0, 0))],
         out_specs=[split(s) if s == routed else whole(s) for s in shapes],
-        compiler_params=pltpu.CompilerParams(vmem_limit_bytes=48 << 20),
+        compiler_params=pltpu.CompilerParams(vmem_limit_bytes=63 << 20),
         name="widen",
-    )(*results)
+    )(*results, results[-1])
     out = list(out)
-    for i in (2, 7, 9):
-        out[i] = out[i][0]
     for i in (3, 4, 5, 8):
         out[i] = out[i].T
     for i in (10, 11, 12):

time: 196 us -> 176 us (0.90)
  local copies, waits for them, and re-layouts: 14.2 us -> 0 us
  Pallas kernels: 179 us -> 175 us
    unnamed x20 -> x0, local copies, waits for them, and re-layouts: 10.5 us -> none
    pallas_call x1, Pallas kernels: 175 us -> 167 us  [per_device(): pl.pallas_call(functools.partial(kernel, p, names), out_shape=[jax.ShapeD...]
    broadcast_in_dim x3 -> x0, local copies, waits for them, and re-layouts: 3.73 us -> none  [the longest x1 1.24 us: per_device(): gain_attn[None]]
    pallas_call x1, Pallas kernels: 4.5 us -> 7.52 us  [widen(): pl.pallas_call(functools.partial(widen_kernel, p), grid=(p.EB,), out_shap...]
where the time goes in v3:
time: 176 us
  Pallas kernels  175 us (99%)
    pallas_call x1, Pallas kernels, per_device(): pl.pallas_call(functools.partial(kernel, p, names), out_shape=[jax.ShapeD...  167 us
    pallas_call x1, Pallas kernels, widen(): pl.pallas_call(functools.partial(widen_kernel, p), grid=(p.EB,), out_shap...  7.52 us

profile of v3, /device:TPU:1, one launch (start us, length us, event | category | flops | bytes accessed | tf_op | source)
XLA Modules:
  0.0 175.7 jit_solution(927735283726488685)
XLA Ops:
  0.7 167.4 %block.1 = (bf16[512,384]{1,0:T(8,128)(2,1)}, f32[512,384]{1,0:T(8,128)}, bf16[384,384]{1,0:T(8,128)(2,1)}, f32[16,384]{1,0:T(8,128)}, bf16[5,3,2,192,384]{4,3,2,1,0:T(8,128)(2,1)}) custom-call(s32[2]{0:T(128)} %len_ref.1, s32[2,2048]{1,0:T(2,128)} %bitcast.29, bf16[384]{0:T(512)(128)(2,1)} %gain_attn_ref.1, bf16[384]{0:T(512)(128)(2,1)} %gain_ffn_ref.1, ...), custom_call_target="tpu_custom_call" | custom-call | tf_op jit(solution)/shard_map/block/pallas_call | solution.py:953
  168.1 7.5 %widen.1 = (bf16[512,384]{1,0:T(8,128)(2,1)}, f32[512,384]{1,0:T(8,128)}, f32[384]{0:T(512)}, f32[96,384]{1,0:T(8,128)}, f32[96,384]{1,0:T(8,128)}, /*index=5*/f...) custom-call(bf16[512,384]{1,0:T(8,128)(2,1)} %get-tuple-element.37.o, ...), custom_call_target="tpu_custom_call" | custom-call | tf_op jit(solution)/shard_map/widen/pallas_call | solution.py:1031

commit v4 on v3

--- a/solution.py
+++ b/solution.py
@@ -57,12 +57,13 @@
         self.NB = self.EB + 1
         assert ff == self.B == width and LEN == 2 * rows
         self.E, self.eff, self.ff = experts, eff, ff
-        self.share = min(4, nd)
+        assert nd % 8 == 0
         self.nc = nd // 2
         self.hp = 2 * self.HC
         assert 2 * self.hp == width == self.B
         self.pr = max(16, self.hp // self.nc)
         self.owners = self.hp // self.pr
+        self.att_owners = LANES // 32
         assert self.owners * self.pr == self.hp and self.pr % 16 == 0 and self.owners <= self.nc
 
 
@@ -78,23 +79,24 @@
 
 def sem_plan(p):
     s, names = Sems(), {}
-    names["w"] = s.take(3 * (4 // p.share))
-    names["f"] = s.take(3 * (4 // p.share) * max(p.share - 1, 1))
+    names["w"] = s.take(3)
+    names["f"] = s.take(9)
+    names["g"] = s.take(12)
     names["x"] = s.take(1)
     for way in "rl":
         names["c" + way] = s.take(4)
         names["n" + way] = s.take(8)
-    names["dx"] = s.take(3)
+    names["dx"] = s.take(4)
     names["o"] = s.take(3)
     names["h1"] = s.take(p.NB)
     names["h2"] = s.take(p.NB * max(p.nc - 1, 1))
     names["h3"] = s.take(p.NB * max(p.nc - 1, 1))
     names["h4"] = s.take(p.NB * p.nc)
     names["px"] = s.take(1)
-    names["f1"] = s.take(1)
-    names["f2"] = s.take(max(p.nc - 1, 1))
-    names["f3"] = s.take(3)
-    names["f4"] = s.take(p.nd - 1)
+    names["f1"] = s.take(p.NG)
+    names["f2"] = s.take(p.NG * (p.nc - 1))
+    names["f3"] = s.take(p.NG * NT)
+    names["f4"] = s.take(p.NG * (p.nd - 1))
     names["s1"] = s.take(p.nd - 1)
     names["s2"] = s.take(3)
     return s.n, names
@@ -153,6 +155,7 @@
     oT,
     lse,
     bias,
+    o_acc,
     mid,
     dx_own,
     out_own,
@@ -168,7 +171,6 @@
     dON,
     dOT,
     delta,
-    pxr,
     A,
     f1,
     f2,
@@ -255,7 +257,7 @@
     halves = [slice(i * QB, (i + 1) * QB) for i in range(R // QB)]
 
     V = pltpu.VMEM
-    x_in, cot_in = xs.at[half_own], cotg.at[z]
+    x_in, cot_in = xs.at[0], cotg.at[z]
     loads = [
         pltpu.make_async_copy(src, dst, lsem.at[i])
         for i, (src, dst) in enumerate(
@@ -284,41 +286,39 @@
     lax.fori_loop(1, p.nd, greet, 0)
     pl.semaphore_wait(barrier, 3 + p.nd - 1)
 
-    S = p.share
-    member = lax.rem(dp, S)
-    base = dp - member
+    member = lax.rem(dp, 8)
+    quad = lax.div(member, 2)
+
+    def w_rows(matrix, at, side):
+        start = at * p.HC + side * (p.HC // 2)
+        return wfull.at[matrix, pl.ds(pl.multiple_of(start, 16), p.HC // 2)]
+
+    def w_copy(k, at):
+        part = w_rows(quad, at, core)
+        return remote(part, part, "w", k - 1, to_z(k))
+
+    def f_copy(k, j, matrix):
+        part = w_rows(matrix, zk[k], core)
+        there = dp - member + 2 * lax.rem(quad + j, 4) + core
+        return remote(part, part, "f", (k - 1) * 3 + j - 1, (there, z))
+
+    def g_copy(k, j, side):
+        part = w_rows(lax.rem(quad + 4 - j, 4), zk[k], side)
+        return remote(part, part, "g", (k - 1) * 4 + j, (mate, z))
+
     own_cols = pl.ds(pl.multiple_of(z * p.HC, 32), p.HC)
-
-    def cols_of(k):
-        return pl.ds(pl.multiple_of(zk[k] * p.HC, 32), p.HC)
-
-    def w_send(k, i):
-        m = member + S * i
-        return remote(wfull.at[m, own_cols], wfull.at[m, own_cols], "w", (k - 1) * (4 // S) + i, to_z(k))
-
-    def w_recv(k, i):
-        m = member + S * i
-        return remote(wfull.at[m, cols_of(k)], wfull.at[m, cols_of(k)], "w", (k - 1) * (4 // S) + i, to_z(k))
-
-    def w_forward(k, i, j):
-        m = member + S * i
-        there = base + lax.rem(member + j, S)
-        return remote(
-            wfull.at[m, cols_of(k)],
-            wfull.at[m, cols_of(k)],
-            "f",
-            ((k - 1) * (4 // S) + i) * (S - 1) + j - 1,
-            (there, z),
-        )
-
     for m, ref in enumerate((wq_ref, wk_ref, wv_ref, wo_ref)):
         wfull[m, own_cols] = ref[...]
-    x_copy = remote(x_in, x_in, "x", 0, to_z(1))
     for k in (1, 2, 3):
-        for i in range(4 // S):
-            w_send(k, i).start()
+        w_copy(k, z).start()
     loads[0].wait()
-    x_copy.start()
+    x_copy = remote(xs.at[0], xs.at[1], "x", 0, (dp, z + 1 - 2 * zlo))
+    late = zlo == 1
+
+    @pl.when(zlo == 0)
+    def _():
+        x_copy.start()
+
     gain_attn = gain_attn_ref[...].astype(F32)[None]
     gain_ffn = gain_ffn_ref[...].astype(F32)[None]
     rext32[0 : p.E] = router_ref[...].astype(F32)
@@ -329,19 +329,19 @@
     rext[...] = rext32[...].astype(BF)
     rextT[...] = jnp.concatenate([rext32[...], jnp.zeros((LANES - 16, W), F32)], axis=0).T.astype(BF)
 
-    def mask_rows(i, carry):
+    for k in (1, 2, 3):
+        w_copy(k, zk[k]).wait_recv()
+        for j in (1, 2, 3):
+            f_copy(k, j, quad).start()
+        g_copy(k, 0, core).start()
+
+    length = len_ref[lax.div(z, 2)]
+    for i in range(R // QB):
         key = lax.broadcasted_iota(jnp.int32, (QB, R), 0) + i * QB
-        query = lax.broadcasted_iota(jnp.int32, (QB, R), 1) + half_own * R
-        length = len_ref[lax.div(z, 2)]
-        bias[pl.ds(pl.multiple_of(i * QB, QB), QB)] = jnp.where((key <= query) & (key < length), 0.0, NEG)
-        return carry
-
-    lax.fori_loop(0, LEN // QB, mask_rows, 0)
-    for k in (1, 2, 3):
-        for i in range(4 // S):
-            w_recv(k, i).wait_recv()
-            for j in range(1, S):
-                w_forward(k, i, j).start()
+        query = lax.broadcasted_iota(jnp.int32, (QB, R), 1)
+        bias[i * QB : (i + 1) * QB] = jnp.where((key <= query) & (key + half_own * R < length), 0.0, NEG)
+    v = x_in[...].astype(F32)
+    xn[0] = (v * inv_rms(v) * gain_attn).astype(BF)
 
     for c in loads[1:]:
         c.wait()
@@ -358,19 +358,14 @@
 
     lax.fori_loop(0, p.EB, turn, 0)
     wdT[p.EB] = wd[p.EB].T
-    x_copy.wait_recv()
+    for k in (1, 2, 3):
+        for j in (1, 2, 3):
+            f_copy(k, j, lax.rem(quad + 4 - j, 4)).wait_recv()
+            g_copy(k, j, core).start()
     send_own("c", cotg, 0, slice(None))
-
-    def norm_half(i, carry):
-        v = xs[i].astype(F32)
-        xn[pl.ds(pl.multiple_of(i * R, R), R)] = (v * inv_rms(v) * gain_attn).astype(BF)
-        return carry
-
-    lax.fori_loop(0, 2, norm_half, 0)
     for k in (1, 2, 3):
-        for i in range(4 // S):
-            for j in range(1, S):
-                w_forward(k, i, j).wait_recv()
+        for j in range(4):
+            g_copy(k, j, 1 - core).wait_recv()
 
     own_pos = pl.ds(pl.multiple_of(half_own * R, R), R)
     lane = lax.broadcasted_iota(jnp.int32, (1, LANES), 1)
@@ -379,7 +374,7 @@
     def swap_halves(v):
         return jnp.where(low_half, pltpu.roll(v, LANES - HD // 2, 1), pltpu.roll(v, HD // 2, 1))
 
-    q_pre = nt(wfull[0], xn[own_pos])
+    q_pre = nt(wfull[0], xn[0])
     cos_own, sin_own = cost[:, own_pos], sint[:, own_pos]
     for h in range(W // HD):
         a = q_pre[h * HD : h * HD + HD // 2]
@@ -387,59 +382,107 @@
         qT[h * HD : h * HD + HD // 2] = ((a * cos_own - b * sin_own) * (SCALE * LOG2E)).astype(BF)
         qT[h * HD + HD // 2 : (h + 1) * HD] = ((a * sin_own + b * cos_own) * (SCALE * LOG2E)).astype(BF)
 
-    def project(i, carry):
-        rows = pl.ds(pl.multiple_of(i * QB, QB), QB)
-        xb = xn[rows]
-        k_pre = nt(xb, wfull[1])
-        v_pre = nt(xb, wfull[2])
-        c, s = cosk[rows], sink[rows]
+    def keys_values(slot, start):
+        def project(i, carry):
+            rows = pl.ds(pl.multiple_of(i * QB, QB), QB)
+            at = pl.ds(pl.multiple_of(start + i * QB, QB), QB)
+            xb = xn[slot, rows]
+            k_pre = nt(xb, wfull[1])
+            v_pre = nt(xb, wfull[2])
+            c, s = cosk[at], sink[at]
+            for g in range(NG):
+                kg = k_pre[:, g * LANES : (g + 1) * LANES]
+                kN[slot, g, rows] = (kg * c + swap_halves(kg) * s).astype(BF)
+                vN[slot, g, rows] = v_pre[:, g * LANES : (g + 1) * LANES].astype(BF)
+            return carry
+
+        lax.fori_loop(0, R // QB, project, 0)
         for g in range(NG):
-            kg = k_pre[:, g * LANES : (g + 1) * LANES]
-            kN[g, rows] = (kg * c + swap_halves(kg) * s).astype(BF)
-            vN[g, rows] = v_pre[:, g * LANES : (g + 1) * LANES].astype(BF)
-        return carry
-
-    lax.fori_loop(0, LEN // QB, project, 0)
+            kvT[slot, g * LANES : (g + 1) * LANES] = vN[slot, g].T
+
+    keys_values(0, half_own * R)
     for g in range(NG):
-        rows = slice(g * LANES, (g + 1) * LANES)
-        kvT[rows] = vN[g].T
-        qN[g] = qT[rows].T
+        qN[g] = qT[g * LANES : (g + 1) * LANES].T
 
     head_row = lax.div(lax.broadcasted_iota(jnp.int32, (LANES, 1), 0), HD)
     head_lane = lax.div(lane, HD)
     HPG = LANES // HD
 
-    def scores(g, h, qb):
-        qg = qT[pl.ds(pl.multiple_of(g * LANES, LANES), LANES), qb * QB : (qb + 1) * QB]
-        masked = jnp.where(head_row == h, qg, jnp.zeros_like(qg))
-        return nn(kN[g], masked) + bias[:, qb * QB : (qb + 1) * QB]
+    def one_head(ref, g, h, cols):
+        v = ref[pl.ds(pl.multiple_of(g * LANES, LANES), LANES), cols]
+        return jnp.where(head_row == h, v, jnp.zeros_like(v))
+
+    def rows_of(g, h):
+        return pl.ds(pl.multiple_of(g * LANES + h * HD, HD), HD)
+
+    every = slice(0, R)
+
+    def early_bias(n):
+        one = jnp.where(lax.broadcasted_iota(jnp.int32, (R, LANES), 0) < length, 0.0, NEG)
+        return jnp.concatenate([one] * (n // LANES), axis=1)
+
+    def softmax_parts(slot, g, h, keys, cols, addend):
+        s = nn(kN[slot, g, keys], one_head(qT, g, h, cols)) + addend
+        top = jnp.max(s, axis=0, keepdims=True)
+        e = jnp.exp2(s - top)
+        total = jnp.sum(e, axis=0, keepdims=True)
+        return top, total, nn(kvT[slot, rows_of(g, h), keys], e.astype(BF))
+
+    def own_keys(g, carry):
+        for qb in range(R // QB):
+            keys, cols = slice(0, (qb + 1) * QB), halves[qb]
+            for h in range(HPG):
+                head = pl.ds(g * HPG + h, 1)
+                lse[head, cols], delta[head, cols], o_acc[rows_of(g, h), cols] = softmax_parts(
+                    0, g, h, keys, cols, bias[keys, cols]
+                )
+        return carry
+
+    lax.fori_loop(0, NG, own_keys, 0)
+    arrive("c", cotg, 0, 0, slice(None))
+
+    @pl.when(late)
+    def _():
+        x_copy.wait_recv()
+        v = xs[1].astype(F32)
+        xn[1] = (v * inv_rms(v) * gain_attn).astype(BF)
+        keys_values(1, 0)
+
+    def early_keys(g, carry):
+        addend = early_bias(R)
+        for h in range(HPG):
+            head = pl.ds(g * HPG + h, 1)
+            top, total, o = softmax_parts(1, g, h, every, every, addend)
+            old = lse[head]
+            new = jnp.maximum(top, old)
+            keep_old, keep_new = jnp.exp2(old - new), jnp.exp2(top - new)
+            lse[head] = new
+            delta[head] = delta[head] * keep_old + total * keep_new
+            at = rows_of(g, h)
+            o_acc[at] = o_acc[at] * keep_old + o * keep_new
+        return carry
+
+    @pl.when(late)
+    def _():
+        lax.fori_loop(0, NG, early_keys, 0)
 
     for qb in range(R // QB):
-        cols = slice(qb * QB, (qb + 1) * QB)
-
-        def heads(g, carry):
-            for h in range(HPG):
-                s = scores(g, h, qb)
-                top = jnp.max(s, axis=0, keepdims=True)
-                e = jnp.exp2(s - top)
-                total = jnp.sum(e, axis=0, keepdims=True)
-                at = pl.ds(pl.multiple_of(g * LANES + h * HD, HD), HD)
-                o = nn(kvT[at], e.astype(BF)) * (1.0 / total)
-                oT[at, cols] = o.astype(BF)
-                lse[pl.ds(g * HPG + h, 1), cols] = top + jnp.log(total) * LOG2E
-            return carry
-
-        lax.fori_loop(0, NG, heads, 0)
-        rows = slice(qb * QB, (qb + 1) * QB)
-        m = x_in[rows].astype(F32) + nn(oT[:, cols].T, wfull[3])
+        rows = halves[qb]
+        for h in range(W // HD):
+            at = slice(h * HD, (h + 1) * HD)
+            oT[at, rows] = (o_acc[at, rows] * (1.0 / delta[h : h + 1, rows])).astype(BF)
+        lse[0 : W // HD, rows] = lse[0 : W // HD, rows] + jnp.log(delta[0 : W // HD, rows]) * LOG2E
+        m = x_in[rows].astype(F32) + nn(oT[:, rows].T, wfull[3])
         mid[rows] = m
         normg[z, rows] = (m * inv_rms(m) * gain_ffn).astype(BF)
-        if qb == 0:
-            arrive("c", cotg, 0, 0, slice(None))
         send_own("n", normg, qb, rows)
-    arrive("c", cotg, 1, 0, slice(None))
     for g in range(NG):
-        kvT[g * LANES : (g + 1) * LANES] = kN[g].T
+        at = slice(g * LANES, (g + 1) * LANES)
+        kvT[0, at] = kN[0, g].T
+
+        @pl.when(late)
+        def _(g=g, at=at):
+            kvT[1, at] = kN[1, g].T
 
     def zero_acc(i, carry):
         acc[pl.ds(pl.multiple_of(i * 16, 16), 16)] = jnp.zeros((16, W), F32)
@@ -461,11 +504,11 @@
     owns = owner(chip)
 
     def h1_copy(b):
-        return remote(stage.at[b, :, 1 - core], h1.at[b], "h1", b, (mate, z))
+        return remote(stage.at[b], h1.at[b], "h1", b, (mate, z))
 
     def h2_copy(b, j):
         i = b * (p.nc - 1) + j - 1
-        return remote(stage.at[b, :, core, chip_rows(j)], h2.at[j - 1, b], "h2", i, on_chip(j))
+        return remote(h1.at[b, :, chip_rows(j)], h2.at[j - 1, b], "h2", i, on_chip(j))
 
     def h3_copy(b, j):
         i = b * (p.nc - 1) + j - 1
@@ -478,25 +521,40 @@
     def keep(b):
         return pltpu.make_async_copy(fin.at[b], res.at[b, :, core, chip_rows(0)], lsem.at[b])
 
+    def block_half(b, kind, side, turned=False):
+        first = (3 * b + kind) * W
+        if not turned:
+            return acc[pl.ds(pl.multiple_of(first + side * p.hp, p.hp), p.hp)]
+        v = acc[pl.ds(pl.multiple_of(first, W), W)].T
+        return jnp.where(side == 0, v[: p.hp], v[p.hp :])
+
+    def each_half(b, side, step):
+        step(2, block_half(b, 2, side))
+
+        @pl.when(b < p.EB)
+        def _():
+            for kind in range(2):
+                step(kind, block_half(b, kind, side))
+
+        @pl.when(b == p.EB)
+        def _():
+            for kind in range(2):
+                step(kind, block_half(b, kind, side, True))
+
     def mate_half(b):
-        for kind in range(3):
-            v = acc[pl.ds(pl.multiple_of((3 * b + kind) * W, W), W)].astype(BF)
-            stage[b, kind, 0] = v[: p.hp]
-            stage[b, kind, 1] = v[p.hp :]
-
-        @pl.when(b == p.EB)
-        def _():
-            for kind in range(2):
-                v = acc[(3 * p.EB + kind) * W : (3 * p.EB + kind + 1) * W].astype(BF).T
-                stage[b, kind, 0] = v[: p.hp]
-                stage[b, kind, 1] = v[p.hp :]
-
+        def step(kind, v):
+            stage[b, kind] = v.astype(BF)
+
+        each_half(b, 1 - core, step)
         h1_copy(b).start()
 
     def to_chips(b):
         h1_copy(b).wait_recv()
-        for kind in range(3):
-            stage[b, kind, core] = (stage[b, kind, core].astype(F32) + h1[b, kind].astype(F32)).astype(BF)
+
+        def step(kind, v):
+            h1[b, kind] = (v + h1[b, kind].astype(F32)).astype(BF)
+
+        each_half(b, core, step)
         for j in range(1, p.nc):
             owner(chip_at(j))(lambda j=j: h2_copy(b, j).start())
 
@@ -506,7 +564,7 @@
             for j in range(1, p.nc):
                 h2_copy(b, j).wait_recv()
             for kind in range(3):
-                v = stage[b, kind, core, chip_rows(0)].astype(F32)
+                v = h1[b, kind, chip_rows(0)].astype(F32)
                 for j in range(1, p.nc):
                     v += h2[j - 1, b, kind].astype(F32)
                 fin[b, kind] = v.astype(BF)
@@ -524,18 +582,19 @@
                 h3_copy(b, j).wait_recv()
                 h4_copy(b, p.nc - j).start()
 
-    def unit(gates, xT, gT, out_acc, dx_acc, k, carry):
+    def unit(gates, xT, gT, out_acc, dx_acc, last, part, k, carry):
         c = chunk_of(k)
-
-        xT[...] = normg[c].T
-        gT[...] = cotg[c].T
+        n = part.stop - part.start
+
+        xT[...] = normg[c, part].T
+        gT[...] = cotg[c, part].T
         logits = nn(rext[...], xT[...])
-        down = lax.broadcasted_iota(jnp.int32, (16, R), 0)
+        down = lax.broadcasted_iota(jnp.int32, (16, n), 0)
         is_expert = down < p.E
         lg = jnp.where(is_expert, logits, NEG)
         ex = jnp.exp(lg - jnp.max(lg, axis=0, keepdims=True))
         route = ex / jnp.sum(ex, axis=0, keepdims=True)
-        at = pl.ds(pl.multiple_of(c * R, R), R)
+        at = pl.ds(pl.multiple_of(c * R + part.start, n), n)
         named = (down == ids_ref[0:1, at]) | (down == ids_ref[1:2, at]) | ((down >= p.E) & (down < p.E + 2))
         chosen = jnp.where(named, 1.0, 0.0)
         gate = jnp.where(is_expert, route, lax.logistic(logits)) * chosen
@@ -547,17 +606,19 @@
         dx_acc[...] = jnp.zeros_like(dx_acc)
 
         def block(b, carry):
-            @pl.when((b == 0) & (k < NT - 1))
-            def _():
-                arrive("n", normg, k, 0, halves[0])
-
-            @pl.when((b == 3) & (k < NT - 1))
-            def _():
-                arrive("n", normg, k, 1, halves[1])
-
-            @pl.when((b == 1) & (k == 1))
-            def _():
-                arrive("c", cotg, 2, 0, slice(None))
+            if not last:
+
+                @pl.when((b == 1) & (k > 0))
+                def _():
+                    arrive("c", cotg, k, 0, slice(None))
+
+                @pl.when(b == 2)
+                def _():
+                    arrive("n", normg, k, 0, halves[0])
+
+                @pl.when(b == 4)
+                def _():
+                    arrive("n", normg, k, 1, halves[1])
 
             au = nn(wgu[b], xT[...])
             hg = nn(wd[b], gT[...])
@@ -573,7 +634,7 @@
                     act = a * sig
                     slope = sig + act * (1.0 - sig)
                     h = act * u
-                    sums += jnp.sum((h * back).reshape(TILE // 8, 8, R), axis=0)
+                    sums += jnp.sum((h * back).reshape(TILE // 8, 8, n), axis=0)
                     scaled = back * gc
                     h_parts.append((h * gc).astype(BF))
                     a_parts.append((scaled * u * slope).astype(BF))
@@ -583,16 +644,12 @@
             dau = jnp.concatenate(a_parts + u_parts, axis=0)
             out_acc[...] += nn(wdT[b], hs)
             dx_acc[...] += nn(wguT[b], dau)
-            acc[pl.ds(pl.multiple_of(3 * b * W, W), 2 * W)] += nn(dau, normg[c])
-            acc[pl.ds(pl.multiple_of((3 * b + 2) * W, W), W)] += nn(hs, cotg[c])
-
-            @pl.when(k == NT - 1)
-            def _():
+            acc[pl.ds(pl.multiple_of(3 * b * W, W), 2 * W)] += nn(dau, normg[c, part])
+            acc[pl.ds(pl.multiple_of((3 * b + 2) * W, W), W)] += nn(hs, cotg[c, part])
+
+            if last == 1:
                 mate_half(b)
-
-                @pl.when(b > 0)
-                def _():
-                    to_chips(b - 1)
+                pl.when(b > 0)(lambda: to_chips(b - 1))
 
             return carry
 
@@ -601,37 +658,55 @@
         rg = gates[3] * chosen
         dot = jnp.sum(jnp.where(is_expert, route * rg, 0.0), axis=0, keepdims=True)
         lgrad = jnp.where(is_expert, route * (rg - dot), rg * gate * (1.0 - gate))
-        drext[...] += nn(lgrad.astype(BF), normg[c])
-        lwide = jnp.concatenate([lgrad, jnp.zeros((LANES - 16, R), F32)], axis=0).astype(BF)
+        drext[...] += nn(lgrad.astype(BF), normg[c, part])
+        lwide = jnp.concatenate([lgrad, jnp.zeros((LANES - 16, n), F32)], axis=0).astype(BF)
         dx = dx_acc[...] + nn(rextT[...], lwide)
-        for b in range(R // QB):
-            handed_on("n", normg, c, b, halves[b])
-        handed_on("c", cotg, c, 0, slice(None))
-
-        @pl.when(k == 0)
-        def _():
-            dx_own[...] = dx.T
-            out_own[...] = out_acc[...].T
+        if last != 1:
+            for b in range(R // QB):
+                handed_on("n", normg, c, b, halves[b])
+            handed_on("c", cotg, c, 0, slice(None))
+
+        if not last:
+
+            @pl.when(k == 0)
+            def _():
+                dx_own[...] = dx.T
+                out_own[...] = out_acc[...].astype(BF).T
 
         @pl.when(k > 0)
         def _():
-            normg[c] = dx.astype(BF).T
-            cotg[c] = out_acc[...].astype(BF).T
-            remote(normg.at[c], dxr.at[k - 1], "dx", k - 1, (dp, c)).start()
+            normg[c, part] = dx.astype(BF).T
+            cotg[c, part] = out_acc[...].astype(BF).T
+            remote(normg.at[c, part], dxr.at[k - 1, part], "dx", NT - last if last else k - 1, (dp, c)).start()
 
         return carry
 
-    def chunks(gates, xT, gT, out_acc, dx_acc):
-        lax.fori_loop(0, NT, functools.partial(unit, gates, xT, gT, out_acc, dx_acc), 0)
-
-    pl.run_scoped(chunks, V((4, 16, R), F32), V((W, R), BF), V((W, R), BF), V((W, R), F32), V((W, R), F32))
-
+    def chunks(n, body):
+        pl.run_scoped(body, V((4, 16, n), F32), V((W, n), BF), V((W, n), BF), V((W, n), F32), V((W, n), F32))
+
+    chunks(R, lambda *refs: lax.fori_loop(0, NT - 1, functools.partial(unit, *refs, 0, every), 0) and None)
+    for i, part in enumerate(halves):
+        chunks(QB, lambda *refs, i=i, part=part: unit(*refs, len(halves) - i, part, NT - 1, 0) and None)
     to_chips(p.NB - 1)
 
-    for k in (1, 2, 3):
-        remote(normg.at[zk[k]], dxr.at[k - 1], "dx", k - 1, to_z(k)).wait_recv()
-    for k in (1, 2, 3):
-        remote(cotg.at[zk[k]], outr.at[k - 1], "o", k - 1, to_z(k)).start()
+    def dx_copies():
+        copies = [remote(normg.at[zk[k]], dxr.at[k - 1], "dx", k - 1, to_z(k)) for k in range(1, NT - 1)]
+        for i, part in enumerate(halves):
+            at = normg.at[zk[NT - 1], part]
+            copies.append(remote(at, dxr.at[NT - 2, part], "dx", NT - len(halves) + i, to_z(NT - 1)))
+        return copies
+
+    for copy in dx_copies():
+        copy.wait_recv()
+    def o_next(i):
+        return remote(cotg.at[zk[1 + 2 * i]], outr.at[i], "o", i, to_z(1))
+
+    def o_far():
+        return remote(cotg.at[zk[2]], outr.at[2], "o", 2, to_z(2))
+
+    for i in (1, 0):
+        o_next(i).start()
+
     dn = dx_own[...] + dxr[0].astype(F32) + dxr[1].astype(F32) + dxr[2].astype(F32)
     mid_back, dgain = rms_back(mid[...], dn, gain_ffn)
     sm_own = jnp.sum(dgain, axis=0, keepdims=True)
@@ -649,79 +724,190 @@
         delta[h : h + 1] = jnp.sum(both[h * HD : (h + 1) * HD], axis=0, keepdims=True)
 
     dw = [acc.at[m * W : (m + 1) * W] for m in range(4)]
-    dxn = acc.at[4 * W : 4 * W + LEN]
+    dxn, dxn_early = acc.at[4 * W : 4 * W + R], acc.at[4 * W + R : 4 * W + 2 * R]
     dw[3][...] = nn(oT[...], agrad[...])
-    dxn[...] = jnp.zeros_like(dxn)
-
-    def back_group(pT, dsT, dk_acc, dv_acc, dqT, g, carry):
-        def chips(b, carry):
-            from_chips(b)
+    dw[1][...] = jnp.zeros((W, W), F32)
+    dw[2][...] = jnp.zeros((W, W), F32)
+    dxn[...] = jnp.zeros((R, W), F32)
+    dxn_early[...] = jnp.zeros((R, W), F32)
+    o_acc[...] = jnp.zeros_like(o_acc)
+    pxs = agrad
+    px_copy = remote(pxs, xs.at[1], "px", 0, (dp, z + 1 - 2 * zlo))
+
+    def score_grads(pT, dsT, slot, g, h, keys, cols, addend, place):
+        head = pl.ds(g * HPG + h, 1)
+        s = nn(kN[slot, g, keys], one_head(qT, g, h, cols)) + addend
+        prob = jnp.exp2(s - lse[head, cols])
+        d_prob = nn(vN[slot, g, keys], one_head(dOT, g, h, cols))
+        ds = (prob * (d_prob - delta[head, cols])).astype(BF)
+        pT[keys, place] = prob.astype(BF)
+        dsT[keys, place] = ds
+        o_acc[rows_of(g, h), cols] += nn(kvT[slot, rows_of(g, h), keys], ds) * SCALE
+
+    def all_heads(ref, g, rows):
+        v = ref[g, rows]
+        return jnp.concatenate([jnp.where(head_lane == h, v, jnp.zeros_like(v)) for h in range(HPG)], axis=0)
+
+    def unturn(dk, at):
+        return (dk * cosk[at] - swap_halves(dk) * sink[at]).astype(BF)
+
+    def keys_back(slot, g, at_g, dk, dv, sums):
+        dv = dv.astype(BF)
+        dw[1][at_g] += nn(dk.T, xn[slot])
+        dw[2][at_g] += nn(dv.T, xn[slot])
+        sums[...] += nn(dk, wfull[1, at_g]) + nn(dv, wfull[2, at_g])
+
+    def f1_copy(g):
+        return remote(A.at[g], f1.at[g], "f1", g, (mate, z))
+
+    def f2_rows(j):
+        return pl.ds(pl.multiple_of(chip_at(j) * 16, 16), 16)
+
+    def f2_copy(g, j):
+        i = g * (p.nc - 1) + j - 1
+        return remote(f1.at[g, :, f2_rows(j)], f2.at[j - 1, g], "f2", i, on_chip(j))
+
+    def sums_heads(c):
+        return (lambda f: f()) if p.att_owners == p.nc else pl.when(c < p.att_owners)
+
+    def home(g, side, c):
+        head = HPG * g + (HPG // 2) * side + lax.div(c, 2)
+        to = lax.div(head, p.HC // HD)
+        return to, g * LANES + side * (LANES // 2) + c * 16 - to * p.HC
+
+    def f3_copy(g, at):
+        to, _ = home(g, core, chip)
+        return remote(fD.at[g], f3.at[g, at], "f3", g * NT + at, (dp, to))
+
+    def f4_copy(g, j, row):
+        part = att.at[:, pl.ds(pl.multiple_of(row, 16), 16)]
+        return remote(part, part, "f4", g * (p.nd - 1) + j - 1, (lax.rem(dp + j, p.nd), z))
+
+    def head_half(g, m, side):
+        at = g * LANES + side * (LANES // 2)
+        return dw[m][pl.ds(pl.multiple_of(at, LANES // 2), LANES // 2)]
+
+    def stage_heads(g):
+        for m in range(4):
+            A[g, m] = head_half(g, m, 1 - core).astype(BF)
+        f1_copy(g).start()
+
+    def heads_to_chips(g):
+        f1_copy(g).wait_recv()
+        for m in range(4):
+            f1[g, m] = (head_half(g, m, core) + f1[g, m].astype(F32)).astype(BF)
+        for j in range(1, p.nc):
+            sums_heads(chip_at(j))(lambda j=j: f2_copy(g, j).start())
+
+    def heads_along_z(g):
+        @sums_heads(chip)
+        def _():
+            for j in range(1, p.nc):
+                f2_copy(g, j).wait_recv()
+            for m in range(4):
+                v = f1[g, m, f2_rows(0)].astype(F32)
+                for j in range(1, p.nc):
+                    v += f2[j - 1, g, m].astype(F32)
+                fD[g, m] = v.astype(BF)
+            to, _ = home(g, core, chip)
+
+            @pl.when(to != z)
+            def _():
+                f3_copy(g, z).start()
+
+    def heads_home(g):
+        @sums_heads(chip)
+        def _():
+            to, row = home(g, core, chip)
+
+            @pl.when(to == z)
+            def _():
+                for at in range(NT):
+
+                    @pl.when(at != z)
+                    def _(at=at):
+                        f3_copy(g, at).wait_recv()
+
+                f3[g, z] = fD[g]
+                for m in range(4):
+                    v = f3[g, 0, m].astype(F32)
+                    for at in range(1, NT):
+                        v += f3[g, at, m].astype(F32)
+                    att[m, pl.ds(pl.multiple_of(row, 16), 16)] = v.astype(BF)
+                for j in range(1, p.nd):
+                    f4_copy(g, j, row).start()
+
+    def chips(b, carry):
+        from_chips(b)
+        return carry
+
+    lax.fori_loop(0, p.NB, chips, 0)
+
+    def back(pT, dsT):
+        @pl.when(late)
+        def _():
+            def early(g, carry):
+                at_g = pl.ds(pl.multiple_of(g * LANES, LANES), LANES)
+                for h in range(HPG):
+                    place = slice(h * R, (h + 1) * R)
+                    score_grads(pT, dsT, 1, g, h, every, every, early_bias(R), place)
+                dv = nn(pT[...], all_heads(dON, g, every))
+                dk = nn(dsT[...], all_heads(qN, g, every)) * LN2
+                keys_back(1, g, at_g, unturn(dk, every), dv, dxn_early)
+                return carry
+
+            lax.fori_loop(0, NG, early, 0)
+            pxs[...] = dxn_early[...].astype(BF)
+            px_copy.start()
+
+        def own(g, carry):
+            @pl.when(g > 0)
+            def _():
+                heads_to_chips(g - 1)
+
+            at_g = pl.ds(pl.multiple_of(g * LANES, LANES), LANES)
+            for qb in range(R // QB):
+                keys, cols = slice(0, (qb + 1) * QB), halves[qb]
+                for h in range(HPG):
+                    first = (qb * HPG + h) * QB
+                    score_grads(pT, dsT, 0, g, h, keys, cols, bias[keys, cols], slice(first, first + QB))
+            dk, dv = [], []
+            for qb in range(R // QB):
+                keys, place = slice(0, (qb + 1) * QB), slice(qb * HPG * QB, (qb + 1) * HPG * QB)
+                dv.append(nn(pT[keys, place], all_heads(dON, g, halves[qb])))
+                dk.append(nn(dsT[keys, place], all_heads(qN, g, halves[qb])))
+            dv = jnp.concatenate([dv[0] + dv[1][:QB], dv[1][QB:]], axis=0)
+            dk = jnp.concatenate([dk[0] + dk[1][:QB], dk[1][QB:]], axis=0) * LN2
+            keys_back(0, g, at_g, unturn(dk, own_pos), dv, dxn)
+            parts = []
+            for h in range(HPG):
+                a = o_acc[pl.ds(pl.multiple_of(g * LANES + h * HD, 16), HD // 2)]
+                b = o_acc[pl.ds(pl.multiple_of(g * LANES + h * HD + HD // 2, 16), HD // 2)]
+                parts += [a * cos_own + b * sin_own, b * cos_own - a * sin_own]
+            dq = jnp.concatenate(parts, axis=0).astype(BF)
+            dw[0][at_g] = nn(dq, xn[0])
+            dxn[...] += nn(dq.T, wfull[0, at_g])
+            stage_heads(g)
             return carry
 
-        lax.fori_loop(2 * g, jnp.minimum(2 * g + 2, p.NB), chips, 0)
-        at_g = pl.ds(pl.multiple_of(g * LANES, LANES), LANES)
-        for qb in range(R // QB):
-            cols = slice(qb * QB, (qb + 1) * QB)
-            for h in range(HPG):
-                s = scores(g, h, qb)
-                prob = jnp.exp2(s - lse[pl.ds(g * HPG + h, 1), cols])
-                og = dOT[at_g, cols]
-                d_prob = nn(vN[g], jnp.where(head_row == h, og, jnp.zeros_like(og)))
-                ds = (prob * (d_prob - delta[pl.ds(g * HPG + h, 1), cols])).astype(BF)
-                pT[:, h * QB : (h + 1) * QB] = prob.astype(BF)
-                dsT[:, h * QB : (h + 1) * QB] = ds
-                at = pl.ds(pl.multiple_of(g * LANES + h * HD, HD), HD)
-                dqT[h * HD : (h + 1) * HD, cols] = nn(kvT[at], ds) * SCALE
-            og, qg = dON[g, cols], qN[g, cols]
-            o_heads = jnp.concatenate([jnp.where(head_lane == h, og, jnp.zeros_like(og)) for h in range(HPG)], axis=0)
-            q_heads = jnp.concatenate([jnp.where(head_lane == h, qg, jnp.zeros_like(qg)) for h in range(HPG)], axis=0)
-            dv = nn(pT[...], o_heads)
-            dk = nn(dsT[...], q_heads) * LN2
-            if qb == 0:
-                dv_acc[...] = dv
-                dk_acc[...] = dk
-            else:
-                dv_acc[...] += dv
-                dk_acc[...] += dk
-        dv = dv_acc[...].astype(BF)
-        dk = dk_acc[...]
-        dk = (dk * cosk[...] - swap_halves(dk) * sink[...]).astype(BF)
-        parts = []
-        for h in range(HPG):
-            a = dqT[h * HD : h * HD + HD // 2]
-            b = dqT[h * HD + HD // 2 : (h + 1) * HD]
-            parts += [a * cos_own + b * sin_own, b * cos_own - a * sin_own]
-        dq = jnp.concatenate(parts, axis=0).astype(BF)
-        dw[0][at_g] = nn(dq, xn[own_pos])
-        dw[1][at_g] = nn(dk.T, xn[...])
-        dw[2][at_g] = nn(dv.T, xn[...])
-        dxn[...] += nn(dk, wfull[1, at_g]) + nn(dv, wfull[2, at_g])
-        dxn[own_pos] += nn(dq.T, wfull[0, at_g])
-        return carry
-
-    def back(pT, dsT, dk_acc, dv_acc, dqT):
-        lax.fori_loop(0, NG, functools.partial(back_group, pT, dsT, dk_acc, dv_acc, dqT), 0)
-
-    wide = V((LEN, HPG * QB), BF)
-    pl.run_scoped(back, wide, wide, V((LEN, LANES), F32), V((LEN, LANES), F32), V((LANES, R), F32))
-
-    pxs = agrad
-    pxs[...] = dxn[pl.ds(pl.multiple_of((1 - half_own) * R, R), R)].astype(BF)
-    px_copy = remote(pxs, pxr, "px", 0, to_z(1))
-    px_copy.start()
-
-    for t in range(NT):
-        for m in range(4):
-            row = m * p.HC
-            A[t, row // p.hp, row % p.hp : row % p.hp + p.HC] = dw[m][t * p.HC : (t + 1) * p.HC].astype(BF)
-    f1_copy = remote(A.at[:, 1 - core], f1, "f1", 0, (mate, z))
-    f1_copy.start()
-
-    dg = jnp.zeros((1, W), F32)
-    for half in range(2):
-        v = xs[half].astype(F32)
-        dg += jnp.sum(dxn[half * R : (half + 1) * R] * (v * inv_rms(v)), axis=0, keepdims=True)
-    rext32[0:1] = dg
+        o_next(1).wait_recv()
+        cotg[zk[2]] = (cotg[zk[2]].astype(F32) + outr[1].astype(F32)).astype(BF)
+        o_far().start()
+        lax.fori_loop(0, NG, own, 0)
+
+    wide = V((R, HPG * R), BF)
+    pl.run_scoped(back, wide, wide)
+
+    def gain_part(slot, sums):
+        v = xs[slot].astype(F32)
+        return jnp.sum(sums[...] * (v * inv_rms(v)), axis=0, keepdims=True)
+
+    rext32[0:1] = gain_part(0, dxn)
+
+    @pl.when(late)
+    def _():
+        rext32[0:1] += gain_part(1, dxn_early)
+
     rext32[1:2] = sm_own
     rext32[2:16] = drext[0:14]
     smr[dp] = rext32[...].astype(BF)
@@ -733,30 +919,11 @@
     for j in range(1, p.nd):
         small(j).start()
 
-    f1_copy.wait_recv()
-    for t in range(NT):
-        A[t, core] = (A[t, core].astype(F32) + f1[t].astype(F32)).astype(BF)
-
-    def f2_copy(j):
-        return remote(A.at[:, core, chip_rows(j)], f2.at[j - 1], "f2", j - 1, on_chip(j))
-
-    for j in range(1, p.nc):
-        owner(chip_at(j))(lambda j=j: f2_copy(j).start())
-
-    def f3_copy(k):
-        return remote(fD.at[zk[k]], f3.at[k - 1], "f3", k - 1, to_z(k))
-
-    @owns
-    def _():
-        for j in range(1, p.nc):
-            f2_copy(j).wait_recv()
-        for t in range(NT):
-            v = A[t, core, chip_rows(0)].astype(F32)
-            for j in range(1, p.nc):
-                v += f2[j - 1, t].astype(F32)
-            fD[t] = v.astype(BF)
-        for k in (1, 2, 3):
-            f3_copy(k).start()
+    heads_to_chips(NG - 1)
+    for g in range(NG):
+        heads_along_z(g)
+    for g in range(NG - 1):
+        heads_home(g)
 
     for j in range(1, p.nd):
         small(j).wait_recv()
@@ -770,29 +937,19 @@
 
     for k in (1, 2, 3):
         small_z(k).start()
-    def f4_copy(j):
-        there = lax.rem(dp + j, p.nd)
-        part = att.at[core, chip_rows(0)]
-        return remote(part, part, "f4", j - 1, (there, z))
-
-    @owns
+    heads_home(NG - 1)
+
+    @pl.when(zlo == 0)
     def _():
-        for k in (1, 2, 3):
-            f3_copy(k).wait_recv()
-        v = fD[z].astype(F32)
-        for k in (1, 2, 3):
-            v += f3[k - 1].astype(F32)
-        att[core, chip_rows(0)] = v.astype(BF)
-        for j in range(1, p.nd):
-            f4_copy(j).start()
-
-    px_copy.wait_recv()
-    dn = dxn[own_pos] + pxr[...].astype(F32)
+        px_copy.wait_recv()
+        dxn[...] += xs[1].astype(F32)
+
+    dn = dxn[...]
     x_back, _ = rms_back(x_in[...].astype(F32), dn, gain_attn)
     din_ref[...] = dx_own[...] + x_back
-    for k in (1, 2, 3):
-        remote(cotg.at[zk[k]], outr.at[k - 1], "o", k - 1, to_z(k)).wait_recv()
-    whole = mid[...] + (out_own[...] + outr[0].astype(F32) + outr[1].astype(F32) + outr[2].astype(F32))
+    o_next(0).wait_recv()
+    o_far().wait_recv()
+    whole = mid[...] + (out_own[...].astype(F32) + outr[0].astype(F32) + outr[2].astype(F32))
     out_ref[...] = whole.astype(BF)
 
     for k in (1, 2, 3):
@@ -811,28 +968,47 @@
         return carry
 
     lax.fori_loop(0, p.NB, mate_done, 0)
-    for j in range(1, p.nd):
-        sender = lax.rem(dp + p.nd - j, p.nd)
-        owner(lax.div(sender, 2))(lambda j=j: f4_copy(j).wait_recv())
-    for c in range(2):
-        att_ref[c * p.hp : (c + 1) * p.hp] = att[c]
+    for g in range(NG):
+        for j in range(1, p.nd):
+            sender = lax.rem(dp + p.nd - j, p.nd)
+            c, side = lax.div(sender, 2), lax.rem(sender, 2)
+
+            @sums_heads(c)
+            def _(g=g, j=j, c=c, side=side):
+                to, row = home(g, side, c)
+                pl.when(to == z)(lambda: f4_copy(g, j, row).wait_recv())
+
+    for m in range(4):
+        att_ref[m * p.HC : (m + 1) * p.HC] = att[m]
 
     for k in (1, 2, 3):
-        for i in range(4 // S):
-            w_send(k, i).wait_send()
-            for j in range(1, S):
-                w_forward(k, i, j).wait_send()
-        remote(normg.at[zk[k]], dxr.at[k - 1], "dx", k - 1, to_z(k)).wait_send()
-        remote(cotg.at[zk[k]], outr.at[k - 1], "o", k - 1, to_z(k)).wait_send()
+        w_copy(k, z).wait_send()
+        for j in (1, 2, 3):
+            f_copy(k, j, quad).wait_send()
+        for j in range(4):
+            g_copy(k, j, core).wait_send()
         small_z(k).wait_send()
+    for copy in dx_copies() + [o_next(0), o_next(1), o_far()]:
+        copy.wait_send()
     own_sent("c", cotg, 0, slice(None))
     for b in range(R // QB):
         own_sent("n", normg, b, halves[b])
-    x_copy.wait_send()
-    px_copy.wait_send()
-    f1_copy.wait_send()
-    for j in range(1, p.nc):
-        owner(chip_at(j))(lambda j=j: f2_copy(j).wait_send())
+    pl.when(zlo == 0)(lambda: x_copy.wait_send())
+    pl.when(late)(lambda: px_copy.wait_send())
+    for g in range(NG):
+        f1_copy(g).wait_send()
+        for j in range(1, p.nc):
+            sums_heads(chip_at(j))(lambda g=g, j=j: f2_copy(g, j).wait_send())
+
+        @sums_heads(chip)
+        def _(g=g):
+            to, row = home(g, core, chip)
+            pl.when(to != z)(lambda: f3_copy(g, z).wait_send())
+
+            @pl.when(to == z)
+            def _():
+                for j in range(1, p.nd):
+                    f4_copy(g, j, row).wait_send()
 
     def sums_sent(b, carry):
         h1_copy(b).wait_send()
@@ -847,13 +1023,6 @@
     lax.fori_loop(0, p.NB, sums_sent, 0)
     for j in range(1, p.nd):
         small(j).wait_send()
-
-    @owns
-    def _():
-        for k in (1, 2, 3):
-            f3_copy(k).wait_send()
-        for j in range(1, p.nd):
-            f4_copy(j).wait_send()
 
 
 def tables():
@@ -910,7 +1079,7 @@
         V((16, W), BF),
         V((W, LANES), BF),
         V((2, R, W), BF),
-        V((LEN, W), BF),
+        V((2, R, W), BF),
         V((NT, R, W), BF),
         V((NT, R, W), BF),
         V((p.NB, 2 * p.B, W), BF),
@@ -919,20 +1088,21 @@
         V((p.NB, W, p.B), BF),
         V((W, R), BF),
         V((p.NG, R, LANES), BF),
-        V((p.NG, LEN, LANES), BF),
-        V((W, LEN), BF),
-        V((p.NG, LEN, LANES), BF),
+        V((2, p.NG, R, LANES), BF),
+        V((2, W, R), BF),
+        V((2, p.NG, R, LANES), BF),
         V((W, R), BF),
         V((up16(hc), R), F32),
-        V((LEN, R), F32),
+        V((R, R), F32),
+        V((W, R), F32),
         V((R, W), F32),
         V((R, W), F32),
-        V((R, W), F32),
+        V((R, W), BF),
         V((3, R, W), BF),
         V((3, R, W), BF),
         V((3 * p.NB * W, W), F32),
         V((16, W), F32),
-        V((p.NB, 3, 2, p.hp, W), BF),
+        V((p.NB, 3, p.hp, W), BF),
         V((p.NB, 3, p.hp, W), BF),
         V((max(p.nc - 1, 1), p.NB, 3, p.pr, W), BF),
         V((p.NB, 3, p.pr, W), BF),
@@ -940,13 +1110,12 @@
         V((p.NG, R, LANES), BF),
         V((W, R), BF),
         V((up16(hc), R), F32),
-        V((R, W), BF),
-        V((NT, 2, p.hp, W), BF),
-        V((NT, p.hp, W), BF),
-        V((max(p.nc - 1, 1), NT, p.pr, W), BF),
-        V((NT, p.pr, W), BF),
-        V((3, p.pr, W), BF),
-        V((2, p.hp, W), BF),
+        V((p.NG, 4, LANES // 2, W), BF),
+        V((p.NG, 4, LANES // 2, W), BF),
+        V((p.nc - 1, p.NG, 4, 16, W), BF),
+        V((p.NG, 4, 16, W), BF),
+        V((p.NG, NT, 4, 16, W), BF),
+        V((4, p.HC, W), BF),
         V((nd, 16, W), BF),
         V((NT, 16, W), F32),
     ]

time: 176 us -> 169 us (0.960)
  Pallas kernels: 175 us -> 167 us
    pallas_call x1, Pallas kernels: 167 us -> 159 us  [per_device(): pl.pallas_call(functools.partial(kernel, p, names), out_shape=[jax.ShapeD...]
where the time goes in v4:
time: 169 us; the launch traced here: 168 us
  Pallas kernels  167 us (99%)
    pallas_call x1, Pallas kernels, per_device(): pl.pallas_call(functools.partial(kernel, p, names), out_shape=[jax.ShapeD...  159 us
    pallas_call x1, Pallas kernels, widen(): pl.pallas_call(functools.partial(widen_kernel, p), grid=(p.EB,), out_shap...  7.52 us

profile of v4, /device:TPU:1, one launch (start us, length us, event | category | flops | bytes accessed | tf_op | source)
XLA Modules:
  0.0 167.8 jit_solution(6855000546141265244)
XLA Ops:
  0.7 159.4 %block.1 = (bf16[512,384]{1,0:T(8,128)(2,1)}, f32[512,384]{1,0:T(8,128)}, bf16[384,384]{1,0:T(8,128)(2,1)}, f32[16,384]{1,0:T(8,128)}, bf16[5,3,2,192,384]{4,3,2,1,0:T(8,128)(2,1)}) custom-call(s32[2]{0:T(128)} %len_ref.1, s32[2,2048]{1,0:T(2,128)} %bitcast.29, bf16[384]{0:T(512)(128)(2,1)} %gain_attn_ref.1, bf16[384]{0:T(512)(128)(2,1)} %gain_ffn_ref.1, ...), custom_call_target="tpu_custom_call" | custom-call | tf_op jit(solution)/shard_map/block/pallas_call | solution.py:1122
  160.1 7.5 %widen.1 = (bf16[512,384]{1,0:T(8,128)(2,1)}, f32[512,384]{1,0:T(8,128)}, f32[384]{0:T(512)}, f32[96,384]{1,0:T(8,128)}, f32[96,384]{1,0:T(8,128)}, /*index=5*/f...) custom-call(bf16[512,384]{1,0:T(8,128)(2,1)} %get-tuple-element.37.o, ...), custom_call_target="tpu_custom_call" | custom-call | tf_op jit(solution)/shard_map/widen/pallas_call | solution.py:1200

commit v5 on v4

--- a/solution.py
+++ b/solution.py
@@ -421,21 +421,27 @@
         one = jnp.where(lax.broadcasted_iota(jnp.int32, (R, LANES), 0) < length, 0.0, NEG)
         return jnp.concatenate([one] * (n // LANES), axis=1)
 
-    def softmax_parts(slot, g, h, keys, cols, addend):
-        s = nn(kN[slot, g, keys], one_head(qT, g, h, cols)) + addend
-        top = jnp.max(s, axis=0, keepdims=True)
-        e = jnp.exp2(s - top)
-        total = jnp.sum(e, axis=0, keepdims=True)
-        return top, total, nn(kvT[slot, rows_of(g, h), keys], e.astype(BF))
+    def softmax_heads(slot, g, keys, cols, addend):
+        scores, parts, found = {}, {}, []
+        for step in range(HPG + 2):
+            if step < HPG:
+                scores[step] = nn(kN[slot, g, keys], one_head(qT, g, step, cols)) + addend
+            if 1 <= step <= HPG:
+                s = scores.pop(step - 1)
+                top = jnp.max(s, axis=0, keepdims=True)
+                e = jnp.exp2(s - top)
+                parts[step - 1] = top, jnp.sum(e, axis=0, keepdims=True), e.astype(BF)
+            if step >= 2:
+                top, total, e = parts.pop(step - 2)
+                found.append((top, total, nn(kvT[slot, rows_of(g, step - 2), keys], e)))
+        return found
 
     def own_keys(g, carry):
         for qb in range(R // QB):
             keys, cols = slice(0, (qb + 1) * QB), halves[qb]
-            for h in range(HPG):
+            for h, found in enumerate(softmax_heads(0, g, keys, cols, bias[keys, cols])):
                 head = pl.ds(g * HPG + h, 1)
-                lse[head, cols], delta[head, cols], o_acc[rows_of(g, h), cols] = softmax_parts(
-                    0, g, h, keys, cols, bias[keys, cols]
-                )
+                lse[head, cols], delta[head, cols], o_acc[rows_of(g, h), cols] = found
         return carry
 
     lax.fori_loop(0, NG, own_keys, 0)
@@ -449,10 +455,8 @@
         keys_values(1, 0)
 
     def early_keys(g, carry):
-        addend = early_bias(R)
-        for h in range(HPG):
+        for h, (top, total, o) in enumerate(softmax_heads(1, g, every, every, early_bias(R))):
             head = pl.ds(g * HPG + h, 1)
-            top, total, o = softmax_parts(1, g, h, every, every, addend)
             old = lse[head]
             new = jnp.maximum(top, old)
             keep_old, keep_new = jnp.exp2(old - new), jnp.exp2(top - new)
@@ -696,6 +700,11 @@
             copies.append(remote(at, dxr.at[NT - 2, part], "dx", NT - len(halves) + i, to_z(NT - 1)))
         return copies
 
+    def chips(b, carry):
+        from_chips(b)
+        return carry
+
+    lax.fori_loop(0, p.NB - 2, chips, 0)
     for copy in dx_copies():
         copy.wait_recv()
     def o_next(i):
@@ -734,15 +743,25 @@
     pxs = agrad
     px_copy = remote(pxs, xs.at[1], "px", 0, (dp, z + 1 - 2 * zlo))
 
-    def score_grads(pT, dsT, slot, g, h, keys, cols, addend, place):
-        head = pl.ds(g * HPG + h, 1)
-        s = nn(kN[slot, g, keys], one_head(qT, g, h, cols)) + addend
-        prob = jnp.exp2(s - lse[head, cols])
-        d_prob = nn(vN[slot, g, keys], one_head(dOT, g, h, cols))
-        ds = (prob * (d_prob - delta[head, cols])).astype(BF)
-        pT[keys, place] = prob.astype(BF)
-        dsT[keys, place] = ds
-        o_acc[rows_of(g, h), cols] += nn(kvT[slot, rows_of(g, h), keys], ds) * SCALE
+    def score_grads(pT, dsT, slot, g, keys, cols, addend, first):
+        n = cols.stop - cols.start
+        made, turned = {}, {}
+        for step in range(HPG + 2):
+            if step < HPG:
+                s = nn(kN[slot, g, keys], one_head(qT, g, step, cols)) + addend
+                made[step] = s, nn(vN[slot, g, keys], one_head(dOT, g, step, cols))
+            if 1 <= step <= HPG:
+                s, d_prob = made.pop(step - 1)
+                head = pl.ds(g * HPG + step - 1, 1)
+                prob = jnp.exp2(s - lse[head, cols])
+                ds = (prob * (d_prob - delta[head, cols])).astype(BF)
+                place = slice(first + (step - 1) * n, first + step * n)
+                pT[keys, place] = prob.astype(BF)
+                dsT[keys, place] = ds
+                turned[step - 1] = ds
+            if step >= 2:
+                at = rows_of(g, step - 2)
+                o_acc[at, cols] += nn(kvT[slot, at, keys], turned.pop(step - 2)) * SCALE
 
     def all_heads(ref, g, rows):
         v = ref[g, rows]
@@ -837,20 +856,14 @@
                 for j in range(1, p.nd):
                     f4_copy(g, j, row).start()
 
-    def chips(b, carry):
-        from_chips(b)
-        return carry
-
-    lax.fori_loop(0, p.NB, chips, 0)
+    lax.fori_loop(p.NB - 2, p.NB, chips, 0)
 
     def back(pT, dsT):
         @pl.when(late)
         def _():
             def early(g, carry):
                 at_g = pl.ds(pl.multiple_of(g * LANES, LANES), LANES)
-                for h in range(HPG):
-                    place = slice(h * R, (h + 1) * R)
-                    score_grads(pT, dsT, 1, g, h, every, every, early_bias(R), place)
+                score_grads(pT, dsT, 1, g, every, every, early_bias(R), 0)
                 dv = nn(pT[...], all_heads(dON, g, every))
                 dk = nn(dsT[...], all_heads(qN, g, every)) * LN2
                 keys_back(1, g, at_g, unturn(dk, every), dv, dxn_early)
@@ -868,9 +881,7 @@
             at_g = pl.ds(pl.multiple_of(g * LANES, LANES), LANES)
             for qb in range(R // QB):
                 keys, cols = slice(0, (qb + 1) * QB), halves[qb]
-                for h in range(HPG):
-                    first = (qb * HPG + h) * QB
-                    score_grads(pT, dsT, 0, g, h, keys, cols, bias[keys, cols], slice(first, first + QB))
+                score_grads(pT, dsT, 0, g, keys, cols, bias[keys, cols], qb * HPG * QB)
             dk, dv = [], []
             for qb in range(R // QB):
                 keys, place = slice(0, (qb + 1) * QB), slice(qb * HPG * QB, (qb + 1) * HPG * QB)

time: 169 us -> 166 us (0.982)
  Pallas kernels: 167 us -> 165 us
    pallas_call x1, Pallas kernels: 159 us -> 158 us  [per_device(): pl.pallas_call(functools.partial(kernel, p, names), out_shape=[jax.ShapeD...]
where the time goes in v5:
time: 166 us
  Pallas kernels  165 us (99%)
    pallas_call x1, Pallas kernels, per_device(): pl.pallas_call(functools.partial(kernel, p, names), out_shape=[jax.ShapeD...  158 us
    pallas_call x1, Pallas kernels, widen(): pl.pallas_call(functools.partial(widen_kernel, p), grid=(p.EB,), out_shap...  7.52 us

profile of v5, /device:TPU:1, one launch (start us, length us, event | category | flops | bytes accessed | tf_op | source)
XLA Modules:
  0.0 165.9 jit_solution(6588844291555596643)
XLA Ops:
  0.7 157.6 %block.1 = (bf16[512,384]{1,0:T(8,128)(2,1)}, f32[512,384]{1,0:T(8,128)}, bf16[384,384]{1,0:T(8,128)(2,1)}, f32[16,384]{1,0:T(8,128)}, bf16[5,3,2,192,384]{4,3,2,1,0:T(8,128)(2,1)}) custom-call(s32[2]{0:T(128)} %len_ref.1, s32[2,2048]{1,0:T(2,128)} %bitcast.29, bf16[384]{0:T(512)(128)(2,1)} %gain_attn_ref.1, bf16[384]{0:T(512)(128)(2,1)} %gain_ffn_ref.1, ...), custom_call_target="tpu_custom_call" | custom-call | tf_op jit(solution)/shard_map/block/pallas_call | solution.py:1133
  158.2 7.5 %widen.1 = (bf16[512,384]{1,0:T(8,128)(2,1)}, f32[512,384]{1,0:T(8,128)}, f32[384]{0:T(512)}, f32[96,384]{1,0:T(8,128)}, f32[96,384]{1,0:T(8,128)}, /*index=5*/f...) custom-call(bf16[512,384]{1,0:T(8,128)(2,1)} %get-tuple-element.37.o, ...), custom_call_target="tpu_custom_call" | custom-call | tf_op jit(solution)/shard_map/widen/pallas_call | solution.py:1211

commit v6 on v5

--- a/solution.py
+++ b/solution.py
@@ -624,16 +624,18 @@
                 def _():
                     arrive("n", normg, k, 1, halves[1])
 
-            au = nn(wgu[b], xT[...])
-            hg = nn(wd[b], gT[...])
-            h_parts, a_parts, u_parts = [], [], []
-            for e in range(2):
+            def made(e):
+                rows = slice(e * p.eff, (e + 1) * p.eff)
+                up = slice(p.B + e * p.eff, p.B + (e + 1) * p.eff)
+                return nn(wgu[b, rows], xT[...]), nn(wgu[b, up], xT[...]), nn(wd[b, rows], gT[...])
+
+            def worked(e, a_all, u_all, back_all):
                 expert = pl.ds(2 * b + e, 1)
                 gc = gates[2, expert]
-                sums = 0.0
-                for first in range(e * p.eff, (e + 1) * p.eff, TILE):
+                sums, h_parts, a_parts, u_parts = 0.0, [], [], []
+                for first in range(0, p.eff, TILE):
                     rows = slice(first, first + TILE)
-                    a, u, back = au[rows], au[p.B + first : p.B + first + TILE], hg[rows]
+                    a, u, back = a_all[rows], u_all[rows], back_all[rows]
                     sig = 0.5 * jnp.tanh(0.5 * a) + 0.5
                     act = a * sig
                     slope = sig + act * (1.0 - sig)
@@ -644,12 +646,21 @@
                     a_parts.append((scaled * u * slope).astype(BF))
                     u_parts.append((scaled * act).astype(BF))
                 gates[3, expert] = jnp.sum(sums, axis=0, keepdims=True)
-            hs = jnp.concatenate(h_parts, axis=0)
-            dau = jnp.concatenate(a_parts + u_parts, axis=0)
+                return [jnp.concatenate(v, axis=0) for v in (a_parts, u_parts, h_parts)]
+
+            def weights_back(e, da, du, hs):
+                for kind, v, rows in ((0, da, normg), (1, du, normg), (2, hs, cotg)):
+                    at = pl.ds(pl.multiple_of((3 * b + kind) * W + e * p.eff, p.eff), p.eff)
+                    acc[at] += nn(v, rows[c, part])
+
+            products = [made(0), made(1)]
+            first = worked(0, *products[0])
+            weights_back(0, *first)
+            second = worked(1, *products[1])
+            da, du, hs = (jnp.concatenate(v, axis=0) for v in zip(first, second))
             out_acc[...] += nn(wdT[b], hs)
-            dx_acc[...] += nn(wguT[b], dau)
-            acc[pl.ds(pl.multiple_of(3 * b * W, W), 2 * W)] += nn(dau, normg[c, part])
-            acc[pl.ds(pl.multiple_of((3 * b + 2) * W, W), W)] += nn(hs, cotg[c, part])
+            dx_acc[...] += nn(wguT[b], jnp.concatenate([da, du], axis=0))
+            weights_back(1, *second)
 
             if last == 1:
                 mate_half(b)

time: 166 us -> 164 us (0.988)
  Pallas kernels: 165 us -> 163 us
    pallas_call x1, Pallas kernels: 158 us -> 155 us  [per_device(): pl.pallas_call(functools.partial(kernel, p, names), out_shape=[jax.ShapeD...]
where the time goes in v6:
time: 164 us; the launch traced here: 163 us
  Pallas kernels  163 us (99%)
    pallas_call x1, Pallas kernels, per_device(): pl.pallas_call(functools.partial(kernel, p, names), out_shape=[jax.ShapeD...  155 us
    pallas_call x1, Pallas kernels, widen(): pl.pallas_call(functools.partial(widen_kernel, p), grid=(p.EB,), out_shap...  7.52 us

profile of v6, /device:TPU:1, one launch (start us, length us, event | category | flops | bytes accessed | tf_op | source)
XLA Modules:
  0.0 163.4 jit_solution(7498265807664909288)
XLA Ops:
  0.7 155.0 %block.1 = (bf16[512,384]{1,0:T(8,128)(2,1)}, f32[512,384]{1,0:T(8,128)}, bf16[384,384]{1,0:T(8,128)(2,1)}, f32[16,384]{1,0:T(8,128)}, bf16[5,3,2,192,384]{4,3,2,1,0:T(8,128)(2,1)}) custom-call(s32[2]{0:T(128)} %len_ref.1, s32[2,2048]{1,0:T(2,128)} %bitcast.29, bf16[384]{0:T(512)(128)(2,1)} %gain_attn_ref.1, bf16[384]{0:T(512)(128)(2,1)} %gain_ffn_ref.1, ...), custom_call_target="tpu_custom_call" | custom-call | tf_op jit(solution)/shard_map/block/pallas_call | solution.py:1144
  155.7 7.5 %widen.1 = (bf16[512,384]{1,0:T(8,128)(2,1)}, f32[512,384]{1,0:T(8,128)}, f32[384]{0:T(512)}, f32[96,384]{1,0:T(8,128)}, f32[96,384]{1,0:T(8,128)}, /*index=5*/f...) custom-call(bf16[512,384]{1,0:T(8,128)(2,1)} %get-tuple-element.37.o, ...), custom_call_target="tpu_custom_call" | custom-call | tf_op jit(solution)/shard_map/widen/pallas_call | solution.py:1222
